TPU v7x, 128 devices: a whole 4x4x4 slice. The times are simulated.
128 devices in a mesh: lat: 8 (over x, core), lon: 16 (over y, z).
Axes of the slice: x: 4, y: 4, z: 4, core: 2. Of those that a mesh axis runs over, the one named last changes fastest.
Arguments:
- species: float32 [4096, 48, 128], P(('lat', 'lon')), may hold values from -6 to 6
- reaction_rates: float32 [48, 48], replicated, may hold values from -0.875 to 0.875
- mix_rate: float32 [48], replicated, may hold values from 0.05 to 0.9
- shift_list: int32 [2, 8, 32], P(None, 'lat'), may hold values from -2 to 2, as said below
- arrival: int32 [2, 4096], P(None, ('lat', 'lon')), may hold values from 0 to 31, as said below
- cell_index: int32 [2, 4096, 128], P(None, ('lat', 'lon')), may hold values from 0 to 131071, as said below
Outputs:
- final_species: float32 [4096, 48, 128], P(('lat', 'lon'))
Inputs may be any that keep to these rules, and one draw needn't show every extreme that they name: `shift_list`: in every step the first and last band move exactly 8 slots by +1 and by -1 sector and 4 slots by +2 and by -2; the other bands half of each; all other slots stay. Which slots is random. `arrival`: each device's 32 entries of a step are a permutation of its slots. `cell_index`: A parcel's cell is owned (cell // 1024 in band-major order) by its own device or one of the eight beside it; bands do not wrap, sectors wrap.
All inputs are finite; a program needn't handle non-finite values.
Results may differ from a plain program's by a relative error of at most 0.0001.
Values sent between devices are 32-bit elements; how exact they have to be, the bound alone decides.
A program may use at most 64 MiB of HBM per device.

v0:
```python
import jax
import jax.numpy as jnp
from jax import lax
from jax.sharding import PartitionSpec as P

CELL_DEV = 1024
STEPS = 2
SUB = 32


def passed_along(value, axis, steps):
    count = lax.axis_size(axis)
    pairs = [(source, (source + steps) % count) for source in range(count)]
    return lax.ppermute(value, axis, pairs)


def padded(block, sides, width):
    for axis, dim in sides:
        count = lax.axis_size(axis)
        forward = [(i, i + 1) for i in range(count - 1)]
        forward.append((count - 1, 0))
        backward = [(target, source) for source, target in forward]
        low = lax.ppermute(
            lax.slice_in_dim(block, block.shape[dim] - width, None, axis=dim), axis, forward
        )
        high = lax.ppermute(lax.slice_in_dim(block, 0, width, axis=dim), axis, backward)
        block = jnp.concatenate([low, block, high], axis=dim)
    return block


def chemistry(state, reaction_rates):
    substep = 2.0 / SUB

    def advance(counter, current):
        pushed = jnp.einsum("st,btp->bsp", reaction_rates, current, precision=lax.Precision.HIGHEST)
        return current + substep * jnp.tanh(pushed)

    return lax.fori_loop(0, SUB, advance, state)


def region_totals(moved, region, region_cells):
    blocks, width, parcels = moved.shape
    groups = blocks // 4
    grouped_state = moved.reshape(groups, 4, width, parcels)
    grouped_region = region.reshape(groups, 4, parcels)
    columns = jnp.arange(region_cells, dtype=jnp.int32)

    def accumulate(carry, pieces):
        sums, counts = carry
        piece_state, piece_region = pieces
        onehot = (piece_region[:, :, None] == columns[None, None, :]).astype(jnp.float32)
        sums = sums + jnp.einsum(
            "bsp,bpc->sc", piece_state, onehot, precision=lax.Precision.HIGHEST
        )
        counts = counts + jnp.sum(onehot, axis=(0, 1))[None, :]
        return ((sums, counts), None)

    start = (
        jnp.zeros((width, region_cells), jnp.float32),
        jnp.zeros((1, region_cells), jnp.float32),
    )
    (sums, counts), unused = lax.scan(accumulate, start, (grouped_state, grouped_region))
    return (sums, counts)


def region_pick(means, region):
    blocks, parcels = region.shape
    groups = blocks // 4
    region_cells = means.shape[1]
    grouped_region = region.reshape(groups, 4, parcels)
    columns = jnp.arange(region_cells, dtype=jnp.int32)

    def select(carry, piece_region):
        onehot = (piece_region[:, :, None] == columns[None, None, :]).astype(jnp.float32)
        return (carry, jnp.einsum("sc,bpc->bsp", means, onehot, precision=lax.Precision.HIGHEST))

    unused, picked = lax.scan(select, 0, grouped_region)
    return picked.reshape(blocks, means.shape[0], parcels)


def shards(species, reaction_rates, mix_rate, shift_list, arrival, cell_index):
    blocks, width, parcels = species.shape
    capacity = blocks // 4
    sectors = lax.axis_size("lon")
    own_band = lax.axis_index("lat")
    own_sector = lax.axis_index("lon")
    slot_ids = jnp.arange(blocks, dtype=jnp.int32)
    state = species
    for section in range(STEPS):
        moved_by = shift_list[section, 0]
        earlier = (moved_by[None, :] == moved_by[:, None]) & (slot_ids[None, :] < slot_ids[:, None])
        slot_rank = jnp.minimum(jnp.sum(earlier.astype(jnp.int32), axis=1), capacity - 1)
        arrivals = []
        for offset in (1, -1, 2, -2):
            chosen = jnp.argsort(jnp.where(moved_by == offset, 0, 1) * blocks + slot_ids)[:capacity]
            leaving = jnp.sum((moved_by == offset).astype(jnp.int32))
            filled = jnp.arange(capacity, dtype=jnp.int32) < leaving
            arrivals.append(
                passed_along(jnp.where(filled[:, None, None], state[chosen], 0.0), "lon", offset)
            )
        pool = jnp.concatenate(arrivals, 0)
        direction = jnp.where(
            moved_by == 1, 0, jnp.where(moved_by == -1, 1, jnp.where(moved_by == 2, 2, 3))
        )
        row_index = direction * capacity + slot_rank
        landed = jnp.where((moved_by == 0)[:, None, None], state, pool[row_index])
        moved = landed[arrival[section]]
        chem = chemistry(moved, reaction_rates)
        cell_ids = cell_index[section]
        owner_dev = cell_ids // CELL_DEV
        rel_band = owner_dev // sectors - own_band + 1
        rel_sector = (owner_dev % sectors - own_sector + 1) % sectors
        region = (rel_band * 3 + rel_sector) * CELL_DEV + cell_ids % CELL_DEV
        near_sums, near_counts = region_totals(moved, region, 9 * CELL_DEV)
        grid_sums = near_sums.reshape(width, 3, 3, CELL_DEV).transpose(1, 2, 0, 3)
        grid_counts = near_counts.reshape(1, 3, 3, CELL_DEV).transpose(1, 2, 0, 3)
        rim_sums, rim_counts = (
            padded(grid_sums, (("lat", 0), ("lon", 1)), 1),
            padded(grid_counts, (("lat", 0), ("lon", 1)), 1),
        )
        total_sums = jnp.sum(rim_sums[0::2, 0::2], axis=(0, 1))
        total_counts = jnp.sum(rim_counts[0::2, 0::2], axis=(0, 1))
        cell_means = total_sums / jnp.maximum(total_counts, 1.0)
        near_means = padded(cell_means[None, None], (("lat", 0), ("lon", 1)), 1)
        region_means = near_means.transpose(2, 0, 1, 3).reshape(width, 9 * CELL_DEV)
        picked = region_pick(region_means, region)
        state = chem + mix_rate[None, :, None] * (picked - moved)
    return state


def solution(mesh):
    placed = (
        P(("lat", "lon"), None, None),
        P(),
        P(),
        P(None, "lat", None),
        P(None, ("lat", "lon")),
        P(None, ("lat", "lon"), None),
    )
    return jax.shard_map(
        shards, mesh=mesh, in_specs=placed, out_specs=P(("lat", "lon"), None, None), check_vma=False
    )
```

profile of v0, /device:TPU:5, one launch (start us, length us, event | category | flops | bytes accessed | tf_op | source)
XLA Modules:
  0.0 792.9 jit_solution(9837202826114209840)
XLA Ops:
  11.4 4.7 collective-permute-start.1
  23.3 5.1 collective-permute-start.3
  36.3 114.1 %while.72 = (s32[]{:T(128)}, f32[48,9216]{1,0:T(8,128)}, f32[1,9216]{1,0:T(1,128)S(1)}, f32[8,4,48,128]{3,2,1,0:T(8,128)S(1)}, s32[8,4,128]{2,1,0:T(4,128)S(1)}, /*index=5*/s32[]{:T(128)}, s32[]{:T(128)}) while((s32[]{:T(128)}, f32[48,9216]{1,0:T(8,128)}, f32[1,9216]{1,0:T(1,128)S(1)}, f32[8,4,48,128]{3,2,1,0:T(8,128)S(1)}, ...), condition=%wide.region_13.14_spmd.clone, body=%wide.region_11.13_spmd.clone.sunk | while | flops 2737677312 | bytes 3792992 | solution.py:62
  36.5 8.4 %fusion.152 = f32[48,9216]{1,0:T(8,128)} fusion(s32[4,128]{1,0:T(4,128)S(1)} %dynamic-slice_bitcast_fusion.10, f32[48,9216]{1,0:T(8,128)} %get-tuple-element.517, pred[]{:T(512)S(6)} %compare.60, f32[8,4,48,128]{3,2,1,0:T(8,128)S(1)} %get-tuple-element.526, s32[]{:T(128)} %get-tuple-element.516), kind=kOutput, calls=%fused_computation.45.clone.1 | convolution fusion | flops 2723512320 | bytes 3639301 | tf_op jit(solution)/shard_map/while/body/eval_jaxpr/bsp,bpc->sc/dot_general | solution.py:52
  44.9 4.4 fusion.153
  49.5 9.9 %fusion.152 = f32[48,9216]{1,0:T(8,128)} fusion(s32[4,128]{1,0:T(4,128)S(1)} %dynamic-slice_bitcast_fusion.10, f32[48,9216]{1,0:T(8,128)} %get-tuple-element.517, pred[]{:T(512)S(6)} %compare.60, f32[8,4,48,128]{3,2,1,0:T(8,128)S(1)} %get-tuple-element.526, s32[]{:T(128)} %get-tuple-element.516), kind=kOutput, calls=%fused_computation.45.clone.1 | convolution fusion | flops 2723512320 | bytes 3639301 | tf_op jit(solution)/shard_map/while/body/eval_jaxpr/bsp,bpc->sc/dot_general | solution.py:52
  63.9 9.9 %fusion.152 = f32[48,9216]{1,0:T(8,128)} fusion(s32[4,128]{1,0:T(4,128)S(1)} %dynamic-slice_bitcast_fusion.10, f32[48,9216]{1,0:T(8,128)} %get-tuple-element.517, pred[]{:T(512)S(6)} %compare.60, f32[8,4,48,128]{3,2,1,0:T(8,128)S(1)} %get-tuple-element.526, s32[]{:T(128)} %get-tuple-element.516), kind=kOutput, calls=%fused_computation.45.clone.1 | convolution fusion | flops 2723512320 | bytes 3639301 | tf_op jit(solution)/shard_map/while/body/eval_jaxpr/bsp,bpc->sc/dot_general | solution.py:52
  78.3 9.9 %fusion.152 = f32[48,9216]{1,0:T(8,128)} fusion(s32[4,128]{1,0:T(4,128)S(1)} %dynamic-slice_bitcast_fusion.10, f32[48,9216]{1,0:T(8,128)} %get-tuple-element.517, pred[]{:T(512)S(6)} %compare.60, f32[8,4,48,128]{3,2,1,0:T(8,128)S(1)} %get-tuple-element.526, s32[]{:T(128)} %get-tuple-element.516), kind=kOutput, calls=%fused_computation.45.clone.1 | convolution fusion | flops 2723512320 | bytes 3639301 | tf_op jit(solution)/shard_map/while/body/eval_jaxpr/bsp,bpc->sc/dot_general | solution.py:52
  88.2 4.4 fusion.153
  92.7 9.9 %fusion.152 = f32[48,9216]{1,0:T(8,128)} fusion(s32[4,128]{1,0:T(4,128)S(1)} %dynamic-slice_bitcast_fusion.10, f32[48,9216]{1,0:T(8,128)} %get-tuple-element.517, pred[]{:T(512)S(6)} %compare.60, f32[8,4,48,128]{3,2,1,0:T(8,128)S(1)} %get-tuple-element.526, s32[]{:T(128)} %get-tuple-element.516), kind=kOutput, calls=%fused_computation.45.clone.1 | convolution fusion | flops 2723512320 | bytes 3639301 | tf_op jit(solution)/shard_map/while/body/eval_jaxpr/bsp,bpc->sc/dot_general | solution.py:52
  102.6 4.4 fusion.153
  107.1 9.9 %fusion.152 = f32[48,9216]{1,0:T(8,128)} fusion(s32[4,128]{1,0:T(4,128)S(1)} %dynamic-slice_bitcast_fusion.10, f32[48,9216]{1,0:T(8,128)} %get-tuple-element.517, pred[]{:T(512)S(6)} %compare.60, f32[8,4,48,128]{3,2,1,0:T(8,128)S(1)} %get-tuple-element.526, s32[]{:T(128)} %get-tuple-element.516), kind=kOutput, calls=%fused_computation.45.clone.1 | convolution fusion | flops 2723512320 | bytes 3639301 | tf_op jit(solution)/shard_map/while/body/eval_jaxpr/bsp,bpc->sc/dot_general | solution.py:52
  117.0 4.4 fusion.153
  121.6 9.9 %fusion.152 = f32[48,9216]{1,0:T(8,128)} fusion(s32[4,128]{1,0:T(4,128)S(1)} %dynamic-slice_bitcast_fusion.10, f32[48,9216]{1,0:T(8,128)} %get-tuple-element.517, pred[]{:T(512)S(6)} %compare.60, f32[8,4,48,128]{3,2,1,0:T(8,128)S(1)} %get-tuple-element.526, s32[]{:T(128)} %get-tuple-element.516), kind=kOutput, calls=%fused_computation.45.clone.1 | convolution fusion | flops 2723512320 | bytes 3639301 | tf_op jit(solution)/shard_map/while/body/eval_jaxpr/bsp,bpc->sc/dot_general | solution.py:52
  131.4 4.4 fusion.153
  136.0 9.9 %fusion.152 = f32[48,9216]{1,0:T(8,128)} fusion(s32[4,128]{1,0:T(4,128)S(1)} %dynamic-slice_bitcast_fusion.10, f32[48,9216]{1,0:T(8,128)} %get-tuple-element.517, pred[]{:T(512)S(6)} %compare.60, f32[8,4,48,128]{3,2,1,0:T(8,128)S(1)} %get-tuple-element.526, s32[]{:T(128)} %get-tuple-element.516), kind=kOutput, calls=%fused_computation.45.clone.1 | convolution fusion | flops 2723512320 | bytes 3639301 | tf_op jit(solution)/shard_map/while/body/eval_jaxpr/bsp,bpc->sc/dot_general | solution.py:52
  145.8 4.4 fusion.153
  171.5 4.8 collective-permute-start.7
  181.3 4.8 collective-permute-start.11
  186.6 12.5 %collective-permute-done.10 = f32[5,1,1,1024]{3,1,0,2:T(1,128)S(1)} collective-permute-done((f32[5,1,1,1024]{3,1,0,2:T(1,128)S(1)}, f32[5,1,1,1024]{3,1,0,2:T(1,128)S(1)}, u32[]{:S(2)}, u32[]{:S(2)}) %collective-permute-start.10) | collective-permute-done | bytes 20512 | tf_op jit(solution)/shard_map/ppermute | solution.py:23
  199.4 5.9 pad_maximum_fusion
  205.3 60.6 %slice.126 = f32[3,3,48,1024]{3,1,0,2:T(4,128)S(1)} slice(f32[5,5,48,1024]{3,1,0,2:T(8,128)} %pad_maximum_fusion), slice={[0:5:2], [0:5:2], [0:48:1], [0:1024:1]} | slice | bytes 3538944 | tf_op jit(solution)/shard_map/slice | solution.py:121
  275.7 5.3 collective-permute-start.15
  281.0 29.1 %while.68 = (s32[]{:T(128)}, f32[32,48,128]{2,1,0:T(8,128)S(1)}, f32[48,48]{1,0:T(8,128)S(1)}, s32[]{:T(128)}) while((s32[]{:T(128)}, f32[32,48,128]{2,1,0:T(8,128)S(1)}, f32[48,48]{1,0:T(8,128)S(1)}, s32[]{:T(128)}) %tuple.155), condition=%wide.region_10.11_spmd, body=%wide.region_9.10_spmd.sunk | while | flops 113639424 | bytes 3154997 | solution.py:38
  316.5 88.3 %while.70 = (s32[]{:T(128)}, f32[8,4,48,128]{3,2,1,0:T(8,128)S(1)}, s32[8,4,128]{2,1,0:T(4,128)S(1)}, f32[48,9216]{1,0:T(8,128)}, s32[]{:T(128)}) while((s32[]{:T(128)}, f32[8,4,48,128]{3,2,1,0:T(8,128)S(1)}, s32[8,4,128]{2,1,0:T(4,128)S(1)}, f32[48,9216]{1,0:T(8,128)}, s32[]{:T(128)}) %tuple.158), condition=%wide.region_17.18_spmd.clone, body=%wide.region_16.17_spmd.clone.sunk | while | flops 2722627584 | bytes 1873989 | solution.py:77
  316.5 11.1 %fusion.148 = f32[8,4,48,128]{3,2,1,0:T(8,128)S(1)} fusion(f32[8,4,48,128]{3,2,1,0:T(8,128)S(1)} %get-tuple-element.536, s32[]{:T(128)} %get-tuple-element.535, f32[48,9216]{1,0:T(8,128)} %get-tuple-element.543, s32[4,128]{1,0:T(4,128)S(1)} %dynamic-slice_bitcast_fusion.8), kind=kOutput, calls=%fused_computation.31.clone.1 | convolution fusion | flops 2722627584 | bytes 1869828 | tf_op jit(solution)/shard_map/while/body/eval_jaxpr/sc,bpc->bsp/dot_general | solution.py:75
  327.6 11.0 %fusion.148 = f32[8,4,48,128]{3,2,1,0:T(8,128)S(1)} fusion(f32[8,4,48,128]{3,2,1,0:T(8,128)S(1)} %get-tuple-element.536, s32[]{:T(128)} %get-tuple-element.535, f32[48,9216]{1,0:T(8,128)} %get-tuple-element.543, s32[4,128]{1,0:T(4,128)S(1)} %dynamic-slice_bitcast_fusion.8), kind=kOutput, calls=%fused_computation.31.clone.1 | convolution fusion | flops 2722627584 | bytes 1869828 | tf_op jit(solution)/shard_map/while/body/eval_jaxpr/sc,bpc->bsp/dot_general | solution.py:75
  338.7 11.0 %fusion.148 = f32[8,4,48,128]{3,2,1,0:T(8,128)S(1)} fusion(f32[8,4,48,128]{3,2,1,0:T(8,128)S(1)} %get-tuple-element.536, s32[]{:T(128)} %get-tuple-element.535, f32[48,9216]{1,0:T(8,128)} %get-tuple-element.543, s32[4,128]{1,0:T(4,128)S(1)} %dynamic-slice_bitcast_fusion.8), kind=kOutput, calls=%fused_computation.31.clone.1 | convolution fusion | flops 2722627584 | bytes 1869828 | tf_op jit(solution)/shard_map/while/body/eval_jaxpr/sc,bpc->bsp/dot_general | solution.py:75
  349.7 11.0 %fusion.148 = f32[8,4,48,128]{3,2,1,0:T(8,128)S(1)} fusion(f32[8,4,48,128]{3,2,1,0:T(8,128)S(1)} %get-tuple-element.536, s32[]{:T(128)} %get-tuple-element.535, f32[48,9216]{1,0:T(8,128)} %get-tuple-element.543, s32[4,128]{1,0:T(4,128)S(1)} %dynamic-slice_bitcast_fusion.8), kind=kOutput, calls=%fused_computation.31.clone.1 | convolution fusion | flops 2722627584 | bytes 1869828 | tf_op jit(solution)/shard_map/while/body/eval_jaxpr/sc,bpc->bsp/dot_general | solution.py:75
  360.7 11.0 %fusion.148 = f32[8,4,48,128]{3,2,1,0:T(8,128)S(1)} fusion(f32[8,4,48,128]{3,2,1,0:T(8,128)S(1)} %get-tuple-element.536, s32[]{:T(128)} %get-tuple-element.535, f32[48,9216]{1,0:T(8,128)} %get-tuple-element.543, s32[4,128]{1,0:T(4,128)S(1)} %dynamic-slice_bitcast_fusion.8), kind=kOutput, calls=%fused_computation.31.clone.1 | convolution fusion | flops 2722627584 | bytes 1869828 | tf_op jit(solution)/shard_map/while/body/eval_jaxpr/sc,bpc->bsp/dot_general | solution.py:75
  371.8 11.0 %fusion.148 = f32[8,4,48,128]{3,2,1,0:T(8,128)S(1)} fusion(f32[8,4,48,128]{3,2,1,0:T(8,128)S(1)} %get-tuple-element.536, s32[]{:T(128)} %get-tuple-element.535, f32[48,9216]{1,0:T(8,128)} %get-tuple-element.543, s32[4,128]{1,0:T(4,128)S(1)} %dynamic-slice_bitcast_fusion.8), kind=kOutput, calls=%fused_computation.31.clone.1 | convolution fusion | flops 2722627584 | bytes 1869828 | tf_op jit(solution)/shard_map/while/body/eval_jaxpr/sc,bpc->bsp/dot_general | solution.py:75
  382.8 11.0 %fusion.148 = f32[8,4,48,128]{3,2,1,0:T(8,128)S(1)} fusion(f32[8,4,48,128]{3,2,1,0:T(8,128)S(1)} %get-tuple-element.536, s32[]{:T(128)} %get-tuple-element.535, f32[48,9216]{1,0:T(8,128)} %get-tuple-element.543, s32[4,128]{1,0:T(4,128)S(1)} %dynamic-slice_bitcast_fusion.8), kind=kOutput, calls=%fused_computation.31.clone.1 | convolution fusion | flops 2722627584 | bytes 1869828 | tf_op jit(solution)/shard_map/while/body/eval_jaxpr/sc,bpc->bsp/dot_general | solution.py:75
  393.8 11.0 %fusion.148 = f32[8,4,48,128]{3,2,1,0:T(8,128)S(1)} fusion(f32[8,4,48,128]{3,2,1,0:T(8,128)S(1)} %get-tuple-element.536, s32[]{:T(128)} %get-tuple-element.535, f32[48,9216]{1,0:T(8,128)} %get-tuple-element.543, s32[4,128]{1,0:T(4,128)S(1)} %dynamic-slice_bitcast_fusion.8), kind=kOutput, calls=%fused_computation.31.clone.1 | convolution fusion | flops 2722627584 | bytes 1869828 | tf_op jit(solution)/shard_map/while/body/eval_jaxpr/sc,bpc->bsp/dot_general | solution.py:75
  406.4 4.8 collective-permute-start.17
  412.7 5.1 collective-permute-start.19
  417.8 4.5 collective-permute-done.18
  426.6 114.1 %while.73 = (s32[]{:T(128)}, f32[48,9216]{1,0:T(8,128)}, f32[1,9216]{1,0:T(1,128)S(1)}, f32[8,4,48,128]{3,2,1,0:T(8,128)S(1)}, s32[8,4,128]{2,1,0:T(4,128)S(1)}, /*index=5*/s32[]{:T(128)}, s32[]{:T(128)}) while((s32[]{:T(128)}, f32[48,9216]{1,0:T(8,128)}, f32[1,9216]{1,0:T(1,128)S(1)}, f32[8,4,48,128]{3,2,1,0:T(8,128)S(1)}, ...), condition=%wide.region_31.32_spmd.clone, body=%wide.region_29.31_spmd.clone.sunk | while | flops 2737677312 | bytes 3792992 | solution.py:62
  426.8 8.4 %fusion.156 = f32[48,9216]{1,0:T(8,128)} fusion(s32[4,128]{1,0:T(4,128)S(1)} %dynamic-slice_bitcast_fusion.11, f32[48,9216]{1,0:T(8,128)} %get-tuple-element.565, pred[]{:T(512)S(6)} %compare.61, f32[8,4,48,128]{3,2,1,0:T(8,128)S(1)} %get-tuple-element.574, s32[]{:T(128)} %get-tuple-element.564), kind=kOutput, calls=%fused_computation.58.clone.1 | convolution fusion | flops 2723512320 | bytes 3639301 | tf_op jit(solution)/shard_map/while/body/eval_jaxpr/bsp,bpc->sc/dot_general | solution.py:52
  439.7 9.9 %fusion.156 = f32[48,9216]{1,0:T(8,128)} fusion(s32[4,128]{1,0:T(4,128)S(1)} %dynamic-slice_bitcast_fusion.11, f32[48,9216]{1,0:T(8,128)} %get-tuple-element.565, pred[]{:T(512)S(6)} %compare.61, f32[8,4,48,128]{3,2,1,0:T(8,128)S(1)} %get-tuple-element.574, s32[]{:T(128)} %get-tuple-element.564), kind=kOutput, calls=%fused_computation.58.clone.1 | convolution fusion | flops 2723512320 | bytes 3639301 | tf_op jit(solution)/shard_map/while/body/eval_jaxpr/bsp,bpc->sc/dot_general | solution.py:52
  449.6 4.4 fusion.157
  454.2 9.9 %fusion.156 = f32[48,9216]{1,0:T(8,128)} fusion(s32[4,128]{1,0:T(4,128)S(1)} %dynamic-slice_bitcast_fusion.11, f32[48,9216]{1,0:T(8,128)} %get-tuple-element.565, pred[]{:T(512)S(6)} %compare.61, f32[8,4,48,128]{3,2,1,0:T(8,128)S(1)} %get-tuple-element.574, s32[]{:T(128)} %get-tuple-element.564), kind=kOutput, calls=%fused_computation.58.clone.1 | convolution fusion | flops 2723512320 | bytes 3639301 | tf_op jit(solution)/shard_map/while/body/eval_jaxpr/bsp,bpc->sc/dot_general | solution.py:52
  464.0 4.4 fusion.157
  468.6 9.9 %fusion.156 = f32[48,9216]{1,0:T(8,128)} fusion(s32[4,128]{1,0:T(4,128)S(1)} %dynamic-slice_bitcast_fusion.11, f32[48,9216]{1,0:T(8,128)} %get-tuple-element.565, pred[]{:T(512)S(6)} %compare.61, f32[8,4,48,128]{3,2,1,0:T(8,128)S(1)} %get-tuple-element.574, s32[]{:T(128)} %get-tuple-element.564), kind=kOutput, calls=%fused_computation.58.clone.1 | convolution fusion | flops 2723512320 | bytes 3639301 | tf_op jit(solution)/shard_map/while/body/eval_jaxpr/bsp,bpc->sc/dot_general | solution.py:52
  483.0 9.9 %fusion.156 = f32[48,9216]{1,0:T(8,128)} fusion(s32[4,128]{1,0:T(4,128)S(1)} %dynamic-slice_bitcast_fusion.11, f32[48,9216]{1,0:T(8,128)} %get-tuple-element.565, pred[]{:T(512)S(6)} %compare.61, f32[8,4,48,128]{3,2,1,0:T(8,128)S(1)} %get-tuple-element.574, s32[]{:T(128)} %get-tuple-element.564), kind=kOutput, calls=%fused_computation.58.clone.1 | convolution fusion | flops 2723512320 | bytes 3639301 | tf_op jit(solution)/shard_map/while/body/eval_jaxpr/bsp,bpc->sc/dot_general | solution.py:52
  497.4 9.9 %fusion.156 = f32[48,9216]{1,0:T(8,128)} fusion(s32[4,128]{1,0:T(4,128)S(1)} %dynamic-slice_bitcast_fusion.11, f32[48,9216]{1,0:T(8,128)} %get-tuple-element.565, pred[]{:T(512)S(6)} %compare.61, f32[8,4,48,128]{3,2,1,0:T(8,128)S(1)} %get-tuple-element.574, s32[]{:T(128)} %get-tuple-element.564), kind=kOutput, calls=%fused_computation.58.clone.1 | convolution fusion | flops 2723512320 | bytes 3639301 | tf_op jit(solution)/shard_map/while/body/eval_jaxpr/bsp,bpc->sc/dot_general | solution.py:52
  511.8 9.9 %fusion.156 = f32[48,9216]{1,0:T(8,128)} fusion(s32[4,128]{1,0:T(4,128)S(1)} %dynamic-slice_bitcast_fusion.11, f32[48,9216]{1,0:T(8,128)} %get-tuple-element.565, pred[]{:T(512)S(6)} %compare.61, f32[8,4,48,128]{3,2,1,0:T(8,128)S(1)} %get-tuple-element.574, s32[]{:T(128)} %get-tuple-element.564), kind=kOutput, calls=%fused_computation.58.clone.1 | convolution fusion | flops 2723512320 | bytes 3639301 | tf_op jit(solution)/shard_map/while/body/eval_jaxpr/bsp,bpc->sc/dot_general | solution.py:52
  526.3 9.9 %fusion.156 = f32[48,9216]{1,0:T(8,128)} fusion(s32[4,128]{1,0:T(4,128)S(1)} %dynamic-slice_bitcast_fusion.11, f32[48,9216]{1,0:T(8,128)} %get-tuple-element.565, pred[]{:T(512)S(6)} %compare.61, f32[8,4,48,128]{3,2,1,0:T(8,128)S(1)} %get-tuple-element.574, s32[]{:T(128)} %get-tuple-element.564), kind=kOutput, calls=%fused_computation.58.clone.1 | convolution fusion | flops 2723512320 | bytes 3639301 | tf_op jit(solution)/shard_map/while/body/eval_jaxpr/bsp,bpc->sc/dot_general | solution.py:52
  546.9 6.5 collective-permute-done.20
  559.3 4.8 collective-permute-start.23
  568.5 4.8 collective-permute-start.27
  573.2 12.9 %collective-permute-done.26 = f32[5,1,1,1024]{3,1,0,2:T(1,128)S(1)} collective-permute-done((f32[5,1,1,1024]{3,1,0,2:T(1,128)S(1)}, f32[5,1,1,1024]{3,1,0,2:T(1,128)S(1)}, u32[]{:S(2)}, u32[]{:S(2)}) %collective-permute-start.26) | collective-permute-done | bytes 20512 | tf_op jit(solution)/shard_map/ppermute | solution.py:23
  586.4 5.9 pad_maximum_fusion.1
  592.4 60.6 %slice.144 = f32[3,3,48,1024]{3,1,0,2:T(4,128)S(1)} slice(f32[5,5,48,1024]{3,1,0,2:T(8,128)} %pad_maximum_fusion.1), slice={[0:5:2], [0:5:2], [0:48:1], [0:1024:1]} | slice | bytes 3538944 | tf_op jit(solution)/shard_map/slice | solution.py:121
  662.5 5.4 collective-permute-start.31
  667.9 29.0 %while.69 = (s32[]{:T(128)}, f32[32,48,128]{2,1,0:T(8,128)S(1)}, f32[48,48]{1,0:T(8,128)S(1)}, s32[]{:T(128)}) while((s32[]{:T(128)}, f32[32,48,128]{2,1,0:T(8,128)S(1)}, f32[48,48]{1,0:T(8,128)S(1)}, s32[]{:T(128)}) %tuple.156), condition=%wide.region_28.29_spmd, body=%wide.region_27.28_spmd.sunk | while | flops 113639424 | bytes 3154997 | solution.py:38
  703.3 88.3 %while.71 = (s32[]{:T(128)}, f32[8,4,48,128]{3,2,1,0:T(8,128)S(1)}, s32[8,4,128]{2,1,0:T(4,128)S(1)}, f32[48,9216]{1,0:T(8,128)}, s32[]{:T(128)}) while((s32[]{:T(128)}, f32[8,4,48,128]{3,2,1,0:T(8,128)S(1)}, s32[8,4,128]{2,1,0:T(4,128)S(1)}, f32[48,9216]{1,0:T(8,128)}, s32[]{:T(128)}) %tuple.157), condition=%wide.region_35.36_spmd.clone, body=%wide.region_34.35_spmd.clone.sunk | while | flops 2722627584 | bytes 1873989 | solution.py:77
  703.3 11.1 %fusion.150 = f32[8,4,48,128]{3,2,1,0:T(8,128)S(1)} fusion(f32[8,4,48,128]{3,2,1,0:T(8,128)S(1)} %get-tuple-element.584, s32[]{:T(128)} %get-tuple-element.583, f32[48,9216]{1,0:T(8,128)} %get-tuple-element.591, s32[4,128]{1,0:T(4,128)S(1)} %dynamic-slice_bitcast_fusion.9), kind=kOutput, calls=%fused_computation.38.clone.1 | convolution fusion | flops 2722627584 | bytes 1869828 | tf_op jit(solution)/shard_map/while/body/eval_jaxpr/sc,bpc->bsp/dot_general | solution.py:75
  714.4 11.0 %fusion.150 = f32[8,4,48,128]{3,2,1,0:T(8,128)S(1)} fusion(f32[8,4,48,128]{3,2,1,0:T(8,128)S(1)} %get-tuple-element.584, s32[]{:T(128)} %get-tuple-element.583, f32[48,9216]{1,0:T(8,128)} %get-tuple-element.591, s32[4,128]{1,0:T(4,128)S(1)} %dynamic-slice_bitcast_fusion.9), kind=kOutput, calls=%fused_computation.38.clone.1 | convolution fusion | flops 2722627584 | bytes 1869828 | tf_op jit(solution)/shard_map/while/body/eval_jaxpr/sc,bpc->bsp/dot_general | solution.py:75
  725.4 11.0 %fusion.150 = f32[8,4,48,128]{3,2,1,0:T(8,128)S(1)} fusion(f32[8,4,48,128]{3,2,1,0:T(8,128)S(1)} %get-tuple-element.584, s32[]{:T(128)} %get-tuple-element.583, f32[48,9216]{1,0:T(8,128)} %get-tuple-element.591, s32[4,128]{1,0:T(4,128)S(1)} %dynamic-slice_bitcast_fusion.9), kind=kOutput, calls=%fused_computation.38.clone.1 | convolution fusion | flops 2722627584 | bytes 1869828 | tf_op jit(solution)/shard_map/while/body/eval_jaxpr/sc,bpc->bsp/dot_general | solution.py:75
  736.4 11.0 %fusion.150 = f32[8,4,48,128]{3,2,1,0:T(8,128)S(1)} fusion(f32[8,4,48,128]{3,2,1,0:T(8,128)S(1)} %get-tuple-element.584, s32[]{:T(128)} %get-tuple-element.583, f32[48,9216]{1,0:T(8,128)} %get-tuple-element.591, s32[4,128]{1,0:T(4,128)S(1)} %dynamic-slice_bitcast_fusion.9), kind=kOutput, calls=%fused_computation.38.clone.1 | convolution fusion | flops 2722627584 | bytes 1869828 | tf_op jit(solution)/shard_map/while/body/eval_jaxpr/sc,bpc->bsp/dot_general | solution.py:75
  747.5 11.0 %fusion.150 = f32[8,4,48,128]{3,2,1,0:T(8,128)S(1)} fusion(f32[8,4,48,128]{3,2,1,0:T(8,128)S(1)} %get-tuple-element.584, s32[]{:T(128)} %get-tuple-element.583, f32[48,9216]{1,0:T(8,128)} %get-tuple-element.591, s32[4,128]{1,0:T(4,128)S(1)} %dynamic-slice_bitcast_fusion.9), kind=kOutput, calls=%fused_computation.38.clone.1 | convolution fusion | flops 2722627584 | bytes 1869828 | tf_op jit(solution)/shard_map/while/body/eval_jaxpr/sc,bpc->bsp/dot_general | solution.py:75
  758.5 11.0 %fusion.150 = f32[8,4,48,128]{3,2,1,0:T(8,128)S(1)} fusion(f32[8,4,48,128]{3,2,1,0:T(8,128)S(1)} %get-tuple-element.584, s32[]{:T(128)} %get-tuple-element.583, f32[48,9216]{1,0:T(8,128)} %get-tuple-element.591, s32[4,128]{1,0:T(4,128)S(1)} %dynamic-slice_bitcast_fusion.9), kind=kOutput, calls=%fused_computation.38.clone.1 | convolution fusion | flops 2722627584 | bytes 1869828 | tf_op jit(solution)/shard_map/while/body/eval_jaxpr/sc,bpc->bsp/dot_general | solution.py:75
  769.5 11.0 %fusion.150 = f32[8,4,48,128]{3,2,1,0:T(8,128)S(1)} fusion(f32[8,4,48,128]{3,2,1,0:T(8,128)S(1)} %get-tuple-element.584, s32[]{:T(128)} %get-tuple-element.583, f32[48,9216]{1,0:T(8,128)} %get-tuple-element.591, s32[4,128]{1,0:T(4,128)S(1)} %dynamic-slice_bitcast_fusion.9), kind=kOutput, calls=%fused_computation.38.clone.1 | convolution fusion | flops 2722627584 | bytes 1869828 | tf_op jit(solution)/shard_map/while/body/eval_jaxpr/sc,bpc->bsp/dot_general | solution.py:75
  780.6 11.0 %fusion.150 = f32[8,4,48,128]{3,2,1,0:T(8,128)S(1)} fusion(f32[8,4,48,128]{3,2,1,0:T(8,128)S(1)} %get-tuple-element.584, s32[]{:T(128)} %get-tuple-element.583, f32[48,9216]{1,0:T(8,128)} %get-tuple-element.591, s32[4,128]{1,0:T(4,128)S(1)} %dynamic-slice_bitcast_fusion.9), kind=kOutput, calls=%fused_computation.38.clone.1 | convolution fusion | flops 2722627584 | bytes 1869828 | tf_op jit(solution)/shard_map/while/body/eval_jaxpr/sc,bpc->bsp/dot_general | solution.py:75
  (404 shorter events, 202.4 us)
Async XLA Ops:
  0.0 28.4 %copy-start.17 = (s32[2,1,32]{2,1,0:T(1,128)S(1)}, s32[2,1,32]{2,1,0:T(1,128)}, u32[]{:S(2)}) copy-start(s32[2,1,32]{2,1,0:T(1,128)} %param.21) | copy-start | bytes 772
  0.0 22.0 %copy-start.8 = (f32[32,48,128]{2,1,0:T(8,128)S(1)}, f32[32,48,128]{2,1,0:T(8,128)}, u32[]{:S(2)}) copy-start(f32[32,48,128]{2,1,0:T(8,128)} %param.18) | copy-start | bytes 2359300
  0.0 28.7 %copy-start.19 = (s32[2,32]{1,0:T(2,128)S(1)}, s32[2,32]{1,0:T(2,128)}, u32[]{:S(2)}) copy-start(s32[2,32]{1,0:T(2,128)} %param.22) | copy-start | bytes 772
  0.0 28.7 %copy-start.16 = (s32[2,32,128]{2,1,0:T(8,128)S(1)}, s32[2,32,128]{2,1,0:T(8,128)}, u32[]{:S(2)}) copy-start(s32[2,32,128]{2,1,0:T(8,128)} %param.23) | copy-start | bytes 98308
  5.7 26.5 %collective-permute-start = (f32[8,48,128]{2,1,0:T(8,128)S(1)}, f32[8,48,128]{2,1,0:T(8,128)S(1)}, u32[]{:S(2)}, u32[]{:S(2)}) collective-permute-start(f32[8,48,128]{2,1,0:T(8,128)S(1)} %broadcast_select_fusion.11), channel_id=1, source_target_pairs={{0,1},{1,2},{2,3},{3,4},{4,5},{5,6},{6,7},{7,8},{8,9},{9,10},{10,1... | collective-permute-start | bytes 589832 | tf_op jit(solution)/shard_map/ppermute | solution.py:14
  11.4 20.8 %collective-permute-start.1 = (f32[8,48,128]{2,1,0:T(8,128)S(1)}, f32[8,48,128]{2,1,0:T(8,128)S(1)}, u32[]{:S(2)}, u32[]{:S(2)}) collective-permute-start(f32[8,48,128]{2,1,0:T(8,128)S(1)} %broadcast_select_fusion.10), channel_id=1, source_target_pairs={{0,15},{1,0},{2,1},{3,2},{4,3},{5,4},{6,5},{7,6},{8,7},{9,8},{10,9... | collective-permute-start | bytes 589832 | tf_op jit(solution)/shard_map/ppermute | solution.py:14
  20.2 12.0 %collective-permute-start.2 = (f32[8,48,128]{2,1,0:T(8,128)S(1)}, f32[8,48,128]{2,1,0:T(8,128)S(1)}, u32[]{:S(2)}, u32[]{:S(2)}) collective-permute-start(f32[8,48,128]{2,1,0:T(8,128)S(1)} %broadcast_select_fusion.9), channel_id=1, source_target_pairs={{0,2},{1,3},{2,4},{3,5},{4,6},{5,7},{6,8},{7,9},{8,10},{9,11},{10,... | collective-permute-start | bytes 589832 | tf_op jit(solution)/shard_map/ppermute | solution.py:14
  23.3 11.6 %collective-permute-start.3 = (f32[8,48,128]{2,1,0:T(8,128)S(1)}, f32[8,48,128]{2,1,0:T(8,128)S(1)}, u32[]{:S(2)}, u32[]{:S(2)}) collective-permute-start(f32[8,48,128]{2,1,0:T(8,128)S(1)} %broadcast_select_fusion.8), channel_id=1, source_target_pairs={{0,14},{1,15},{2,0},{3,1},{4,2},{5,3},{6,4},{7,5},{8,6},{9,7},{10,... | collective-permute-start | bytes 589832 | tf_op jit(solution)/shard_map/ppermute | solution.py:14
  150.4 120.4 %copy-start = (f32[8,4,48,128]{3,2,1,0:T(8,128)}, f32[8,4,48,128]{3,2,1,0:T(8,128)S(1)}, u32[]{:S(2)}) copy-start(f32[8,4,48,128]{3,2,1,0:T(8,128)S(1)} %get-tuple-element.593) | copy-start | bytes 2359300
  155.4 8.4 %collective-permute-start.4 = (f32[1,3,48,1024]{3,2,1,0:T(8,128)}, f32[1,3,48,1024]{3,2,1,0:T(8,128)}, u32[]{:S(2)}, u32[]{:S(2)}) collective-permute-start(f32[1,3,48,1024]{3,2,1,0:T(8,128)} %copy.27), channel_id=1, source_target_pairs={{0,16},{16,32},{32,48},{48,64},{64,80},{80,96},{96,112},{112,0},{1... | collective-permute-start | bytes 1769480 | tf_op jit(solution)/shard_map/ppermute | solution.py:23
  157.8 9.6 %collective-permute-start.5 = (f32[1,3,48,1024]{3,2,1,0:T(8,128)}, f32[1,3,48,1024]{3,2,1,0:T(8,128)}, u32[]{:S(2)}, u32[]{:S(2)}) collective-permute-start(f32[1,3,48,1024]{3,2,1,0:T(8,128)} %copy.28), channel_id=1, source_target_pairs={{16,0},{32,16},{48,32},{64,48},{80,64},{96,80},{112,96},{0,112},{1... | collective-permute-start | bytes 1769480 | tf_op jit(solution)/shard_map/ppermute | solution.py:26
  165.3 3.6 copy-start.4
  168.9 2.6 copy-start.5
  171.5 27.8 %collective-permute-start.6 = (f32[5,1,48,1024]{3,1,0,2:T(1,128)}, f32[5,1,48,1024]{3,1,0,2:T(1,128)}, u32[]{:S(2)}, u32[]{:S(2)}) collective-permute-start(f32[5,1,48,1024]{3,1,0,2:T(1,128)} %get-tuple-element.305), channel_id=1, source_target_pairs={{0,1},{1,2},{2,3},{3,4},{4,5},{5,6},{6,7},{7,8},{8,9},{9,10},{10,1... | collective-permute-start | bytes 2949128 | tf_op jit(solution)/shard_map/ppermute | solution.py:23
  171.5 27.8 %collective-permute-start.7 = (f32[5,1,48,1024]{3,1,0,2:T(1,128)}, f32[5,1,48,1024]{3,1,0,2:T(1,128)}, u32[]{:S(2)}, u32[]{:S(2)}) collective-permute-start(f32[5,1,48,1024]{3,1,0,2:T(1,128)} %get-tuple-element.306), channel_id=1, source_target_pairs={{1,0},{2,1},{3,2},{4,3},{5,4},{6,5},{7,6},{8,7},{9,8},{10,9},{11,1... | collective-permute-start | bytes 2949128 | tf_op jit(solution)/shard_map/ppermute | solution.py:26
  176.4 3.1 collective-permute-start.8
  177.6 3.6 collective-permute-start.9
  181.2 17.9 %collective-permute-start.10 = (f32[5,1,1,1024]{3,1,0,2:T(1,128)S(1)}, f32[5,1,1,1024]{3,1,0,2:T(1,128)S(1)}, u32[]{:S(2)}, u32[]{:S(2)}) collective-permute-start(f32[5,1,1,1024]{3,1,0,2:T(1,128)S(1)} %get-tuple-element.313), channel_id=1, source_target_pairs={{0,1},{1,2},{2,3},{3,4},{4,5},{5,6},{6,7},{7,8},{8,9},{9,10},{10,1... | collective-permute-start | bytes 61448 | tf_op jit(solution)/shard_map/ppermute | solution.py:23
  181.3 17.8 %collective-permute-start.11 = (f32[5,1,1,1024]{3,1,0,2:T(1,128)S(1)}, f32[5,1,1,1024]{3,1,0,2:T(1,128)S(1)}, u32[]{:S(2)}, u32[]{:S(2)}) collective-permute-start(f32[5,1,1,1024]{3,1,0,2:T(1,128)S(1)} %get-tuple-element.314), channel_id=1, source_target_pairs={{1,0},{2,1},{3,2},{4,3},{5,4},{6,5},{7,6},{8,7},{9,8},{10,9},{11,1... | collective-permute-start | bytes 61448 | tf_op jit(solution)/shard_map/ppermute | solution.py:26
  265.9 15.1 %copy-start.9 = (f32[48,48]{1,0:T(8,128)S(1)}, f32[48,48]{1,0:T(8,128)}, u32[]{:S(2)}) copy-start(f32[48,48]{1,0:T(8,128)} %param.19) | copy-start | bytes 27652
  268.6 4.1 collective-permute-start.12
  270.0 5.1 collective-permute-start.13
  272.6 8.4 %copy-start.10 = (f32[1,1,48,1024]{3,1,0,2:T(1,128)}, f32[1,1,48,1024]{3,1,0,2:T(1,128)S(1)}, u32[]{:S(2)}) copy-start(f32[1,1,48,1024]{3,1,0,2:T(1,128)S(1)} %collective-permute-done.12) | copy-start | bytes 589828
  275.1 5.9 copy-start.11
  275.6 34.5 %collective-permute-start.14 = (f32[3,1,48,1024]{3,1,0,2:T(1,128)S(1)}, f32[3,1,48,1024]{3,1,0,2:T(1,128)S(1)}, u32[]{:S(2)}, u32[]{:S(2)}) collective-permute-start(f32[3,1,48,1024]{3,1,0,2:T(1,128)S(1)} %pad_maximum_fusion.10), channel_id=1, source_target_pairs={{0,1},{1,2},{2,3},{3,4},{4,5},{5,6},{6,7},{7,8},{8,9},{9,10},{10,1... | collective-permute-start | bytes 1769480 | tf_op jit(solution)/shard_map/ppermute | solution.py:23
  275.7 35.3 %collective-permute-start.15 = (f32[3,1,48,1024]{3,1,0,2:T(1,128)S(1)}, f32[3,1,48,1024]{3,1,0,2:T(1,128)}, u32[]{:S(2)}, u32[]{:S(2)}) collective-permute-start(f32[3,1,48,1024]{3,1,0,2:T(1,128)S(1)} %pad_maximum_fusion.10), channel_id=1, source_target_pairs={{1,0},{2,1},{3,2},{4,3},{5,4},{6,5},{7,6},{8,7},{9,8},{10,9},{11,1... | collective-permute-start | bytes 1769480 | tf_op jit(solution)/shard_map/ppermute | solution.py:26
  310.2 0.8 copy-start.14
  316.5 88.3 %copy-start.1 = (f32[8,4,48,128]{3,2,1,0:T(8,128)S(1)}, f32[8,4,48,128]{3,2,1,0:T(8,128)}, u32[]{:S(2)}) copy-start(f32[8,4,48,128]{3,2,1,0:T(8,128)} %copy-done) | copy-start | bytes 2359300
  316.5 88.3 %copy-start.18 = (f32[48]{0:T(128)S(1)}, f32[48]{0:T(128)}, u32[]{:S(2)}) copy-start(f32[48]{0:T(128)} %param.20) | copy-start | bytes 580
  405.7 12.1 %collective-permute-start.16 = (f32[8,48,128]{2,1,0:T(8,128)S(1)}, f32[8,48,128]{2,1,0:T(8,128)S(1)}, u32[]{:S(2)}, u32[]{:S(2)}) collective-permute-start(f32[8,48,128]{2,1,0:T(8,128)S(1)} %broadcast_select_fusion.7), channel_id=1, source_target_pairs={{0,1},{1,2},{2,3},{3,4},{4,5},{5,6},{6,7},{7,8},{8,9},{9,10},{10,1... | collective-permute-start | bytes 589832 | tf_op jit(solution)/shard_map/ppermute | solution.py:14
  406.4 11.4 %collective-permute-start.17 = (f32[8,48,128]{2,1,0:T(8,128)S(1)}, f32[8,48,128]{2,1,0:T(8,128)S(1)}, u32[]{:S(2)}, u32[]{:S(2)}) collective-permute-start(f32[8,48,128]{2,1,0:T(8,128)S(1)} %broadcast_select_fusion.6), channel_id=1, source_target_pairs={{0,15},{1,0},{2,1},{3,2},{4,3},{5,4},{6,5},{7,6},{8,7},{9,8},{10,9... | collective-permute-start | bytes 589832 | tf_op jit(solution)/shard_map/ppermute | solution.py:14
  411.9 10.4 %collective-permute-start.18 = (f32[8,48,128]{2,1,0:T(8,128)S(1)}, f32[8,48,128]{2,1,0:T(8,128)S(1)}, u32[]{:S(2)}, u32[]{:S(2)}) collective-permute-start(f32[8,48,128]{2,1,0:T(8,128)S(1)} %broadcast_select_fusion.5), channel_id=1, source_target_pairs={{0,2},{1,3},{2,4},{3,5},{4,6},{5,7},{6,8},{7,9},{8,10},{9,11},{10,... | collective-permute-start | bytes 589832 | tf_op jit(solution)/shard_map/ppermute | solution.py:14
  412.7 12.5 %collective-permute-start.19 = (f32[8,48,128]{2,1,0:T(8,128)S(1)}, f32[8,48,128]{2,1,0:T(8,128)S(1)}, u32[]{:S(2)}, u32[]{:S(2)}) collective-permute-start(f32[8,48,128]{2,1,0:T(8,128)S(1)} %broadcast_select_fusion.4), channel_id=1, source_target_pairs={{0,14},{1,15},{2,0},{3,1},{4,2},{5,3},{6,4},{7,5},{8,6},{9,7},{10,... | collective-permute-start | bytes 589832 | tf_op jit(solution)/shard_map/ppermute | solution.py:14
  540.7 116.2 %copy-start.2 = (f32[8,4,48,128]{3,2,1,0:T(8,128)}, f32[8,4,48,128]{3,2,1,0:T(8,128)S(1)}, u32[]{:S(2)}) copy-start(f32[8,4,48,128]{3,2,1,0:T(8,128)S(1)} %get-tuple-element.594) | copy-start | bytes 2359300
  544.8 8.6 %collective-permute-start.20 = (f32[1,3,48,1024]{3,2,1,0:T(8,128)S(1)}, f32[1,3,48,1024]{3,2,1,0:T(8,128)S(1)}, u32[]{:S(2)}, u32[]{:S(2)}) collective-permute-start(f32[1,3,48,1024]{3,2,1,0:T(8,128)S(1)} %copy.33), channel_id=1, source_target_pairs={{0,16},{16,32},{32,48},{48,64},{64,80},{80,96},{96,112},{112,0},{1... | collective-permute-start | bytes 1769480 | tf_op jit(solution)/shard_map/ppermute | solution.py:23
  546.9 9.3 %collective-permute-start.21 = (f32[1,3,48,1024]{3,2,1,0:T(8,128)S(1)}, f32[1,3,48,1024]{3,2,1,0:T(8,128)S(1)}, u32[]{:S(2)}, u32[]{:S(2)}) collective-permute-start(f32[1,3,48,1024]{3,2,1,0:T(8,128)S(1)} %copy.34), channel_id=1, source_target_pairs={{16,0},{32,16},{48,32},{64,48},{80,64},{96,80},{112,96},{0,112},{1... | collective-permute-start | bytes 1769480 | tf_op jit(solution)/shard_map/ppermute | solution.py:26
  553.8 5.4 copy-start.6
  556.6 2.6 copy-start.7
  559.2 27.2 %collective-permute-start.22 = (f32[5,1,48,1024]{3,1,0,2:T(1,128)}, f32[5,1,48,1024]{3,1,0,2:T(1,128)}, u32[]{:S(2)}, u32[]{:S(2)}) collective-permute-start(f32[5,1,48,1024]{3,1,0,2:T(1,128)} %get-tuple-element.303), channel_id=1, source_target_pairs={{0,1},{1,2},{2,3},{3,4},{4,5},{5,6},{6,7},{7,8},{8,9},{9,10},{10,1... | collective-permute-start | bytes 2949128 | tf_op jit(solution)/shard_map/ppermute | solution.py:23
  559.3 27.2 %collective-permute-start.23 = (f32[5,1,48,1024]{3,1,0,2:T(1,128)}, f32[5,1,48,1024]{3,1,0,2:T(1,128)}, u32[]{:S(2)}, u32[]{:S(2)}) collective-permute-start(f32[5,1,48,1024]{3,1,0,2:T(1,128)} %get-tuple-element.304), channel_id=1, source_target_pairs={{1,0},{2,1},{3,2},{4,3},{5,4},{6,5},{7,6},{8,7},{9,8},{10,9},{11,1... | collective-permute-start | bytes 2949128 | tf_op jit(solution)/shard_map/ppermute | solution.py:26
  564.1 1.5 collective-permute-start.24
  564.8 3.6 collective-permute-start.25
  568.4 17.8 %collective-permute-start.26 = (f32[5,1,1,1024]{3,1,0,2:T(1,128)S(1)}, f32[5,1,1,1024]{3,1,0,2:T(1,128)S(1)}, u32[]{:S(2)}, u32[]{:S(2)}) collective-permute-start(f32[5,1,1,1024]{3,1,0,2:T(1,128)S(1)} %get-tuple-element.311), channel_id=1, source_target_pairs={{0,1},{1,2},{2,3},{3,4},{4,5},{5,6},{6,7},{7,8},{8,9},{9,10},{10,1... | collective-permute-start | bytes 61448 | tf_op jit(solution)/shard_map/ppermute | solution.py:23
  568.5 17.7 %collective-permute-start.27 = (f32[5,1,1,1024]{3,1,0,2:T(1,128)S(1)}, f32[5,1,1,1024]{3,1,0,2:T(1,128)S(1)}, u32[]{:S(2)}, u32[]{:S(2)}) collective-permute-start(f32[5,1,1,1024]{3,1,0,2:T(1,128)S(1)} %get-tuple-element.312), channel_id=1, source_target_pairs={{1,0},{2,1},{3,2},{4,3},{5,4},{6,5},{7,6},{8,7},{9,8},{10,9},{11,1... | collective-permute-start | bytes 61448 | tf_op jit(solution)/shard_map/ppermute | solution.py:26
  655.6 3.8 collective-permute-start.28
  656.9 5.1 collective-permute-start.29
  659.5 8.4 %copy-start.12 = (f32[1,1,48,1024]{3,1,0,2:T(1,128)}, f32[1,1,48,1024]{3,1,0,2:T(1,128)S(1)}, u32[]{:S(2)}) copy-start(f32[1,1,48,1024]{3,1,0,2:T(1,128)S(1)} %collective-permute-done.28) | copy-start | bytes 589828
  661.9 6.0 copy-start.13
  662.5 34.4 %collective-permute-start.30 = (f32[3,1,48,1024]{3,1,0,2:T(1,128)S(1)}, f32[3,1,48,1024]{3,1,0,2:T(1,128)S(1)}, u32[]{:S(2)}, u32[]{:S(2)}) collective-permute-start(f32[3,1,48,1024]{3,1,0,2:T(1,128)S(1)} %pad_maximum_fusion.11), channel_id=1, source_target_pairs={{0,1},{1,2},{2,3},{3,4},{4,5},{5,6},{6,7},{7,8},{8,9},{9,10},{10,1... | collective-permute-start | bytes 1769480 | tf_op jit(solution)/shard_map/ppermute | solution.py:23
  662.5 35.2 %collective-permute-start.31 = (f32[3,1,48,1024]{3,1,0,2:T(1,128)S(1)}, f32[3,1,48,1024]{3,1,0,2:T(1,128)}, u32[]{:S(2)}, u32[]{:S(2)}) collective-permute-start(f32[3,1,48,1024]{3,1,0,2:T(1,128)S(1)} %pad_maximum_fusion.11), channel_id=1, source_target_pairs={{1,0},{2,1},{3,2},{4,3},{5,4},{6,5},{7,6},{8,7},{9,8},{10,9},{11,1... | collective-permute-start | bytes 1769480 | tf_op jit(solution)/shard_map/ppermute | solution.py:26
  696.9 0.8 copy-start.15
  703.2 88.3 %copy-start.3 = (f32[8,4,48,128]{3,2,1,0:T(8,128)S(1)}, f32[8,4,48,128]{3,2,1,0:T(8,128)}, u32[]{:S(2)}) copy-start(f32[8,4,48,128]{3,2,1,0:T(8,128)} %copy-done.2) | copy-start | bytes 2359300
where the time goes:
time: 805 us; the launch traced here: 793 us
  matrix products  383 us (48%)
  local copies, waits for them, and re-layouts  158 us (20%)
  other arithmetic  125 us (16%)
  waiting for transfers between devices  62.4 us (8%)
  starting transfers between devices  59.4 us (7%)
    dot_general x16, matrix products, select(): jnp.einsum('sc,bpc->bsp', means, onehot, precision=lax.Precision.HIGHEST)  176 us
    dot_general x16, matrix products, accumulate(): jnp.einsum('bsp,bpc->sc', piece_state, onehot, precision=lax.Precision.HI...  155 us
    slice x2, local copies, waits for them, and re-layouts, shards(): total_sums = jnp.sum(rim_sums[0::2, 0::2], axis=(0, 1))  121 us
    reduce_sum x16, other arithmetic, accumulate(): counts = counts + jnp.sum(onehot, axis=(0, 1))[None, :]  71 us
    dot_general x64, matrix products, advance(): jnp.einsum('st,btp->bsp', reaction_rates, current, precision=lax.Precisio...  52.2 us
    ppermute x12, waiting for transfers between devices, padded(): lax.ppermute(lax.slice_in_dim(block, block.shape[dim] - width, None, axis...  38.4 us
    ppermute x12, starting transfers between devices, padded(): lax.ppermute(lax.slice_in_dim(block, 0, width, axis=dim), axis, backward)  29.8 us
    ppermute x8, starting transfers between devices, passed_along(): return lax.ppermute(value, axis, pairs)  21.7 us
  transfers between devices with their start and end apart: 32, of which 16 were waited for; matrix products, arithmetic and copies ran while one was open for 11% of the time, Pallas kernels for 0%

commit v1 on v0

v1 whole, which is shorter than its diff:
```python
import functools

import jax
import jax.numpy as jnp
from jax import lax
from jax.experimental import pallas as pl
from jax.experimental.pallas import tpu as pltpu
from jax.sharding import PartitionSpec as P

S = 48
LANES = 128
BLK = 32
CELL_DEV = 1024
ROWS = CELL_DEV // 2
STEPS = 2
SUB = 32
MOST = 8
BASES = (0, 8, 16, 20)
SIZES = (8, 8, 4, 4)
OFFSETS = (1, -1, 2, -2)
OUTGOING = 24
ACCS = 4
CHUNKS = 2
CHUNK = ROWS // CHUNKS
F32 = jnp.float32
BF16 = jnp.bfloat16
MESH = pl.DeviceIdType.MESH
VMEM = pl.BlockSpec(memory_space=pltpu.VMEM)
SMEM = pl.BlockSpec(memory_space=pltpu.SMEM)
LIMIT = 48 * 2**20


def around(axis, step):
    count = lax.axis_size(axis)
    return lax.rem(lax.axis_index(axis) + step + count, count)


def prepare_kernel(shift_ref, arrival_ref, place_ref, cell_ref, send_ref, source_ref, row_ref, half_ref, pool_ref):
    band = place_ref[0]
    sector = place_ref[1]
    cell = cell_ref[...]
    owner = cell // CELL_DEV
    rel_band = owner // 16 - band + 1
    rel_sector = (owner % 16 - sector + 17) % 16
    row_ref[...] = jnp.clip((rel_band * 3 + rel_sector) * ROWS + cell % ROWS, 0, 9 * ROWS - 1)
    half_ref[...] = (cell // ROWS) % 2
    for step in range(STEPS):
        for k in range(OUTGOING):
            send_ref[step, k] = 0

        def place(slot, counts):
            moved_by = shift_ref[step, 0, slot]
            pool = slot
            later = []
            for offset, base, size, count in zip(OFFSETS, BASES, SIZES, counts):
                hit = moved_by == offset
                where = base + jnp.minimum(count, size - 1)

                @pl.when(hit)
                def _():
                    send_ref[step, where] = slot

                pool = jnp.where(hit, BLK + where, pool)
                later.append(count + hit.astype(jnp.int32))
            pool_ref[slot] = pool
            return tuple(later)

        lax.fori_loop(0, BLK, place, (jnp.int32(0),) * 4)

        @pl.loop(0, BLK)
        def _(slot):
            source_ref[step, slot] = pool_ref[arrival_ref[step, slot]]


def prepare(shift_list, arrival, cell_index):
    place = jnp.stack([lax.axis_index("lat"), lax.axis_index("lon")]).astype(jnp.int32)
    return pl.pallas_call(
        prepare_kernel,
        out_shape=(
            jax.ShapeDtypeStruct((STEPS, OUTGOING), jnp.int32),
            jax.ShapeDtypeStruct((STEPS, BLK), jnp.int32),
            jax.ShapeDtypeStruct((STEPS, BLK, LANES), jnp.int32),
            jax.ShapeDtypeStruct((STEPS, BLK, LANES), jnp.int32),
        ),
        in_specs=[SMEM, SMEM, SMEM, VMEM],
        out_specs=(SMEM, SMEM, VMEM, VMEM),
        scratch_shapes=[pltpu.SMEM((BLK,), jnp.int32)],
        name="prepare",
    )(shift_list, arrival, place, cell_index)


def migrate_kernel(send_ref, source_ref, state_ref, moved_ref, outgoing, pool, send_sem, recv_sem):
    band = lax.axis_index("lat")
    polar = (band == 0) | (band == lax.axis_size("lat") - 1)
    barrier = pltpu.get_barrier_semaphore()
    for offset in OFFSETS:
        pl.semaphore_signal(barrier, inc=1, device_id={"lon": around("lon", offset)}, device_id_type=MESH)

    for k in range(OUTGOING):
        outgoing[k] = state_ref[send_ref[k]]
    pl.semaphore_wait(barrier, len(OFFSETS))

    def copies(share):
        return [
            pltpu.make_async_remote_copy(
                src_ref=outgoing.at[pl.ds(base, size // share)],
                dst_ref=pool.at[pl.ds(BLK + base, size // share)],
                send_sem=send_sem.at[d],
                recv_sem=recv_sem.at[d],
                device_id={"lon": around("lon", offset)},
                device_id_type=MESH,
            )
            for d, (offset, base, size) in enumerate(zip(OFFSETS, BASES, SIZES))
        ]

    def exchange(share):
        moving = copies(share)
        for copy in moving:
            copy.start()
        pool[0:BLK] = state_ref[...]
        for copy in moving:
            copy.wait()

    @pl.when(polar)
    def _():
        exchange(1)

    @pl.when(jnp.logical_not(polar))
    def _():
        exchange(2)

    @pl.loop(0, BLK, unroll=4)
    def _(slot):
        moved_ref[slot] = pool[source_ref[slot]]


def migrate(send, source, state):
    return pl.pallas_call(
        migrate_kernel,
        out_shape=jax.ShapeDtypeStruct((BLK, S, LANES), F32),
        in_specs=[SMEM, SMEM, VMEM],
        out_specs=VMEM,
        scratch_shapes=[
            pltpu.VMEM((OUTGOING, S, LANES), F32),
            pltpu.VMEM((BLK + OUTGOING, S, LANES), F32),
            pltpu.SemaphoreType.DMA((4,)),
            pltpu.SemaphoreType.DMA((4,)),
        ],
        compiler_params=pltpu.CompilerParams(collective_id=1, has_side_effects=True, vmem_limit_bytes=LIMIT),
        name="migrate",
    )(send, source, state)


def deposit_kernel(moved_ref, half_ref, row_ref, sums_ref, rows, *accs):
    blank = jnp.zeros((8, LANES), F32)
    tail = jnp.where(lax.broadcasted_iota(jnp.int32, (16, LANES), 0) == 0, 1.0, 0.0)

    @pl.loop(0, 9 * ROWS // 8, unroll=8)
    def _(i):
        part = pl.ds(pl.multiple_of(i * 8, 8), 8)
        for acc in accs:
            acc[part, :] = blank

    @pl.loop(0, BLK, unroll=2)
    def _(b):
        block = jnp.concatenate([moved_ref[b], tail], 0)
        half = half_ref[pl.ds(b, 1), :]
        both = jnp.concatenate([jnp.where(half == 0, block, 0.0), jnp.where(half == 0, 0.0, block)], 0)
        rows[pl.ds(pl.multiple_of(b * LANES, LANES), LANES), :] = both.T

    @pl.loop(0, BLK)
    def _(b):
        @pl.loop(0, LANES // 32)
        def _(g):
            first = g * 32
            start = pl.multiple_of(b * LANES + first, 32)
            for k in range(32):
                acc = accs[k % ACCS]
                at = pl.ds(row_ref[b, first + k], 1)
                acc[at, :] = acc[at, :] + rows[pl.ds(start + k, 1), :]

    @pl.loop(0, 9 * ROWS // 8, unroll=4)
    def _(i):
        part = pl.ds(pl.multiple_of(i * 8, 8), 8)
        total = accs[0][part, :]
        for acc in accs[1:]:
            total = total + acc[part, :]
        sums_ref[part, :] = total


def deposit(moved, half, row):
    sums = pl.pallas_call(
        deposit_kernel,
        out_shape=jax.ShapeDtypeStruct((9 * ROWS, LANES), F32),
        in_specs=[VMEM, VMEM, SMEM],
        out_specs=VMEM,
        scratch_shapes=[pltpu.VMEM((BLK * LANES, LANES), F32)] + [pltpu.VMEM((9 * ROWS, LANES), F32)] * ACCS,
        compiler_params=pltpu.CompilerParams(vmem_limit_bytes=LIMIT),
        name="deposit",
    )(moved, half, row)
    return sums.reshape(3, 3, ROWS, LANES)


def split(x):
    high = x.astype(BF16)
    return high, (x - high.astype(F32)).astype(BF16)


def pairs_of(rates):
    zero = jnp.zeros((S, S), F32)
    high, low = split(jnp.concatenate([jnp.concatenate([rates, zero], 1), jnp.concatenate([zero, rates], 1)], 0))
    return jnp.concatenate([high, high], 1), low


def exchange_kernel(
    sums_ref, moved_ref, rates_ref, mix_ref, half_ref, row_ref, out_ref,
    below, above, middle, left, right, table, chem, high2, low1, rows,
    up_sem, down_sem, west_sem, east_sem, mwest_sem, meast_sem, mup_sem, mdown_sem,
):
    band = lax.axis_index("lat")
    bands = lax.axis_size("lat")
    has_up = band < bands - 1
    has_down = band > 0
    up = jnp.minimum(band + 1, bands - 1)
    down = jnp.maximum(band - 1, 0)
    east = around("lon", 1)
    west = around("lon", -1)
    barrier = pltpu.get_barrier_semaphore()
    for sector in (east, west):
        pl.semaphore_signal(barrier, inc=1, device_id={"lon": sector}, device_id_type=MESH)

    @pl.when(has_up)
    def _():
        pl.semaphore_signal(barrier, inc=1, device_id={"lat": up}, device_id_type=MESH)

    @pl.when(has_down)
    def _():
        pl.semaphore_signal(barrier, inc=1, device_id={"lat": down}, device_id_type=MESH)

    pl.semaphore_wait(barrier, 2 + has_up.astype(jnp.int32) + has_down.astype(jnp.int32))

    def remote(src, dst, sem, index, device):
        return pltpu.make_async_remote_copy(
            src_ref=src, dst_ref=dst, send_sem=sem.at[(0,) + index], recv_sem=sem.at[(1,) + index],
            device_id=device, device_id_type=MESH,
        )

    def chunk(c):
        return pl.ds(c * CHUNK, CHUNK)

    def sums_up(s, c):
        return remote(sums_ref.at[2, s, chunk(c)], below.at[s, chunk(c)], up_sem, (s, c), {"lat": up})

    def sums_down(s, c):
        return remote(sums_ref.at[0, s, chunk(c)], above.at[s, chunk(c)], down_sem, (s, c), {"lat": down})

    def sums_west(c):
        return remote(middle.at[0, chunk(c)], right.at[chunk(c)], west_sem, (c,), {"lon": west})

    def sums_east(c):
        return remote(middle.at[2, chunk(c)], left.at[chunk(c)], east_sem, (c,), {"lon": east})

    def means_west(c):
        return remote(table.at[1, 1, chunk(c)], table.at[1, 2, chunk(c)], mwest_sem, (c,), {"lon": west})

    def means_east(c):
        return remote(table.at[1, 1, chunk(c)], table.at[1, 0, chunk(c)], meast_sem, (c,), {"lon": east})

    def means_up(s, c):
        return remote(table.at[1, s, chunk(c)], table.at[0, s, chunk(c)], mup_sem, (s, c), {"lat": up})

    def means_down(s, c):
        return remote(table.at[1, s, chunk(c)], table.at[2, s, chunk(c)], mdown_sem, (s, c), {"lat": down})

    order = [(s, c) for c in range(CHUNKS) for s in (0, 2, 1)]

    @pl.when(has_up)
    def _():
        for s, c in order:
            sums_up(s, c).start()

    @pl.when(has_down)
    def _():
        for s, c in order:
            sums_down(s, c).start()

    @pl.when(jnp.logical_not(has_down))
    def _():
        below[...] = jnp.zeros_like(below)
        table[0] = jnp.zeros_like(table[0])

    @pl.when(jnp.logical_not(has_up))
    def _():
        above[...] = jnp.zeros_like(above)
        table[2] = jnp.zeros_like(table[2])

    high, low = pairs_of(rates_ref[...])
    high2[...] = high
    low1[...] = low
    for b in range(BLK):
        chem[(b % 2) * S:(b % 2) * S + S, (b // 2) * LANES:(b // 2 + 1) * LANES] = moved_ref[b]

    def chemistry(substeps):
        def advance(_, current):
            state = chem[...]
            high, low = split(state)
            pushed = jnp.dot(high2[...], jnp.concatenate([high, low], 0), preferred_element_type=F32)
            pushed = pushed + jnp.dot(low1[...], high, preferred_element_type=F32)
            chem[...] = state + (2.0 / SUB) * jnp.tanh(pushed)
            return current

        lax.fori_loop(0, substeps, advance, 0)

    def strips(body):
        @pl.loop(0, CHUNK // 8, unroll=4)
        def _(i):
            body(pl.multiple_of(i * 8, 8))

    chemistry(12)
    for c in range(CHUNKS):
        for s in (0, 2, 1):
            @pl.when(has_down)
            def _():
                sums_up(s, c).wait_recv()

            @pl.when(has_up)
            def _():
                sums_down(s, c).wait_recv()

            def add_bands(i):
                part = pl.ds(c * CHUNK + i, 8)
                middle[s, part, :] = sums_ref[1, s, part, :] + below[s, part, :] + above[s, part, :]

            strips(add_bands)
            if s == 0:
                sums_west(c).start()
            if s == 2:
                sums_east(c).start()

    chemistry(10)
    lane = lax.broadcasted_iota(jnp.int32, (8, LANES), 1)
    for c in range(CHUNKS):
        sums_west(c).wait_recv()
        sums_east(c).wait_recv()

        def mean(i):
            part = pl.ds(c * CHUNK + i, 8)
            total = middle[1, part, :] + left[part, :] + right[part, :]
            count = jnp.where(lane < 64, total[:, S:S + 1], total[:, 64 + S:64 + S + 1])
            table[1, 1, part, :] = total / jnp.maximum(count, 1.0)

        strips(mean)
        means_west(c).start()
        means_east(c).start()

        @pl.when(has_up)
        def _():
            means_up(1, c).start()

        @pl.when(has_down)
        def _():
            means_down(1, c).start()

    chemistry(5)
    for c in range(CHUNKS):
        means_west(c).wait_recv()
        means_east(c).wait_recv()

        @pl.when(has_up)
        def _():
            means_up(0, c).start()
            means_up(2, c).start()

        @pl.when(has_down)
        def _():
            means_down(0, c).start()
            means_down(2, c).start()

    chemistry(5)
    for s, c in order:
        @pl.when(has_up)
        def _():
            means_down(s, c).wait_recv()
            sums_up(s, c).wait_send()
            means_up(s, c).wait_send()

        @pl.when(has_down)
        def _():
            means_up(s, c).wait_recv()
            sums_down(s, c).wait_send()
            means_down(s, c).wait_send()
    for c in range(CHUNKS):
        for copy in (sums_west(c), sums_east(c), means_west(c), means_east(c)):
            copy.wait_send()

    @pl.loop(0, BLK)
    def _(b):
        @pl.loop(0, LANES // 32)
        def _(g):
            first = g * 32
            start = pl.multiple_of(b * LANES + first, 32)
            for k in range(32):
                rows[pl.ds(start + k, 1), :] = table_rows(table, row_ref[b, first + k])

    mix = mix_ref[...]

    @pl.loop(0, BLK // 2)
    def _(pair):
        for side in range(2):
            b = pair * 2 + side
            means = rows[pl.ds(pl.multiple_of(b * LANES, LANES), LANES), :].T
            picked = jnp.where(half_ref[pl.ds(b, 1), :] == 0, means[0:S], means[64:64 + S])
            reacted = chem[side * S:side * S + S, pl.ds(pl.multiple_of(pair * LANES, LANES), LANES)]
            out_ref[b] = reacted + mix * (picked - moved_ref[b])


def table_rows(table, at):
    return table.reshape(9 * ROWS, LANES)[pl.ds(at, 1), :]


def exchange(sums, moved, rates, mix, half, row):
    region = (3, ROWS, LANES)
    pair = pltpu.SemaphoreType.DMA((2, 3, CHUNKS))
    single = pltpu.SemaphoreType.DMA((2, CHUNKS))
    return pl.pallas_call(
        exchange_kernel,
        out_shape=jax.ShapeDtypeStruct((BLK, S, LANES), F32),
        in_specs=[VMEM, VMEM, VMEM, VMEM, VMEM, SMEM],
        out_specs=VMEM,
        scratch_shapes=[
            pltpu.VMEM(region, F32),
            pltpu.VMEM(region, F32),
            pltpu.VMEM(region, F32),
            pltpu.VMEM((ROWS, LANES), F32),
            pltpu.VMEM((ROWS, LANES), F32),
            pltpu.VMEM((3, 3, ROWS, LANES), F32),
            pltpu.VMEM((2 * S, BLK // 2 * LANES), F32),
            pltpu.VMEM((2 * S, 4 * S), BF16),
            pltpu.VMEM((2 * S, 2 * S), BF16),
            pltpu.VMEM((BLK * LANES, LANES), F32),
            pair, pair, single, single, single, single, pair, pair,
        ],
        compiler_params=pltpu.CompilerParams(collective_id=2, has_side_effects=True, vmem_limit_bytes=LIMIT),
        name="exchange",
    )(sums, moved, rates, mix, half, row)


def shards(species, reaction_rates, mix_rate, shift_list, arrival, cell_index):
    send, source, row, half = prepare(shift_list, arrival, cell_index)
    mix = jnp.broadcast_to(mix_rate[:, None], (S, LANES))
    state = species
    for step in range(STEPS):
        moved = migrate(send[step], source[step], state)
        sums = deposit(moved, half[step], row[step])
        state = exchange(sums, moved, reaction_rates, mix, half[step], row[step])
    return state


def solution(mesh):
    placed = (
        P(("lat", "lon"), None, None),
        P(),
        P(),
        P(None, "lat", None),
        P(None, ("lat", "lon")),
        P(None, ("lat", "lon"), None),
    )
    return jax.shard_map(
        shards, mesh=mesh, in_specs=placed, out_specs=P(("lat", "lon"), None, None), check_vma=False
    )
```

time: 805 us -> 151 us (0.19); the launches traced: 793 us -> 149 us
  matrix products: 383 us -> 0 us
  local copies, waits for them, and re-layouts: 158 us -> 5 us
  Pallas kernels: 0 us -> 143 us
  other arithmetic: 125 us -> 0.63 us
  waiting for transfers between devices: 62.4 us -> 0 us
  starting transfers between devices: 59.4 us -> 0 us
    dot_general x96 -> x0, matrix products: 383 us -> none  [the longest x16 176 us: select(): jnp.einsum('sc,bpc->bsp', means, onehot, precision=lax.Precision.HIGHEST)]
    pallas_call x0 -> x7, Pallas kernels: none -> 143 us  [the longest x2 92.7 us: exchange(): pl.pallas_call(exchange_kernel, out_shape=jax.ShapeDtypeStruct((BLK, S, L...]
    slice x17 -> x0, local copies, waits for them, and re-layouts: 125 us -> none  [the longest x2 121 us: shards(): total_sums = jnp.sum(rim_sums[0::2, 0::2], axis=(0, 1))]
    reduce_sum x21 -> x0, other arithmetic: 74.4 us -> none  [the longest x16 71 us: accumulate(): counts = counts + jnp.sum(onehot, axis=(0, 1))[None, :]]
    ppermute x32 -> x0, waiting for transfers between devices: 62.4 us -> none  [the longest x12 38.4 us: padded(): lax.ppermute(lax.slice_in_dim(block, block.shape[dim] - width, None, axis...]
    ppermute x32 -> x0, starting transfers between devices: 59.4 us -> none  [the longest x12 29.8 us: padded(): lax.ppermute(lax.slice_in_dim(block, 0, width, axis=dim), axis, backward)]
    sort x8 -> x0, other arithmetic: 13.1 us -> none  [shards(): jnp.argsort(jnp.where(moved_by == offset, 0, 1) * blocks + slot_ids)]
    concatenate x8 -> x0, other arithmetic: 13.1 us -> none  [the longest x6 13 us: padded(): block = jnp.concatenate([low, block, high], axis=dim)]
  transfers between devices with their start and end apart: 32 -> 0, of which waited for: 16 -> 0; matrix products, arithmetic and copies ran while one was open for 11% -> 0% of each run, Pallas kernels for 0% -> 0%
where the time goes in v1:
time: 151 us; the launch traced here: 149 us
  Pallas kernels  143 us (95%)
  local copies, waits for them, and re-layouts  5 us (3%)
    pallas_call x2, Pallas kernels, exchange(): pl.pallas_call(exchange_kernel, out_shape=jax.ShapeDtypeStruct((BLK, S, L...  92.7 us
    pallas_call x2, Pallas kernels, deposit(): pl.pallas_call(deposit_kernel, out_shape=jax.ShapeDtypeStruct((9 * ROWS,...  27.7 us
    pallas_call x2, Pallas kernels, migrate(): pl.pallas_call(migrate_kernel, out_shape=jax.ShapeDtypeStruct((BLK, S, LA...  19.2 us
    pallas_call x1, Pallas kernels, prepare(): pl.pallas_call(prepare_kernel, out_shape=(jax.ShapeDtypeStruct((STEPS, OU...  3.48 us

profile of v1, /device:TPU:5, one launch (start us, length us, event | category | flops | bytes accessed | tf_op | source)
XLA Modules:
  0.0 148.8 jit_solution(8423315916427485031)
XLA Ops:
  0.0 0.6 pad_add_fusion.place_ref
  0.6 0.7 broadcast_in_dim.2.mix_ref
  1.4 3.5 %prepare.1 = (s32[2,24]{1,0:T(2,128)}, s32[2,32]{1,0:T(2,128)}, s32[2,32,128]{2,1,0:T(8,128)}, s32[2,32,128]{2,1,0:T(8,128)}) custom-call(s32[2,1,32]{2,1,0:T(1,128)} %shift_ref.1, s32[2,32]{1,0:T(2,128)} %arrival_ref.1, s32[2]{0:T(128)} %pad_add_fusion.place_ref, s32[2,32,128]{2,1,0:T(8,128)} %cell_ref.1), custom_call_target="tpu_custom_call" | custom-call | tf_op jit(solution)/shard_map/prepare/pallas_call | solution.py:77
  4.8 0.7 slice_bitcast_fusion.5
  5.6 0.7 slice_bitcast_fusion.4
  6.3 0.8 slice_bitcast_fusion
  7.1 0.0 copy-start
  7.1 1.1 copy-done
  8.2 0.0 copy-start.1
  8.2 10.4 %migrate.2.moved_ref = f32[32,48,128]{2,1,0:T(8,128)S(1)} custom-call(s32[24]{0:T(128)S(1)} %get-tuple-element.19.send_ref, s32[32]{0:T(128)S(1)} %get-tuple-element.17.source_ref, f32[32,48,128]{2,1,0:T(8,128)S(1)} %copy-done), custom_call_target="tpu_custom_call" | custom-call | tf_op jit(solution)/shard_map/migrate/pallas_call | solution.py:138
  18.7 13.9 %deposit.2 = f32[4608,128]{1,0:T(8,128)S(1)} custom-call(f32[32,48,128]{2,1,0:T(8,128)S(1)} %migrate.2.moved_ref, s32[32,128]{1,0:T(8,128)S(1)} %get-tuple-element.21.half_ref, s32[32,128]{1,0:T(8,128)S(1)} %get-tuple-element.14.row_ref), custom_call_target="tpu_custom_call" | custom-call | tf_op jit(solution)/shard_map/deposit/pallas_call | solution.py:192
  32.6 0.0 copy-done.1
  32.6 49.4 %exchange.2.state_ref = f32[32,48,128]{2,1,0:T(8,128)S(1)} custom-call(f32[3,3,512,128]{3,2,1,0:T(8,128)S(1)} %bitcast.21, f32[32,48,128]{2,1,0:T(8,128)S(1)} %migrate.2.moved_ref, f32[48,48]{1,0:T(8,128)S(1)} %copy-done.1, f32[48,128]{1,0:T(8,128)S(1)} %broadcast_in_dim.2.mix_ref, s32[32,128]{1,0:T(8,128)S(1)} %get-tuple-element.21.half_ref, ...), custom_call_target="tpu_custom_call" | custom-call | tf_op jit(solution)/shard_map/exchange/pallas_call | solution.py:425
  81.9 8.8 %migrate.3.moved_ref = f32[32,48,128]{2,1,0:T(8,128)S(1)} custom-call(s32[24]{0:T(128)S(1)} %get-tuple-element.20.send_ref, s32[32]{0:T(128)S(1)} %get-tuple-element.18.source_ref, f32[32,48,128]{2,1,0:T(8,128)S(1)} %exchange.2.state_ref), custom_call_target="tpu_custom_call" | custom-call | tf_op jit(solution)/shard_map/migrate/pallas_call | solution.py:138
  90.7 13.9 %deposit.3 = f32[4608,128]{1,0:T(8,128)S(1)} custom-call(f32[32,48,128]{2,1,0:T(8,128)S(1)} %migrate.3.moved_ref, s32[32,128]{1,0:T(8,128)S(1)} %get-tuple-element.22.half_ref, s32[32,128]{1,0:T(8,128)S(1)} %get-tuple-element.13.row_ref), custom_call_target="tpu_custom_call" | custom-call | tf_op jit(solution)/shard_map/deposit/pallas_call | solution.py:192
  104.6 43.3 %exchange.3 = f32[32,48,128]{2,1,0:T(8,128)S(1)} custom-call(f32[3,3,512,128]{3,2,1,0:T(8,128)S(1)} %bitcast.20, f32[32,48,128]{2,1,0:T(8,128)S(1)} %migrate.3.moved_ref, f32[48,48]{1,0:T(8,128)S(1)} %copy-done.1, f32[48,128]{1,0:T(8,128)S(1)} %broadcast_in_dim.2.mix_ref, s32[32,128]{1,0:T(8,128)S(1)} %get-tuple-element.22.half_ref, ...), custom_call_target="tpu_custom_call" | custom-call | tf_op jit(solution)/shard_map/exchange/pallas_call | solution.py:425
  147.9 0.9 copy.8
Async XLA Ops:
  7.1 1.1 copy-start
  8.2 24.3 %copy-start.1 = (f32[48,48]{1,0:T(8,128)S(1)}, f32[48,48]{1,0:T(8,128)}, u32[]{:S(2)}) copy-start(f32[48,48]{1,0:T(8,128)} %rates_ref.3) | copy-start | bytes 27652

commit v2 on v1

v2 whole, which is shorter than its diff:
```python
import functools

import jax
import jax.numpy as jnp
from jax import lax
from jax.experimental import pallas as pl
from jax.experimental.pallas import tpu as pltpu
from jax.sharding import PartitionSpec as P

S = 48
LANES = 128
BLK = 32
CELL_DEV = 1024
ROWS = CELL_DEV // 2
STEPS = 2
SUB = 32
ACCS = 4
CHUNKS = 4
CHUNK = ROWS // CHUNKS
F32 = jnp.float32
BF16 = jnp.bfloat16
MESH = pl.DeviceIdType.MESH
VMEM = pl.BlockSpec(memory_space=pltpu.VMEM)
SMEM = pl.BlockSpec(memory_space=pltpu.SMEM)
LIMIT = 48 * 2**20
BATCHES = (2, -2, 1, 1, -1, -1)
FIRST = {2: 0, -2: 1, 1: 2, -1: 4}
LAST_FIRST = (3, 0, 1, 2)
PLAN = (6, ("a", 3), 2, ("a", 0), 2, ("a", 1), 2, ("b", 3), ("a", 2), 3, ("b", 0), 2, ("b", 1), 2, ("b", 2), 3, ("c", 0), 3, ("c", 1), 3, ("c", 2), 4)


def around(axis, step):
    count = lax.axis_size(axis)
    return lax.rem(lax.axis_index(axis) + step + count, count)


def is_polar():
    band = lax.axis_index("lat")
    return (band == 0) | (band == lax.axis_size("lat") - 1)


def place_slots(shift_ref, step, unit, visit):
    def place(slot, counts):
        moved_by = shift_ref[step, 0, slot]
        where = 6 * unit + counts[4]
        later = []
        for offset, count in zip((2, -2, 1, -1), counts):
            hit = moved_by == offset
            where = jnp.where(hit, FIRST[offset] * unit + count, where)
            later.append(count + hit.astype(jnp.int32))
        later.append(counts[4] + (moved_by == 0).astype(jnp.int32))
        visit(slot, moved_by, jnp.minimum(where, BLK - 1))
        return tuple(later)

    lax.fori_loop(0, BLK, place, (jnp.int32(0),) * 5)


def batch_copy(pool, send_sem, recv_sem, k, unit):
    return pltpu.make_async_remote_copy(
        src_ref=pool.at[pl.ds(k * unit, unit)],
        dst_ref=pool.at[pl.ds(BLK + k * unit, unit)],
        send_sem=send_sem.at[k],
        recv_sem=recv_sem.at[k],
        device_id={"lon": around("lon", BATCHES[k])},
        device_id_type=MESH,
    )


def each_unit(polar, body):
    @pl.when(polar)
    def _():
        body(4)

    @pl.when(jnp.logical_not(polar))
    def _():
        body(2)


def migrate_kernel(shift_ref, arrival_ref, state_ref, cell_ref, moved_ref, row_ref, pool, pool_at, send_sem, recv_sem):
    polar = is_polar()
    unit = jnp.where(polar, 4, 2)
    barrier = pltpu.get_barrier_semaphore()
    for offset in (1, -1, 2, -2):
        pl.semaphore_signal(barrier, inc=1, device_id={"lon": around("lon", offset)}, device_id_type=MESH)

    def note(slot, moved_by, where):
        pool_at[slot] = where + jnp.where(moved_by == 0, 0, BLK)

    place_slots(shift_ref, 0, unit, note)

    @pl.loop(0, 6 * unit)
    def _(where):
        def seek(slot, found):
            return jnp.where(pool_at[slot] == where + BLK, slot, found)

        pool[where] = state_ref[lax.fori_loop(0, BLK, seek, jnp.int32(0), unroll=True)]

    pl.semaphore_wait(barrier, 4)

    def start(unit):
        for k in range(6):
            batch_copy(pool, send_sem, recv_sem, k, unit).start()

    each_unit(polar, start)
    sectors = lax.axis_size("lon")
    cell = cell_ref[...]
    owner = cell // CELL_DEV
    rel_band = owner // sectors - lax.axis_index("lat") + 1
    rel_sector = (owner % sectors - lax.axis_index("lon") + 1 + sectors) % sectors
    row_ref[...] = jnp.clip((rel_band * 3 + rel_sector) * ROWS + cell % ROWS, 0, 9 * ROWS - 1)

    def wait(unit):
        for k in range(6):
            batch_copy(pool, send_sem, recv_sem, k, unit).wait()

    each_unit(polar, wait)

    @pl.loop(0, BLK, unroll=4)
    def _(slot):
        old = arrival_ref[0, slot]
        at = pool_at[old]
        moved_ref[slot] = jnp.where(at < BLK, state_ref[old], pool[at])


def migrate(shift_list, arrival, state, cell_index):
    return pl.pallas_call(
        migrate_kernel,
        out_shape=(jax.ShapeDtypeStruct((BLK, S, LANES), F32), jax.ShapeDtypeStruct((STEPS, BLK, LANES), jnp.int32)),
        in_specs=[SMEM, SMEM, VMEM, VMEM],
        out_specs=(VMEM, VMEM),
        scratch_shapes=[
            pltpu.VMEM((2 * BLK, S, LANES), F32),
            pltpu.SMEM((BLK,), jnp.int32),
            pltpu.SemaphoreType.DMA((6,)),
            pltpu.SemaphoreType.DMA((6,)),
        ],
        compiler_params=pltpu.CompilerParams(collective_id=1, has_side_effects=True, vmem_limit_bytes=LIMIT),
        name="migrate",
    )(shift_list, arrival, state, cell_index)


def deposit_kernel(step, moved_ref, cell_ref, row_ref, shift_ref, arrival_ref, sums_ref, order_ref, source_ref, even, odd, pool_at, *accs):
    blank = jnp.zeros((8, LANES), F32)
    tail = jnp.where(lax.broadcasted_iota(jnp.int32, (16, LANES), 0) == 0, 1.0, 0.0)

    @pl.loop(0, 9 * ROWS // 8, unroll=8)
    def _(i):
        part = pl.ds(pl.multiple_of(i * 8, 8), 8)
        for acc in accs:
            acc[part, :] = blank

    def turn(b, rows):
        block = jnp.concatenate([moved_ref[b], tail], 0)
        low = (cell_ref[step, pl.ds(b, 1), :] & ROWS) == 0
        rows[...] = jnp.concatenate([jnp.where(low, block, 0.0), jnp.where(low, 0.0, block)], 0).T

    def add(b, rows):
        for k in range(LANES):
            acc = accs[k % ACCS]
            at = pl.ds(row_ref[step, b, k], 1)
            acc[at, :] = acc[at, :] + rows[k:k + 1, :]

    turn(0, even)

    @pl.loop(0, BLK // 2)
    def _(i):
        turn(2 * i + 1, odd)
        add(2 * i, even)
        turn(jnp.minimum(2 * i + 2, BLK - 1), even)
        add(2 * i + 1, odd)

    @pl.loop(0, 9 * ROWS // 8, unroll=4)
    def _(i):
        part = pl.ds(pl.multiple_of(i * 8, 8), 8)
        total = accs[0][part, :]
        for acc in accs[1:]:
            total = total + acc[part, :]
        sums_ref[part, :] = total

    def note(slot, moved_by, where):
        order_ref[where] = slot
        pool_at[slot] = where + jnp.where(moved_by == 0, 0, BLK)

    place_slots(shift_ref, STEPS - 1, jnp.where(is_polar(), 4, 2), note)

    @pl.loop(0, BLK)
    def _(slot):
        source_ref[slot] = pool_at[arrival_ref[STEPS - 1, slot]]


def deposit(step, moved, cell_index, row, shift_list, arrival):
    sums, order, source = pl.pallas_call(
        functools.partial(deposit_kernel, step),
        out_shape=(
            jax.ShapeDtypeStruct((9 * ROWS, LANES), F32),
            jax.ShapeDtypeStruct((BLK,), jnp.int32),
            jax.ShapeDtypeStruct((BLK,), jnp.int32),
        ),
        in_specs=[VMEM, VMEM, SMEM, SMEM, SMEM],
        out_specs=(VMEM, SMEM, SMEM),
        scratch_shapes=[pltpu.VMEM((LANES, LANES), F32)] * 2
        + [pltpu.SMEM((BLK,), jnp.int32)]
        + [pltpu.VMEM((9 * ROWS, LANES), F32)] * ACCS,
        compiler_params=pltpu.CompilerParams(vmem_limit_bytes=LIMIT),
        name="deposit",
    )(moved, cell_index, row, shift_list, arrival)
    return sums.reshape(3, 3, ROWS, LANES), order, source


def split(x):
    high = x.astype(BF16)
    return high, (x - high.astype(F32)).astype(BF16)


def pairs_of(rates):
    zero = jnp.zeros((S, S), F32)
    high, low = split(jnp.concatenate([jnp.concatenate([rates, zero], 1), jnp.concatenate([zero, rates], 1)], 0))
    return jnp.concatenate([high, high], 1), low


def exchange_kernel(
    step, sums_ref, moved_ref, rates_ref, mix_ref, cell_ref, row_ref, order_ref, source_ref, out_ref,
    below, above, middle, left, right, table, chem, high2, low1, even, odd, reacted, pool,
    up_sem, down_sem, west_sem, east_sem, mwest_sem, meast_sem, mup_sem, mdown_sem, send_sem, recv_sem,
):
    last = step == STEPS - 1
    band = lax.axis_index("lat")
    bands = lax.axis_size("lat")
    has_up = band < bands - 1
    has_down = band > 0
    up = jnp.minimum(band + 1, bands - 1)
    down = jnp.maximum(band - 1, 0)
    east = around("lon", 1)
    west = around("lon", -1)
    beside = (1, -1) if last else (1, -1, 2, -2)
    barrier = pltpu.get_barrier_semaphore()
    for offset in beside:
        pl.semaphore_signal(barrier, inc=1, device_id={"lon": around("lon", offset)}, device_id_type=MESH)

    @pl.when(has_up)
    def _():
        pl.semaphore_signal(barrier, inc=1, device_id={"lat": up}, device_id_type=MESH)

    @pl.when(has_down)
    def _():
        pl.semaphore_signal(barrier, inc=1, device_id={"lat": down}, device_id_type=MESH)

    pl.semaphore_wait(barrier, len(beside) + has_up.astype(jnp.int32) + has_down.astype(jnp.int32))

    def remote(src, dst, sem, index, device):
        return pltpu.make_async_remote_copy(
            src_ref=src, dst_ref=dst, send_sem=sem.at[(0,) + index], recv_sem=sem.at[(1,) + index],
            device_id=device, device_id_type=MESH,
        )

    def chunk(c):
        return pl.ds(c * CHUNK, CHUNK)

    def sums_up(s, c):
        return remote(sums_ref.at[2, s, chunk(c)], below.at[s, chunk(c)], up_sem, (s, c), {"lat": up})

    def sums_down(s, c):
        return remote(sums_ref.at[0, s, chunk(c)], above.at[s, chunk(c)], down_sem, (s, c), {"lat": down})

    def sums_west(c):
        return remote(middle.at[0, chunk(c)], right.at[chunk(c)], west_sem, (c,), {"lon": west})

    def sums_east(c):
        return remote(middle.at[2, chunk(c)], left.at[chunk(c)], east_sem, (c,), {"lon": east})

    def means_west(c):
        return remote(table.at[1, 1, chunk(c)], table.at[1, 2, chunk(c)], mwest_sem, (c,), {"lon": west})

    def means_east(c):
        return remote(table.at[1, 1, chunk(c)], table.at[1, 0, chunk(c)], meast_sem, (c,), {"lon": east})

    def means_up(s, c):
        return remote(table.at[1, s, chunk(c)], table.at[0, s, chunk(c)], mup_sem, (s, c), {"lat": up})

    def means_down(s, c):
        return remote(table.at[1, s, chunk(c)], table.at[2, s, chunk(c)], mdown_sem, (s, c), {"lat": down})

    order = [(s, c) for c in LAST_FIRST for s in (0, 2, 1)]

    @pl.when(has_up)
    def _():
        for s, c in order:
            sums_up(s, c).start()

    @pl.when(has_down)
    def _():
        for s, c in order:
            sums_down(s, c).start()

    @pl.when(jnp.logical_not(has_down))
    def _():
        below[...] = jnp.zeros_like(below)
        table[0] = jnp.zeros_like(table[0])

    @pl.when(jnp.logical_not(has_up))
    def _():
        above[...] = jnp.zeros_like(above)
        table[2] = jnp.zeros_like(table[2])

    high, low = pairs_of(rates_ref[...])
    high2[...] = high
    low1[...] = low
    half_blk = BLK // 2
    for b in range(BLK):
        column = b % half_blk * LANES
        chem[b // half_blk, :, column:column + LANES] = moved_ref[b]

    def chemistry(substeps):
        def advance(_, current):
            state = chem[...].reshape(2 * S, half_blk * LANES)
            high, low = split(state)
            pushed = jnp.dot(high2[...], jnp.concatenate([high, low], 0), preferred_element_type=F32)
            pushed = pushed + jnp.dot(low1[...], high, preferred_element_type=F32)
            chem[...] = (state + (2.0 / SUB) * jnp.tanh(pushed)).reshape(2, S, half_blk * LANES)
            return current

        lax.fori_loop(0, substeps, advance, 0)

    def strips(body):
        @pl.loop(0, CHUNK // 8, unroll=4)
        def _(i):
            body(pl.multiple_of(i * 8, 8))

    lane = lax.broadcasted_iota(jnp.int32, (8, LANES), 1)
    spare = lane % 64 >= S

    def bands_summed(c):
        for s in (0, 2, 1):
            @pl.when(has_down)
            def _():
                sums_up(s, c).wait_recv()

            @pl.when(has_up)
            def _():
                sums_down(s, c).wait_recv()

            def add_bands(i):
                part = pl.ds(c * CHUNK + i, 8)
                middle[s, part, :] = sums_ref[1, s, part, :] + below[s, part, :] + above[s, part, :]

            strips(add_bands)
            if s == 0:
                sums_west(c).start()
            if s == 2:
                sums_east(c).start()

    def sectors_summed(c):
        sums_west(c).wait_recv()
        sums_east(c).wait_recv()

        def mean(i):
            part = pl.ds(c * CHUNK + i, 8)
            total = middle[1, part, :] + left[part, :] + right[part, :]
            count = jnp.where(lane < 64, total[:, S:S + 1], total[:, 64 + S:64 + S + 1])
            means = total / jnp.maximum(count, 1.0)
            if c < CHUNKS - 1:
                others = table[1, 1, pl.ds((CHUNKS - 1) * CHUNK + i, 8), :]
                means = jnp.where(spare, pltpu.roll(others, S - 16 * c, 1), means)
            table[1, 1, part, :] = means

        strips(mean)
        if c < CHUNKS - 1:
            means_west(c).start()
            means_east(c).start()

            @pl.when(has_up)
            def _():
                means_up(1, c).start()

            @pl.when(has_down)
            def _():
                means_down(1, c).start()

    def means_passed(c):
        means_west(c).wait_recv()
        means_east(c).wait_recv()

        @pl.when(has_up)
        def _():
            means_up(0, c).start()
            means_up(2, c).start()

        @pl.when(has_down)
        def _():
            means_down(0, c).start()
            means_down(2, c).start()

    parts = {"a": bands_summed, "b": sectors_summed, "c": means_passed}
    for entry in PLAN:
        if isinstance(entry, int):
            chemistry(entry)
        else:
            parts[entry[0]](entry[1])

    for b in range(BLK):
        column = b % half_blk * LANES
        reacted[b] = chem[b // half_blk, :, column:column + LANES]

    for s, c in order:
        @pl.when(has_up)
        def _():
            sums_up(s, c).wait_send()
            if c < CHUNKS - 1:
                means_up(s, c).wait_send()
                means_down(s, c).wait_recv()

        @pl.when(has_down)
        def _():
            sums_down(s, c).wait_send()
            if c < CHUNKS - 1:
                means_down(s, c).wait_send()
                means_up(s, c).wait_recv()
    for c in range(CHUNKS):
        sums_west(c).wait_send()
        sums_east(c).wait_send()
        if c < CHUNKS - 1:
            means_west(c).wait_send()
            means_east(c).wait_send()

    for r in range(3):
        for s in range(3):
            if (r, s) != (1, 1):
                def unpack(i):
                    found = [pltpu.roll(table[r, s, pl.ds(q * CHUNK + i, 8), :], LANES - S + 16 * q, 1) for q in range(3)]
                    spot = lane % 64
                    table[r, s, pl.ds(3 * CHUNK + i, 8), :] = jnp.where(spot < 16, found[0], jnp.where(spot < 32, found[1], found[2]))

                strips(unpack)

    mix = jnp.broadcast_to(mix_ref[...], (LANES, S)).T
    flat = table.reshape(9 * ROWS, LANES)

    def gather(b, rows):
        for k in range(LANES):
            rows[k:k + 1, :] = flat[pl.ds(row_ref[step, b, k], 1), :]

    def mixed(b, rows):
        means = rows[...].T
        low = (cell_ref[step, pl.ds(b, 1), :] & ROWS) == 0
        picked = jnp.where(low, means[0:S], means[64:64 + S])
        return reacted[b] + mix * (picked - moved_ref[b])

    def pair(order_of, target, i):
        first, second = order_of(2 * i), order_of(2 * i + 1)
        gather(first, even)
        gather(second, odd)
        target[2 * i] = mixed(first, even)
        target[2 * i + 1] = mixed(second, odd)

    if last:
        @pl.loop(0, BLK // 2)
        def _(i):
            pair(lambda b: b, out_ref, i)
    else:
        polar = is_polar()
        half_unit = jnp.where(polar, 2, 1)

        @pl.loop(0, 6)
        def _(k):
            @pl.loop(0, half_unit)
            def _(u):
                pair(lambda at: order_ref[at], pool, k * half_unit + u)

            for batch in range(6):
                @pl.when(k == batch)
                def _():
                    each_unit(polar, lambda unit: batch_copy(pool, send_sem, recv_sem, batch, unit).start())

        @pl.loop(6 * half_unit, BLK // 2)
        def _(i):
            pair(lambda at: order_ref[at], pool, i)

        def wait(unit):
            for k in range(6):
                batch_copy(pool, send_sem, recv_sem, k, unit).wait()

        each_unit(polar, wait)

        @pl.loop(0, BLK, unroll=4)
        def _(slot):
            out_ref[slot] = pool[source_ref[slot]]


def exchange(step, sums, moved, rates, mix, cell_index, row, order, source):
    region = (3, ROWS, LANES)
    pair = pltpu.SemaphoreType.DMA((2, 3, CHUNKS))
    single = pltpu.SemaphoreType.DMA((2, CHUNKS))
    return pl.pallas_call(
        functools.partial(exchange_kernel, step),
        out_shape=jax.ShapeDtypeStruct((BLK, S, LANES), F32),
        in_specs=[VMEM, VMEM, VMEM, VMEM, VMEM, SMEM, SMEM, SMEM],
        out_specs=VMEM,
        scratch_shapes=[
            pltpu.VMEM(region, F32),
            pltpu.VMEM(region, F32),
            pltpu.VMEM(region, F32),
            pltpu.VMEM((ROWS, LANES), F32),
            pltpu.VMEM((ROWS, LANES), F32),
            pltpu.VMEM((3, 3, ROWS, LANES), F32),
            pltpu.VMEM((2, S, BLK // 2 * LANES), F32),
            pltpu.VMEM((2 * S, 4 * S), BF16),
            pltpu.VMEM((2 * S, 2 * S), BF16),
            pltpu.VMEM((LANES, LANES), F32),
            pltpu.VMEM((LANES, LANES), F32),
            pltpu.VMEM((BLK, S, LANES), F32),
            pltpu.VMEM((2 * BLK, S, LANES), F32),
            pair, pair, single, single, single, single, pair, pair,
            pltpu.SemaphoreType.DMA((6,)),
            pltpu.SemaphoreType.DMA((6,)),
        ],
        compiler_params=pltpu.CompilerParams(collective_id=2 + step, has_side_effects=True, vmem_limit_bytes=LIMIT),
        name="exchange",
    )(sums, moved, rates, mix, cell_index, row, order, source)


def shards(species, reaction_rates, mix_rate, shift_list, arrival, cell_index):
    moved, row = migrate(shift_list, arrival, species, cell_index)
    mix = mix_rate.reshape(1, S)
    for step in range(STEPS):
        sums, order, source = deposit(step, moved, cell_index, row, shift_list, arrival)
        moved = exchange(step, sums, moved, reaction_rates, mix, cell_index, row, order, source)
    return moved


def solution(mesh):
    placed = (
        P(("lat", "lon"), None, None),
        P(),
        P(),
        P(None, "lat", None),
        P(None, ("lat", "lon")),
        P(None, ("lat", "lon"), None),
    )
    return jax.shard_map(
        shards, mesh=mesh, in_specs=placed, out_specs=P(("lat", "lon"), None, None), check_vma=False
    )
```

time: 151 us -> 118 us (0.78)
  Pallas kernels: 143 us -> 109 us
    pallas_call x7 -> x5, Pallas kernels: 143 us -> 109 us  [the longest x2 77.7 us: exchange(): pl.pallas_call(functools.partial(exchange_kernel, step), out_shape=jax.Sh...]
    unnamed x5 -> x25, local copies, waits for them, and re-layouts: 2.02 us -> 6.3 us
    squeeze x3 -> x0, local copies, waits for them, and re-layouts: 2.26 us -> none  [the longest x2 1.48 us: shards(): moved = migrate(send[step], source[step], state)]
where the time goes in v2:
time: 118 us; the launch traced here: 116 us
  Pallas kernels  109 us (92%)
  local copies, waits for them, and re-layouts  6.3 us (5%)
    pallas_call x2, Pallas kernels, exchange(): pl.pallas_call(functools.partial(exchange_kernel, step), out_shape=jax.Sh...  77.7 us
    pallas_call x2, Pallas kernels, deposit(): pl.pallas_call(functools.partial(deposit_kernel, step), out_shape=(jax.Sh...  20 us
    pallas_call x1, Pallas kernels, migrate(): pl.pallas_call(migrate_kernel, out_shape=(jax.ShapeDtypeStruct((BLK, S, L...  11.8 us
    unnamed x25, local copies, waits for them, and re-layouts  6.3 us

profile of v2, /device:TPU:5, one launch (start us, length us, event | category | flops | bytes accessed | tf_op | source)
XLA Modules:
  0.0 115.9 jit_solution(4199862393490250831)
XLA Ops:
  0.0 0.0 copy-start
  0.0 0.8 copy-done
  0.8 0.0 copy-start.3
  0.8 1.1 copy-done.3
  1.9 0.0 copy-start.6
  1.9 0.7 copy-done.6
  2.6 0.0 copy-start.8
  2.6 0.7 copy-done.8
  3.3 11.8 %migrate.1 = (f32[32,48,128]{2,1,0:T(8,128)S(1)}, s32[2,32,128]{2,1,0:T(8,128)S(1)}) custom-call(s32[2,1,32]{2,1,0:T(1,128)S(1)} %copy-done.6, s32[2,32]{1,0:T(2,128)S(1)} %copy-done.8, f32[32,48,128]{2,1,0:T(8,128)S(1)} %copy-done.3, s32[2,32,128]{2,1,0:T(8,128)S(1)} %copy-done), custom_call_target="tpu_custom_call" | custom-call | tf_op jit(solution)/shard_map/migrate/pallas_call | solution.py:126
  15.0 0.0 copy-start.2
  15.0 0.0 copy-start.7
  15.1 0.0 copy-start.9
  15.1 10.0 %deposit.2 = (f32[4608,128]{1,0:T(8,128)S(1)}, s32[32]{0:T(128)S(1)}, s32[32]{0:T(128)S(1)}) custom-call(f32[32,48,128]{2,1,0:T(8,128)S(1)} %get-tuple-element.13.moved_ref, s32[2,32,128]{2,1,0:T(8,128)S(1)} %copy-done, s32[2,32,128]{2,1,0:T(8,128)S(1)} %get-tuple-element.14.row_ref, s32[2,1,32]{2,1,0:T(1,128)S(1)} %copy-done.6, s32[2,32]{1,0:T(2,128)S(1)} %copy-done.8), custom_call_target="tpu_custom_call" | custom-call | tf_op jit(solution)/shard_map/deposit/pallas_call | solution.py:192
  25.1 0.0 copy-start.1
  25.1 0.7 copy-done.1
  25.8 0.0 copy-start.4
  25.8 0.7 copy-done.4
  26.6 0.0 copy-start.10
  26.6 0.7 copy-done.10
  27.2 0.0 copy-start.5
  27.2 0.0 copy-start.11
  27.2 41.3 %exchange.2.moved_ref = f32[32,48,128]{2,1,0:T(8,128)S(1)} custom-call(f32[3,3,512,128]{3,2,1,0:T(8,128)S(1)} %bitcast.4, f32[32,48,128]{2,1,0:T(8,128)S(1)} %get-tuple-element.13.moved_ref, f32[48,48]{1,0:T(8,128)S(1)} %copy-done.4, f32[1,48]{1,0:T(1,128)S(1)} %bitcast.5, s32[2,32,128]{2,1,0:T(8,128)S(1)} %copy-done.1, ...), custom_call_target="tpu_custom_call" | custom-call | tf_op jit(solution)/shard_map/exchange/pallas_call | solution.py:493
  68.5 0.0 copy-done.2
  68.5 0.0 copy-done.7
  68.5 0.0 copy-done.9
  68.5 10.0 %deposit.3 = (f32[4608,128]{1,0:T(8,128)S(1)}, s32[32]{0:T(128)S(1)}, s32[32]{0:T(128)S(1)}) custom-call(f32[32,48,128]{2,1,0:T(8,128)S(1)} %exchange.2.moved_ref, s32[2,32,128]{2,1,0:T(8,128)S(1)} %copy-done.2, s32[2,32,128]{2,1,0:T(8,128)S(1)} %get-tuple-element.14.row_ref, s32[2,1,32]{2,1,0:T(1,128)S(1)} %copy-done.7, s32[2,32]{1,0:T(2,128)S(1)} %copy-done.9), custom_call_target="tpu_custom_call" | custom-call | tf_op jit(solution)/shard_map/deposit/pallas_call | solution.py:192
  78.6 0.0 copy-done.5
  78.6 0.0 copy-done.11
  78.6 36.4 %exchange.3 = f32[32,48,128]{2,1,0:T(8,128)S(1)} custom-call(f32[3,3,512,128]{3,2,1,0:T(8,128)S(1)} %bitcast.3, f32[32,48,128]{2,1,0:T(8,128)S(1)} %exchange.2.moved_ref, f32[48,48]{1,0:T(8,128)S(1)} %copy-done.5, f32[1,48]{1,0:T(1,128)S(1)} %bitcast.6, s32[2,32,128]{2,1,0:T(8,128)S(1)} %copy-done.2, s32[2,32,128]{2,1,0:T(8,128)S(1)} %get-tuple-element.14.row_ref, ...), custom_call_target="tpu_custom_call" | custom-call | tf_op jit(solution)/shard_map/exchange/pallas_call | solution.py:493
  115.0 0.9 copy.8
Async XLA Ops:
  0.0 0.8 copy-start
  0.8 1.1 copy-start.3
  1.9 0.7 copy-start.6
  2.6 0.7 copy-start.8
  15.0 53.5 %copy-start.2 = (s32[2,32,128]{2,1,0:T(8,128)S(1)}, s32[2,32,128]{2,1,0:T(8,128)}, u32[]{:S(2)}) copy-start(s32[2,32,128]{2,1,0:T(8,128)} %cell_ref.9) | copy-start | bytes 98308
  15.0 53.5 %copy-start.7 = (s32[2,1,32]{2,1,0:T(1,128)S(1)}, s32[2,1,32]{2,1,0:T(1,128)}, u32[]{:S(2)}) copy-start(s32[2,1,32]{2,1,0:T(1,128)} %shift_ref.5) | copy-start | bytes 772
  15.1 53.5 %copy-start.9 = (s32[2,32]{1,0:T(2,128)S(1)}, s32[2,32]{1,0:T(2,128)}, u32[]{:S(2)}) copy-start(s32[2,32]{1,0:T(2,128)} %arrival_ref.5) | copy-start | bytes 772
  25.1 0.8 copy-start.1
  25.8 0.7 copy-start.4
  26.6 0.7 copy-start.10
  27.2 51.3 %copy-start.5 = (f32[48,48]{1,0:T(8,128)S(1)}, f32[48,48]{1,0:T(8,128)}, u32[]{:S(2)}) copy-start(f32[48,48]{1,0:T(8,128)} %rates_ref.3) | copy-start | bytes 27652
  27.2 51.3 %copy-start.11 = (f32[48]{0:T(128)S(1)}, f32[48]{0:T(128)}, u32[]{:S(2)}) copy-start(f32[48]{0:T(128)} %param.8) | copy-start | bytes 580

commit v3 on v2

--- a/solution.py
+++ b/solution.py
@@ -14,7 +14,7 @@
 ROWS = CELL_DEV // 2
 STEPS = 2
 SUB = 32
-ACCS = 4
+ACCS = 6
 CHUNKS = 4
 CHUNK = ROWS // CHUNKS
 F32 = jnp.float32
@@ -22,7 +22,9 @@
 MESH = pl.DeviceIdType.MESH
 VMEM = pl.BlockSpec(memory_space=pltpu.VMEM)
 SMEM = pl.BlockSpec(memory_space=pltpu.SMEM)
-LIMIT = 48 * 2**20
+HBM = pl.BlockSpec(memory_space=pltpu.HBM)
+TABLE = jax.ShapeDtypeStruct((9 * ROWS, LANES), F32)
+LIMIT = 24 * 2**20
 BATCHES = (2, -2, 1, 1, -1, -1)
 FIRST = {2: 0, -2: 1, 1: 2, -1: 4}
 LAST_FIRST = (3, 0, 1, 2)
@@ -76,7 +78,27 @@
         body(2)
 
 
-def migrate_kernel(shift_ref, arrival_ref, state_ref, cell_ref, moved_ref, row_ref, pool, pool_at, send_sem, recv_sem):
+def blank_strips(refs):
+    blank = jnp.zeros((8, LANES), F32)
+
+    @pl.loop(0, 9 * ROWS // 8, unroll=4)
+    def _(i):
+        part = pl.ds(pl.multiple_of(i * 8, 8), 8)
+        for ref in refs:
+            ref[part, :] = blank
+
+
+def migrate_kernel(shift_hbm, arrival_hbm, state_hbm, cell_hbm, moved_ref, row_ref, low_ref, place_ref, source_ref, *rest):
+    accs = rest[:ACCS]
+    shift_ref, arrival_ref, state_ref, cell_ref, pool, pool_at, load_sem, send_sem, recv_sem = rest[ACCS:]
+    loads = [
+        pltpu.make_async_copy(src, dst, load_sem.at[k])
+        for k, (src, dst) in enumerate(
+            ((shift_hbm, shift_ref), (arrival_hbm, arrival_ref), (state_hbm, state_ref), (cell_hbm, cell_ref))
+        )
+    ]
+    for load in loads:
+        load.start()
     polar = is_polar()
     unit = jnp.where(polar, 4, 2)
     barrier = pltpu.get_barrier_semaphore()
@@ -86,7 +108,13 @@
     def note(slot, moved_by, where):
         pool_at[slot] = where + jnp.where(moved_by == 0, 0, BLK)
 
+    def note_later(slot, moved_by, where):
+        place_ref[slot] = where + jnp.where(moved_by == 0, 0, BLK)
+
+    loads[0].wait()
     place_slots(shift_ref, 0, unit, note)
+    loads[1].wait()
+    loads[2].wait()
 
     @pl.loop(0, 6 * unit)
     def _(where):
@@ -102,12 +130,21 @@
             batch_copy(pool, send_sem, recv_sem, k, unit).start()
 
     each_unit(polar, start)
+    loads[3].wait()
     sectors = lax.axis_size("lon")
     cell = cell_ref[...]
     owner = cell // CELL_DEV
     rel_band = owner // sectors - lax.axis_index("lat") + 1
     rel_sector = (owner % sectors - lax.axis_index("lon") + 1 + sectors) % sectors
     row_ref[...] = jnp.clip((rel_band * 3 + rel_sector) * ROWS + cell % ROWS, 0, 9 * ROWS - 1)
+    low_ref[...] = 1 - cell // ROWS % 2
+    place_slots(shift_ref, STEPS - 1, unit, note_later)
+
+    @pl.loop(0, BLK)
+    def _(slot):
+        source_ref[slot] = place_ref[arrival_ref[STEPS - 1, slot]]
+
+    blank_strips(accs)
 
     def wait(unit):
         for k in range(6):
@@ -123,14 +160,21 @@
 
 
 def migrate(shift_list, arrival, state, cell_index):
+    whole = jax.ShapeDtypeStruct((STEPS, BLK, LANES), jnp.int32)
+    slots = jax.ShapeDtypeStruct((BLK,), jnp.int32)
     return pl.pallas_call(
         migrate_kernel,
-        out_shape=(jax.ShapeDtypeStruct((BLK, S, LANES), F32), jax.ShapeDtypeStruct((STEPS, BLK, LANES), jnp.int32)),
-        in_specs=[SMEM, SMEM, VMEM, VMEM],
-        out_specs=(VMEM, VMEM),
+        out_shape=(jax.ShapeDtypeStruct((BLK, S, LANES), F32), whole, whole, slots, slots) + (TABLE,) * ACCS,
+        in_specs=[HBM] * 4,
+        out_specs=(VMEM, VMEM, VMEM, SMEM, SMEM) + (VMEM,) * ACCS,
         scratch_shapes=[
+            pltpu.SMEM((STEPS, 1, BLK), jnp.int32),
+            pltpu.SMEM((STEPS, BLK), jnp.int32),
+            pltpu.VMEM((BLK, S, LANES), F32),
+            pltpu.VMEM((STEPS, BLK, LANES), jnp.int32),
             pltpu.VMEM((2 * BLK, S, LANES), F32),
             pltpu.SMEM((BLK,), jnp.int32),
+            pltpu.SemaphoreType.DMA((4,)),
             pltpu.SemaphoreType.DMA((6,)),
             pltpu.SemaphoreType.DMA((6,)),
         ],
@@ -139,19 +183,14 @@
     )(shift_list, arrival, state, cell_index)
 
 
-def deposit_kernel(step, moved_ref, cell_ref, row_ref, shift_ref, arrival_ref, sums_ref, order_ref, source_ref, even, odd, pool_at, *accs):
-    blank = jnp.zeros((8, LANES), F32)
+def deposit_kernel(step, moved_ref, low_ref, row_ref, place_ref, *rest):
+    accs = rest[ACCS:2 * ACCS]
+    order_ref, even, odd = rest[2 * ACCS:]
     tail = jnp.where(lax.broadcasted_iota(jnp.int32, (16, LANES), 0) == 0, 1.0, 0.0)
-
-    @pl.loop(0, 9 * ROWS // 8, unroll=8)
-    def _(i):
-        part = pl.ds(pl.multiple_of(i * 8, 8), 8)
-        for acc in accs:
-            acc[part, :] = blank
 
     def turn(b, rows):
         block = jnp.concatenate([moved_ref[b], tail], 0)
-        low = (cell_ref[step, pl.ds(b, 1), :] & ROWS) == 0
+        low = low_ref[step, pl.ds(b, 1), :] == 1
         rows[...] = jnp.concatenate([jnp.where(low, block, 0.0), jnp.where(low, 0.0, block)], 0).T
 
     def add(b, rows):
@@ -169,42 +208,23 @@
         turn(jnp.minimum(2 * i + 2, BLK - 1), even)
         add(2 * i + 1, odd)
 
-    @pl.loop(0, 9 * ROWS // 8, unroll=4)
-    def _(i):
-        part = pl.ds(pl.multiple_of(i * 8, 8), 8)
-        total = accs[0][part, :]
-        for acc in accs[1:]:
-            total = total + acc[part, :]
-        sums_ref[part, :] = total
-
-    def note(slot, moved_by, where):
-        order_ref[where] = slot
-        pool_at[slot] = where + jnp.where(moved_by == 0, 0, BLK)
-
-    place_slots(shift_ref, STEPS - 1, jnp.where(is_polar(), 4, 2), note)
-
     @pl.loop(0, BLK)
     def _(slot):
-        source_ref[slot] = pool_at[arrival_ref[STEPS - 1, slot]]
-
-
-def deposit(step, moved, cell_index, row, shift_list, arrival):
-    sums, order, source = pl.pallas_call(
+        order_ref[place_ref[slot] % BLK] = slot
+
+
+def deposit(step, moved, low, row, place, accs):
+    *sums, order = pl.pallas_call(
         functools.partial(deposit_kernel, step),
-        out_shape=(
-            jax.ShapeDtypeStruct((9 * ROWS, LANES), F32),
-            jax.ShapeDtypeStruct((BLK,), jnp.int32),
-            jax.ShapeDtypeStruct((BLK,), jnp.int32),
-        ),
-        in_specs=[VMEM, VMEM, SMEM, SMEM, SMEM],
-        out_specs=(VMEM, SMEM, SMEM),
-        scratch_shapes=[pltpu.VMEM((LANES, LANES), F32)] * 2
-        + [pltpu.SMEM((BLK,), jnp.int32)]
-        + [pltpu.VMEM((9 * ROWS, LANES), F32)] * ACCS,
+        out_shape=(TABLE,) * ACCS + (jax.ShapeDtypeStruct((BLK,), jnp.int32),),
+        in_specs=[VMEM, VMEM, SMEM, SMEM] + [VMEM] * ACCS,
+        out_specs=(VMEM,) * ACCS + (SMEM,),
+        input_output_aliases={4 + k: k for k in range(ACCS)},
+        scratch_shapes=[pltpu.VMEM((LANES, LANES), F32)] * 2,
         compiler_params=pltpu.CompilerParams(vmem_limit_bytes=LIMIT),
         name="deposit",
-    )(moved, cell_index, row, shift_list, arrival)
-    return sums.reshape(3, 3, ROWS, LANES), order, source
+    )(moved, low, row, place, *accs)
+    return sums, order
 
 
 def split(x):
@@ -219,11 +239,33 @@
 
 
 def exchange_kernel(
-    step, sums_ref, moved_ref, rates_ref, mix_ref, cell_ref, row_ref, order_ref, source_ref, out_ref,
-    below, above, middle, left, right, table, chem, high2, low1, even, odd, reacted, pool,
-    up_sem, down_sem, west_sem, east_sem, mwest_sem, meast_sem, mup_sem, mdown_sem, send_sem, recv_sem,
+    step, moved_ref, rates_hbm, mix_hbm, low_ref, row_ref, order_ref, source_ref, *rest
 ):
     last = step == STEPS - 1
+    accs = rest[:ACCS]
+    out_ref = rest[ACCS]
+    blanks = () if last else rest[ACCS + 1:2 * ACCS + 1]
+    (
+        sums_ref, rates_ref, mix_ref, below, above, middle, left, right, table, chem, high2, low1, even, odd, reacted, pool,
+        up_sem, down_sem, west_sem, east_sem, mwest_sem, meast_sem, mup_sem, mdown_sem, send_sem, recv_sem, load_sem,
+    ) = rest[ACCS + 1 + len(blanks):]
+    loads = [
+        pltpu.make_async_copy(rates_hbm, rates_ref, load_sem.at[0]),
+        pltpu.make_async_copy(mix_hbm, mix_ref, load_sem.at[1]),
+    ]
+    for load in loads:
+        load.start()
+
+    def add_up(r):
+        @pl.loop(0, 3 * ROWS // 8, unroll=4)
+        def _(i):
+            at = pl.multiple_of(i * 8, 8)
+            part = pl.ds(r * 3 * ROWS + at, 8)
+            total = accs[0][part, :]
+            for acc in accs[1:]:
+                total = total + acc[part, :]
+            sums_ref[r, at // ROWS, pl.ds(pl.multiple_of(at % ROWS, 8), 8), :] = total
+
     band = lax.axis_index("lat")
     bands = lax.axis_size("lat")
     has_up = band < bands - 1
@@ -245,6 +287,8 @@
     def _():
         pl.semaphore_signal(barrier, inc=1, device_id={"lat": down}, device_id_type=MESH)
 
+    add_up(2)
+    add_up(0)
     pl.semaphore_wait(barrier, len(beside) + has_up.astype(jnp.int32) + has_down.astype(jnp.int32))
 
     def remote(src, dst, sem, index, device):
@@ -302,6 +346,9 @@
         above[...] = jnp.zeros_like(above)
         table[2] = jnp.zeros_like(table[2])
 
+    add_up(1)
+    for load in loads:
+        load.wait()
     high, low = pairs_of(rates_ref[...])
     high2[...] = high
     low1[...] = low
@@ -397,6 +444,8 @@
         else:
             parts[entry[0]](entry[1])
 
+    if not last:
+        blank_strips(blanks)
     for b in range(BLK):
         column = b % half_blk * LANES
         reacted[b] = chem[b // half_blk, :, column:column + LANES]
@@ -441,7 +490,7 @@
 
     def mixed(b, rows):
         means = rows[...].T
-        low = (cell_ref[step, pl.ds(b, 1), :] & ROWS) == 0
+        low = low_ref[step, pl.ds(b, 1), :] == 1
         picked = jnp.where(low, means[0:S], means[64:64 + S])
         return reacted[b] + mix * (picked - moved_ref[b])
 
@@ -486,16 +535,21 @@
             out_ref[slot] = pool[source_ref[slot]]
 
 
-def exchange(step, sums, moved, rates, mix, cell_index, row, order, source):
+def exchange(step, sums, moved, rates, mix, low, row, order, source):
     region = (3, ROWS, LANES)
     pair = pltpu.SemaphoreType.DMA((2, 3, CHUNKS))
     single = pltpu.SemaphoreType.DMA((2, CHUNKS))
+    blanks = 0 if step == STEPS - 1 else ACCS
+    state = jax.ShapeDtypeStruct((BLK, S, LANES), F32)
     return pl.pallas_call(
         functools.partial(exchange_kernel, step),
-        out_shape=jax.ShapeDtypeStruct((BLK, S, LANES), F32),
-        in_specs=[VMEM, VMEM, VMEM, VMEM, VMEM, SMEM, SMEM, SMEM],
-        out_specs=VMEM,
+        out_shape=(state,) + (TABLE,) * blanks,
+        in_specs=[VMEM, HBM, HBM, VMEM, SMEM, SMEM, SMEM] + [VMEM] * ACCS,
+        out_specs=(VMEM,) * (1 + blanks),
         scratch_shapes=[
+            pltpu.VMEM((3, 3, ROWS, LANES), F32),
+            pltpu.VMEM((S, S), F32),
+            pltpu.VMEM((1, S), F32),
             pltpu.VMEM(region, F32),
             pltpu.VMEM(region, F32),
             pltpu.VMEM(region, F32),
@@ -512,18 +566,20 @@
             pair, pair, single, single, single, single, pair, pair,
             pltpu.SemaphoreType.DMA((6,)),
             pltpu.SemaphoreType.DMA((6,)),
+            pltpu.SemaphoreType.DMA((2,)),
         ],
         compiler_params=pltpu.CompilerParams(collective_id=2 + step, has_side_effects=True, vmem_limit_bytes=LIMIT),
         name="exchange",
-    )(sums, moved, rates, mix, cell_index, row, order, source)
+    )(moved, rates, mix, low, row, order, source, *sums)
 
 
 def shards(species, reaction_rates, mix_rate, shift_list, arrival, cell_index):
-    moved, row = migrate(shift_list, arrival, species, cell_index)
+    inputs = (pltpu.with_memory_space_constraint(x, pltpu.HBM) for x in (shift_list, arrival, species, cell_index))
+    moved, row, low, place, source, *accs = migrate(*inputs)
     mix = mix_rate.reshape(1, S)
     for step in range(STEPS):
-        sums, order, source = deposit(step, moved, cell_index, row, shift_list, arrival)
-        moved = exchange(step, sums, moved, reaction_rates, mix, cell_index, row, order, source)
+        sums, order = deposit(step, moved, low, row, place, accs)
+        moved, *accs = exchange(step, sums, moved, reaction_rates, mix, low, row, order, source)
     return moved
 
 

time: 118 us -> 107 us (0.907); the launches traced: 116 us -> 107 us
  local copies, waits for them, and re-layouts: 6.3 us -> 0.89 us
  Pallas kernels: 109 us -> 106 us
    unnamed x25 -> x5, local copies, waits for them, and re-layouts: 6.3 us -> 0.89 us
    pallas_call x4, Pallas kernels: 97.7 us -> 93.6 us  [the longest x2 81.3 us: exchange(): pl.pallas_call(functools.partial(exchange_kernel, step), out_shape=(state...]
where the time goes in v3:
time: 107 us
  Pallas kernels  106 us (99%)
    pallas_call x2, Pallas kernels, exchange(): pl.pallas_call(functools.partial(exchange_kernel, step), out_shape=(state...  81.3 us
    pallas_call x2, Pallas kernels, deposit(): pl.pallas_call(functools.partial(deposit_kernel, step), out_shape=(TABLE,...  12.4 us
    pallas_call x1, Pallas kernels, migrate(): pl.pallas_call(migrate_kernel, out_shape=(jax.ShapeDtypeStruct((BLK, S, L...  12.2 us

profile of v3, /device:TPU:5, one launch (start us, length us, event | category | flops | bytes accessed | tf_op | source)
XLA Modules:
  0.0 106.8 jit_solution(15994469852021185823)
XLA Ops:
  0.0 12.2 %migrate.1 = (f32[32,48,128]{2,1,0:T(8,128)S(1)}, s32[2,32,128]{2,1,0:T(8,128)S(1)}, s32[2,32,128]{2,1,0:T(8,128)S(1)}, s32[32]{0:T(128)S(1)}, s32[32]{0:T(128)S...) custom-call(s32[2,1,32]{2,1,0:T(1,128)} %shift_hbm.1, ...), custom_call_target="tpu_custom_call" | custom-call | tf_op jit(solution)/shard_map/migrate/pallas_call | solution.py:165
  12.2 0.0 copy-start
  12.2 0.0 copy-start.1
  12.2 6.2 %deposit.2 = (f32[4608,128]{1,0:T(8,128)S(1)}, f32[4608,128]{1,0:T(8,128)S(1)}, f32[4608,128]{1,0:T(8,128)S(1)}, f32[4608,128]{1,0:T(8,128)S(1)}, f32[4608,128]{...) custom-call(f32[32,48,128]{2,1,0:T(8,128)S(1)} %get-tuple-element.37, ...), custom_call_target="tpu_custom_call", output_to_operand_aliasing={{0}: (4, {}), {1}: (5, {}), {2}: (6, {}), {3}: (7, {}), {4}... | custom-call | tf_op jit(solution)/shard_map/deposit/pallas_call | solution.py:217
  18.4 0.0 copy-done
  18.4 0.0 copy-done.1
  18.5 41.5 %exchange.2 = (f32[32,48,128]{2,1,0:T(8,128)S(1)}, f32[4608,128]{1,0:T(8,128)S(1)}, f32[4608,128]{1,0:T(8,128)S(1)}, f32[4608,128]{1,0:T(8,128)S(1)}, f32[4608,1...) custom-call(f32[32,48,128]{2,1,0:T(8,128)S(1)} %get-tuple-element.37.moved_ref, ...), custom_call_target="tpu_custom_call" | custom-call | tf_op jit(solution)/shard_map/exchange/pallas_call | solution.py:544
  60.0 6.2 %deposit.3 = (f32[4608,128]{1,0:T(8,128)S(1)}, f32[4608,128]{1,0:T(8,128)S(1)}, f32[4608,128]{1,0:T(8,128)S(1)}, f32[4608,128]{1,0:T(8,128)S(1)}, f32[4608,128]{...) custom-call(f32[32,48,128]{2,1,0:T(8,128)S(1)} %get-tuple-element.55, ...), custom_call_target="tpu_custom_call", output_to_operand_aliasing={{0}: (4, {}), {1}: (5, {}), {2}: (6, {}), {3}: (7, {}), {4}... | custom-call | tf_op jit(solution)/shard_map/deposit/pallas_call | solution.py:217
  66.2 39.7 %exchange.3 = f32[32,48,128]{2,1,0:T(8,128)S(1)} custom-call(f32[32,48,128]{2,1,0:T(8,128)S(1)} %get-tuple-element.55.moved_ref, f32[48,48]{1,0:T(8,128)S(1)} %copy-done, f32[1,48]{1,0:T(1,128)S(1)} %bitcast.2, s32[2,32,128]{2,1,0:T(8,128)S(1)} %get-tuple-element.38.low_ref, s32[2,32,128]{2,1,0:T(8,128)S(1)} %get-tuple-element.39.row_ref, ...), custom_call_target="tpu_custom_call" | custom-call | tf_op jit(solution)/shard_map/exchange/pallas_call | solution.py:544
  105.9 0.9 copy.32
Async XLA Ops:
  12.2 6.2 %copy-start = (f32[48,48]{1,0:T(8,128)S(1)}, f32[48,48]{1,0:T(8,128)}, u32[]{:S(2)}) copy-start(f32[48,48]{1,0:T(8,128)} %rates_hbm.3) | copy-start | bytes 27652
  12.2 6.2 %copy-start.1 = (f32[48]{0:T(128)S(1)}, f32[48]{0:T(128)}, u32[]{:S(2)}) copy-start(f32[48]{0:T(128)} %param.8) | copy-start | bytes 580

commit v4 on v3

--- a/solution.py
+++ b/solution.py
@@ -15,8 +15,10 @@
 STEPS = 2
 SUB = 32
 ACCS = 6
-CHUNKS = 4
-CHUNK = ROWS // CHUNKS
+QUARTER = ROWS // 4
+PACKED = 3 * QUARTER
+PIECES = 6
+PIECE = PACKED // PIECES
 F32 = jnp.float32
 BF16 = jnp.bfloat16
 MESH = pl.DeviceIdType.MESH
@@ -27,8 +29,12 @@
 LIMIT = 24 * 2**20
 BATCHES = (2, -2, 1, 1, -1, -1)
 FIRST = {2: 0, -2: 1, 1: 2, -1: 4}
-LAST_FIRST = (3, 0, 1, 2)
-PLAN = (6, ("a", 3), 2, ("a", 0), 2, ("a", 1), 2, ("b", 3), ("a", 2), 3, ("b", 0), 2, ("b", 1), 2, ("b", 2), 3, ("c", 0), 3, ("c", 1), 3, ("c", 2), 4)
+PLAN = (
+    ("a", 0), 1, ("a", 1), 1, ("a", 2), 2, ("a", 3), 1, ("a", 4), 1, ("a", 5), 1,
+    ("o", 0), ("b", 0), 1, ("o", 1), ("b", 1), 1, ("o", 2), ("b", 2), 1, ("o", 3), ("b", 3), 1, ("o", 4), ("b", 4), 1, ("o", 5), ("b", 5),
+    2, ("c", 0), 2, ("c", 1), 2, ("c", 2), 2, ("c", 3), 2, ("c", 4), 2, ("c", 5), 3,
+)
+EARLY = 5
 
 
 def around(axis, step):
@@ -246,25 +252,41 @@
     out_ref = rest[ACCS]
     blanks = () if last else rest[ACCS + 1:2 * ACCS + 1]
     (
-        sums_ref, rates_ref, mix_ref, below, above, middle, left, right, table, chem, high2, low1, even, odd, reacted, pool,
-        up_sem, down_sem, west_sem, east_sem, mwest_sem, meast_sem, mup_sem, mdown_sem, send_sem, recv_sem, load_sem,
+        sums_ref, counts, tallies, rates_ref, mix_ref, below, above, tally_below, tally_above, middle, tally_middle,
+        left, right, tally_left, tally_right, factors, table, chem, high2, low1, even, odd, reacted, pool,
+        up_sem, down_sem, west_sem, east_sem, mwest_sem, meast_sem, mup_sem, mdown_sem, tally_sem, send_sem, recv_sem, load_sem,
     ) = rest[ACCS + 1 + len(blanks):]
     loads = [
         pltpu.make_async_copy(rates_hbm, rates_ref, load_sem.at[0]),
         pltpu.make_async_copy(mix_hbm, mix_ref, load_sem.at[1]),
     ]
+    lane = lax.broadcasted_iota(jnp.int32, (8, LANES), 1)
+    spot = lane % 64
+    spare = spot >= S
     for load in loads:
         load.start()
 
     def add_up(r):
-        @pl.loop(0, 3 * ROWS // 8, unroll=4)
+        @pl.loop(0, QUARTER // 8)
         def _(i):
             at = pl.multiple_of(i * 8, 8)
-            part = pl.ds(r * 3 * ROWS + at, 8)
-            total = accs[0][part, :]
-            for acc in accs[1:]:
-                total = total + acc[part, :]
-            sums_ref[r, at // ROWS, pl.ds(pl.multiple_of(at % ROWS, 8), 8), :] = total
+            tally = jnp.zeros((8, LANES), F32)
+            for s in range(3):
+                quarters = []
+                for q in range(4):
+                    part = pl.ds((r * 3 + s) * ROWS + q * QUARTER + at, 8)
+                    total = accs[0][part, :]
+                    for acc in accs[1:]:
+                        total = total + acc[part, :]
+                    quarters.append(total)
+                    tally = jnp.where(spot == s * 8 + q, pltpu.roll(total, (s * 8 + q - S) % LANES, 1), tally)
+                for q in range(3):
+                    sums_ref[r, s, pl.ds(q * QUARTER + at, 8), :] = jnp.where(
+                        spare, pltpu.roll(quarters[3], S - 16 * q, 1), quarters[q]
+                    )
+            counts[pl.ds(at, 8), :] = tally
+
+        tallies[r] = counts[...].T.reshape(2, 64, LANES)
 
     band = lax.axis_index("lat")
     bands = lax.axis_size("lat")
@@ -297,53 +319,69 @@
             device_id=device, device_id_type=MESH,
         )
 
-    def chunk(c):
-        return pl.ds(c * CHUNK, CHUNK)
-
-    def sums_up(s, c):
-        return remote(sums_ref.at[2, s, chunk(c)], below.at[s, chunk(c)], up_sem, (s, c), {"lat": up})
-
-    def sums_down(s, c):
-        return remote(sums_ref.at[0, s, chunk(c)], above.at[s, chunk(c)], down_sem, (s, c), {"lat": down})
-
-    def sums_west(c):
-        return remote(middle.at[0, chunk(c)], right.at[chunk(c)], west_sem, (c,), {"lon": west})
-
-    def sums_east(c):
-        return remote(middle.at[2, chunk(c)], left.at[chunk(c)], east_sem, (c,), {"lon": east})
-
-    def means_west(c):
-        return remote(table.at[1, 1, chunk(c)], table.at[1, 2, chunk(c)], mwest_sem, (c,), {"lon": west})
-
-    def means_east(c):
-        return remote(table.at[1, 1, chunk(c)], table.at[1, 0, chunk(c)], meast_sem, (c,), {"lon": east})
-
-    def means_up(s, c):
-        return remote(table.at[1, s, chunk(c)], table.at[0, s, chunk(c)], mup_sem, (s, c), {"lat": up})
-
-    def means_down(s, c):
-        return remote(table.at[1, s, chunk(c)], table.at[2, s, chunk(c)], mdown_sem, (s, c), {"lat": down})
-
-    order = [(s, c) for c in LAST_FIRST for s in (0, 2, 1)]
+    def piece(p):
+        return pl.ds(p * PIECE, PIECE)
+
+    def sums_up(s, p):
+        return remote(sums_ref.at[2, s, piece(p)], below.at[s, piece(p)], up_sem, (s, p), {"lat": up})
+
+    def sums_down(s, p):
+        return remote(sums_ref.at[0, s, piece(p)], above.at[s, piece(p)], down_sem, (s, p), {"lat": down})
+
+    def sums_west(p):
+        return remote(middle.at[0, piece(p)], right.at[piece(p)], west_sem, (p,), {"lon": west})
+
+    def sums_east(p):
+        return remote(middle.at[2, piece(p)], left.at[piece(p)], east_sem, (p,), {"lon": east})
+
+    def means_west(p):
+        return remote(table.at[1, 1, piece(p)], table.at[1, 2, piece(p)], mwest_sem, (p,), {"lon": west})
+
+    def means_east(p):
+        return remote(table.at[1, 1, piece(p)], table.at[1, 0, piece(p)], meast_sem, (p,), {"lon": east})
+
+    def means_up(s, p):
+        return remote(table.at[1, s, piece(p)], table.at[0, s, piece(p)], mup_sem, (s, p), {"lat": up})
+
+    def means_down(s, p):
+        return remote(table.at[1, s, piece(p)], table.at[2, s, piece(p)], mdown_sem, (s, p), {"lat": down})
+
+    def tally_up():
+        return remote(tallies.at[2, :, pl.ds(0, 24)], tally_below, tally_sem, (0,), {"lat": up})
+
+    def tally_down():
+        return remote(tallies.at[0, :, pl.ds(0, 24)], tally_above, tally_sem, (1,), {"lat": down})
+
+    def tally_west():
+        return remote(tally_middle.at[:, pl.ds(0, 8)], tally_right, tally_sem, (2,), {"lon": west})
+
+    def tally_east():
+        return remote(tally_middle.at[:, pl.ds(16, 8)], tally_left, tally_sem, (3,), {"lon": east})
+
+    order = [(s, p) for p in range(PIECES) for s in (0, 2)] + [(1, p) for p in range(PIECES)]
 
     @pl.when(has_up)
     def _():
-        for s, c in order:
-            sums_up(s, c).start()
+        tally_up().start()
+        for s, p in order:
+            sums_up(s, p).start()
 
     @pl.when(has_down)
     def _():
-        for s, c in order:
-            sums_down(s, c).start()
+        tally_down().start()
+        for s, p in order:
+            sums_down(s, p).start()
 
     @pl.when(jnp.logical_not(has_down))
     def _():
         below[...] = jnp.zeros_like(below)
+        tally_below[...] = jnp.zeros_like(tally_below)
         table[0] = jnp.zeros_like(table[0])
 
     @pl.when(jnp.logical_not(has_up))
     def _():
         above[...] = jnp.zeros_like(above)
+        tally_above[...] = jnp.zeros_like(tally_above)
         table[2] = jnp.zeros_like(table[2])
 
     add_up(1)
@@ -368,76 +406,95 @@
 
         lax.fori_loop(0, substeps, advance, 0)
 
-    def strips(body):
-        @pl.loop(0, CHUNK // 8, unroll=4)
+    chemistry(EARLY)
+
+    def strips(first, rows, body):
+        @pl.loop(0, rows // 8, unroll=4)
         def _(i):
-            body(pl.multiple_of(i * 8, 8))
-
-    lane = lax.broadcasted_iota(jnp.int32, (8, LANES), 1)
-    spare = lane % 64 >= S
-
-    def bands_summed(c):
-        for s in (0, 2, 1):
+            body(pl.multiple_of(i * 8, 8) + first)
+
+    def bands_summed(s, p):
+        @pl.when(has_down)
+        def _():
+            sums_up(s, p).wait_recv()
+
+        @pl.when(has_up)
+        def _():
+            sums_down(s, p).wait_recv()
+
+        def add_bands(i):
+            part = pl.ds(i, 8)
+            middle[s, part, :] = sums_ref[1, s, part, :] + below[s, part, :] + above[s, part, :]
+
+        strips(p * PIECE, PIECE, add_bands)
+
+    def sides_summed(p):
+        if p == 0:
             @pl.when(has_down)
             def _():
-                sums_up(s, c).wait_recv()
+                tally_up().wait_recv()
 
             @pl.when(has_up)
             def _():
-                sums_down(s, c).wait_recv()
-
-            def add_bands(i):
-                part = pl.ds(c * CHUNK + i, 8)
-                middle[s, part, :] = sums_ref[1, s, part, :] + below[s, part, :] + above[s, part, :]
-
-            strips(add_bands)
-            if s == 0:
-                sums_west(c).start()
-            if s == 2:
-                sums_east(c).start()
-
-    def sectors_summed(c):
-        sums_west(c).wait_recv()
-        sums_east(c).wait_recv()
+                tally_down().wait_recv()
+
+            tally_middle[...] = tallies[1, :, 0:24] + tally_below[...] + tally_above[...]
+            tally_west().start()
+            tally_east().start()
+        bands_summed(0, p)
+        sums_west(p).start()
+        bands_summed(2, p)
+        sums_east(p).start()
+
+    def own_summed(p):
+        bands_summed(1, p)
+
+    def sectors_summed(p):
+        if p == 0:
+            tally_west().wait_recv()
+            tally_east().wait_recv()
+            tally = tally_middle[:, 8:16] + tally_left[...] + tally_right[...]
+            inverse = (1.0 / jnp.maximum(tally, 1.0)).reshape(16, LANES)
+            factors[...] = jnp.concatenate([inverse, jnp.zeros((LANES - 16, LANES), F32)], 0).T
+        sums_west(p).wait_recv()
+        sums_east(p).wait_recv()
+        q = p * PIECE // QUARTER
 
         def mean(i):
-            part = pl.ds(c * CHUNK + i, 8)
+            part = pl.ds(i, 8)
+            factor = factors[pl.ds(i - q * QUARTER, 8), :]
+            low = jnp.where(spare, factor[:, 3:4], factor[:, q:q + 1])
+            high = jnp.where(spare, factor[:, 11:12], factor[:, 8 + q:9 + q])
             total = middle[1, part, :] + left[part, :] + right[part, :]
-            count = jnp.where(lane < 64, total[:, S:S + 1], total[:, 64 + S:64 + S + 1])
-            means = total / jnp.maximum(count, 1.0)
-            if c < CHUNKS - 1:
-                others = table[1, 1, pl.ds((CHUNKS - 1) * CHUNK + i, 8), :]
-                means = jnp.where(spare, pltpu.roll(others, S - 16 * c, 1), means)
-            table[1, 1, part, :] = means
-
-        strips(mean)
-        if c < CHUNKS - 1:
-            means_west(c).start()
-            means_east(c).start()
-
-            @pl.when(has_up)
-            def _():
-                means_up(1, c).start()
-
-            @pl.when(has_down)
-            def _():
-                means_down(1, c).start()
-
-    def means_passed(c):
-        means_west(c).wait_recv()
-        means_east(c).wait_recv()
+            table[1, 1, part, :] = total * jnp.where(lane < 64, low, high)
+
+        strips(p * PIECE, PIECE, mean)
+        means_west(p).start()
+        means_east(p).start()
 
         @pl.when(has_up)
         def _():
-            means_up(0, c).start()
-            means_up(2, c).start()
+            means_up(1, p).start()
 
         @pl.when(has_down)
         def _():
-            means_down(0, c).start()
-            means_down(2, c).start()
-
-    parts = {"a": bands_summed, "b": sectors_summed, "c": means_passed}
+            means_down(1, p).start()
+
+    def means_passed(p):
+        means_west(p).wait_recv()
+        means_east(p).wait_recv()
+
+        @pl.when(has_up)
+        def _():
+            means_up(0, p).start()
+            means_up(2, p).start()
+
+        @pl.when(has_down)
+        def _():
+            means_down(0, p).start()
+            means_down(2, p).start()
+
+    parts = {"a": sides_summed, "o": own_summed, "b": sectors_summed, "c": means_passed}
     for entry in PLAN:
         if isinstance(entry, int):
             chemistry(entry)
@@ -450,36 +507,35 @@
         column = b % half_blk * LANES
         reacted[b] = chem[b // half_blk, :, column:column + LANES]
 
-    for s, c in order:
-        @pl.when(has_up)
-        def _():
-            sums_up(s, c).wait_send()
-            if c < CHUNKS - 1:
-                means_up(s, c).wait_send()
-                means_down(s, c).wait_recv()
-
-        @pl.when(has_down)
-        def _():
-            sums_down(s, c).wait_send()
-            if c < CHUNKS - 1:
-                means_down(s, c).wait_send()
-                means_up(s, c).wait_recv()
-    for c in range(CHUNKS):
-        sums_west(c).wait_send()
-        sums_east(c).wait_send()
-        if c < CHUNKS - 1:
-            means_west(c).wait_send()
-            means_east(c).wait_send()
+    @pl.when(has_up)
+    def _():
+        tally_up().wait_send()
+        for s, p in order:
+            sums_up(s, p).wait_send()
+            means_up(s, p).wait_send()
+            means_down(s, p).wait_recv()
+
+    @pl.when(has_down)
+    def _():
+        tally_down().wait_send()
+        for s, p in order:
+            sums_down(s, p).wait_send()
+            means_down(s, p).wait_send()
+            means_up(s, p).wait_recv()
+
+    tally_west().wait_send()
+    tally_east().wait_send()
+    for p in range(PIECES):
+        for copy in (sums_west(p), sums_east(p), means_west(p), means_east(p)):
+            copy.wait_send()
 
     for r in range(3):
         for s in range(3):
-            if (r, s) != (1, 1):
-                def unpack(i):
-                    found = [pltpu.roll(table[r, s, pl.ds(q * CHUNK + i, 8), :], LANES - S + 16 * q, 1) for q in range(3)]
-                    spot = lane % 64
-                    table[r, s, pl.ds(3 * CHUNK + i, 8), :] = jnp.where(spot < 16, found[0], jnp.where(spot < 32, found[1], found[2]))
-
-                strips(unpack)
+            def unpack(i):
+                found = [pltpu.roll(table[r, s, pl.ds(q * QUARTER + i, 8), :], LANES - S + 16 * q, 1) for q in range(3)]
+                table[r, s, pl.ds(PACKED + i, 8), :] = jnp.where(spot < 16, found[0], jnp.where(spot < 32, found[1], found[2]))
+
+            strips(0, QUARTER, unpack)
 
     mix = jnp.broadcast_to(mix_ref[...], (LANES, S)).T
     flat = table.reshape(9 * ROWS, LANES)
@@ -536,9 +592,13 @@
 
 
 def exchange(step, sums, moved, rates, mix, low, row, order, source):
-    region = (3, ROWS, LANES)
-    pair = pltpu.SemaphoreType.DMA((2, 3, CHUNKS))
-    single = pltpu.SemaphoreType.DMA((2, CHUNKS))
+    region = pltpu.VMEM((3, PACKED, LANES), F32)
+    beside = pltpu.VMEM((PACKED, LANES), F32)
+    tally = pltpu.VMEM((2, 24, LANES), F32)
+    tally_beside = pltpu.VMEM((2, 8, LANES), F32)
+    square = pltpu.VMEM((LANES, LANES), F32)
+    pair = pltpu.SemaphoreType.DMA((2, 3, PIECES))
+    single = pltpu.SemaphoreType.DMA((2, PIECES))
     blanks = 0 if step == STEPS - 1 else ACCS
     state = jax.ShapeDtypeStruct((BLK, S, LANES), F32)
     return pl.pallas_call(
@@ -547,23 +607,24 @@
         in_specs=[VMEM, HBM, HBM, VMEM, SMEM, SMEM, SMEM] + [VMEM] * ACCS,
         out_specs=(VMEM,) * (1 + blanks),
         scratch_shapes=[
-            pltpu.VMEM((3, 3, ROWS, LANES), F32),
+            pltpu.VMEM((3, 3, PACKED, LANES), F32),
+            square,
+            pltpu.VMEM((3, 2, 64, LANES), F32),
             pltpu.VMEM((S, S), F32),
             pltpu.VMEM((1, S), F32),
-            pltpu.VMEM(region, F32),
-            pltpu.VMEM(region, F32),
-            pltpu.VMEM(region, F32),
-            pltpu.VMEM((ROWS, LANES), F32),
-            pltpu.VMEM((ROWS, LANES), F32),
+            region, region, tally, tally, region, tally,
+            beside, beside, tally_beside, tally_beside,
+            square,
             pltpu.VMEM((3, 3, ROWS, LANES), F32),
             pltpu.VMEM((2, S, BLK // 2 * LANES), F32),
             pltpu.VMEM((2 * S, 4 * S), BF16),
             pltpu.VMEM((2 * S, 2 * S), BF16),
-            pltpu.VMEM((LANES, LANES), F32),
-            pltpu.VMEM((LANES, LANES), F32),
+            square,
+            square,
             pltpu.VMEM((BLK, S, LANES), F32),
             pltpu.VMEM((2 * BLK, S, LANES), F32),
             pair, pair, single, single, single, single, pair, pair,
+            pltpu.SemaphoreType.DMA((2, 4)),
             pltpu.SemaphoreType.DMA((6,)),
             pltpu.SemaphoreType.DMA((6,)),
             pltpu.SemaphoreType.DMA((2,)),

time: 107 us -> 105 us (0.981)
  Pallas kernels: 106 us -> 104 us
    pallas_call x2, Pallas kernels: 81.3 us -> 78.9 us  [exchange(): pl.pallas_call(functools.partial(exchange_kernel, step), out_shape=(state...]
where the time goes in v4:
time: 105 us; the launch traced here: 104 us
  Pallas kernels  104 us (99%)
    pallas_call x2, Pallas kernels, exchange(): pl.pallas_call(functools.partial(exchange_kernel, step), out_shape=(state...  78.9 us
    pallas_call x2, Pallas kernels, deposit(): pl.pallas_call(functools.partial(deposit_kernel, step), out_shape=(TABLE,...  12.4 us
    pallas_call x1, Pallas kernels, migrate(): pl.pallas_call(migrate_kernel, out_shape=(jax.ShapeDtypeStruct((BLK, S, L...  12.2 us

profile of v4, /device:TPU:5, one launch (start us, length us, event | category | flops | bytes accessed | tf_op | source)
XLA Modules:
  0.0 104.5 jit_solution(7190698989275613264)
XLA Ops:
  0.0 12.2 %migrate.1 = (f32[32,48,128]{2,1,0:T(8,128)S(1)}, s32[2,32,128]{2,1,0:T(8,128)S(1)}, s32[2,32,128]{2,1,0:T(8,128)S(1)}, s32[32]{0:T(128)S(1)}, s32[32]{0:T(128)S...) custom-call(s32[2,1,32]{2,1,0:T(1,128)} %shift_hbm.1, ...), custom_call_target="tpu_custom_call" | custom-call | tf_op jit(solution)/shard_map/migrate/pallas_call | solution.py:171
  12.2 0.0 copy-start
  12.2 0.0 copy-start.1
  12.2 6.2 %deposit.2 = (f32[4608,128]{1,0:T(8,128)S(1)}, f32[4608,128]{1,0:T(8,128)S(1)}, f32[4608,128]{1,0:T(8,128)S(1)}, f32[4608,128]{1,0:T(8,128)S(1)}, f32[4608,128]{...) custom-call(f32[32,48,128]{2,1,0:T(8,128)S(1)} %get-tuple-element.37, ...), custom_call_target="tpu_custom_call", output_to_operand_aliasing={{0}: (4, {}), {1}: (5, {}), {2}: (6, {}), {3}: (7, {}), {4}... | custom-call | tf_op jit(solution)/shard_map/deposit/pallas_call | solution.py:223
  18.4 0.0 copy-done
  18.4 0.0 copy-done.1
  18.5 40.8 %exchange.2 = (f32[32,48,128]{2,1,0:T(8,128)S(1)}, f32[4608,128]{1,0:T(8,128)S(1)}, f32[4608,128]{1,0:T(8,128)S(1)}, f32[4608,128]{1,0:T(8,128)S(1)}, f32[4608,1...) custom-call(f32[32,48,128]{2,1,0:T(8,128)S(1)} %get-tuple-element.37.moved_ref, ...), custom_call_target="tpu_custom_call" | custom-call | tf_op jit(solution)/shard_map/exchange/pallas_call | solution.py:604
  59.2 6.2 %deposit.3 = (f32[4608,128]{1,0:T(8,128)S(1)}, f32[4608,128]{1,0:T(8,128)S(1)}, f32[4608,128]{1,0:T(8,128)S(1)}, f32[4608,128]{1,0:T(8,128)S(1)}, f32[4608,128]{...) custom-call(f32[32,48,128]{2,1,0:T(8,128)S(1)} %get-tuple-element.55, ...), custom_call_target="tpu_custom_call", output_to_operand_aliasing={{0}: (4, {}), {1}: (5, {}), {2}: (6, {}), {3}: (7, {}), {4}... | custom-call | tf_op jit(solution)/shard_map/deposit/pallas_call | solution.py:223
  65.4 38.2 %exchange.3 = f32[32,48,128]{2,1,0:T(8,128)S(1)} custom-call(f32[32,48,128]{2,1,0:T(8,128)S(1)} %get-tuple-element.55.moved_ref, f32[48,48]{1,0:T(8,128)S(1)} %copy-done, f32[1,48]{1,0:T(1,128)S(1)} %bitcast.2, s32[2,32,128]{2,1,0:T(8,128)S(1)} %get-tuple-element.38.low_ref, s32[2,32,128]{2,1,0:T(8,128)S(1)} %get-tuple-element.39.row_ref, ...), custom_call_target="tpu_custom_call" | custom-call | tf_op jit(solution)/shard_map/exchange/pallas_call | solution.py:604
  103.6 0.9 copy.32
Async XLA Ops:
  12.2 6.2 %copy-start = (f32[48,48]{1,0:T(8,128)S(1)}, f32[48,48]{1,0:T(8,128)}, u32[]{:S(2)}) copy-start(f32[48,48]{1,0:T(8,128)} %rates_hbm.3) | copy-start | bytes 27652
  12.2 6.2 %copy-start.1 = (f32[48]{0:T(128)S(1)}, f32[48]{0:T(128)}, u32[]{:S(2)}) copy-start(f32[48]{0:T(128)} %param.8) | copy-start | bytes 580

commit v5 on v4

--- a/solution.py
+++ b/solution.py
@@ -10,6 +10,7 @@
 S = 48
 LANES = 128
 BLK = 32
+HALF_BLK = BLK // 2
 CELL_DEV = 1024
 ROWS = CELL_DEV // 2
 STEPS = 2
@@ -30,11 +31,11 @@
 BATCHES = (2, -2, 1, 1, -1, -1)
 FIRST = {2: 0, -2: 1, 1: 2, -1: 4}
 PLAN = (
-    ("a", 0), 1, ("a", 1), 1, ("a", 2), 2, ("a", 3), 1, ("a", 4), 1, ("a", 5), 1,
-    ("o", 0), ("b", 0), 1, ("o", 1), ("b", 1), 1, ("o", 2), ("b", 2), 1, ("o", 3), ("b", 3), 1, ("o", 4), ("b", 4), 1, ("o", 5), ("b", 5),
-    2, ("c", 0), 2, ("c", 1), 2, ("c", 2), 2, ("c", 3), 2, ("c", 4), 2, ("c", 5), 3,
+    ("a", 0), ("a", 1), 1, ("a", 2), ("a", 3), 1, ("a", 4), ("a", 5), 1,
+    ("o", 0), ("b", 0), ("o", 1), ("b", 1), 1, ("o", 2), ("b", 2), ("o", 3), ("b", 3), 1, ("o", 4), ("b", 4), ("o", 5), ("b", 5),
+    1, ("c", 0), 1, ("c", 1), 1, ("c", 2), 1, ("c", 3), 1, ("c", 4), 1, ("c", 5), 2,
 )
-EARLY = 5
+EARLY = 3
 
 
 def around(axis, step):
@@ -189,9 +190,32 @@
     )(shift_list, arrival, state, cell_index)
 
 
-def deposit_kernel(step, moved_ref, low_ref, row_ref, place_ref, *rest):
+def split(x):
+    high = x.astype(BF16)
+    return high, (x - high.astype(F32)).astype(BF16)
+
+
+def pairs_of(rates):
+    zero = jnp.zeros((S, S), F32)
+    high, low = split(jnp.concatenate([jnp.concatenate([rates, zero], 1), jnp.concatenate([zero, rates], 1)], 0))
+    return jnp.concatenate([high, high], 1), low
+
+
+def substep(chem, high2, low1):
+    state = chem[...].reshape(2 * S, HALF_BLK * LANES)
+    high, low = split(state)
+    pushed = jnp.dot(high2[...], jnp.concatenate([high, low], 0), preferred_element_type=F32)
+    pushed = pushed + jnp.dot(low1[...], high, preferred_element_type=F32)
+    chem[...] = (state + (2.0 / SUB) * jnp.tanh(pushed)).reshape(2, S, HALF_BLK * LANES)
+
+
+def deposit_kernel(step, moved_ref, low_ref, row_ref, place_ref, rates_ref, *rest):
     accs = rest[ACCS:2 * ACCS]
-    order_ref, even, odd = rest[2 * ACCS:]
+    order_ref, chem, even, odd, high2, low1 = rest[2 * ACCS:]
+    high2[...], low1[...] = pairs_of(rates_ref[...])
+    for b in range(BLK):
+        column = b % HALF_BLK * LANES
+        chem[b // HALF_BLK, :, column:column + LANES] = moved_ref[b]
     tail = jnp.where(lax.broadcasted_iota(jnp.int32, (16, LANES), 0) == 0, 1.0, 0.0)
 
     def turn(b, rows):
@@ -209,6 +233,7 @@
 
     @pl.loop(0, BLK // 2)
     def _(i):
+        substep(chem, high2, low1)
         turn(2 * i + 1, odd)
         add(2 * i, even)
         turn(jnp.minimum(2 * i + 2, BLK - 1), even)
@@ -219,33 +244,28 @@
         order_ref[place_ref[slot] % BLK] = slot
 
 
-def deposit(step, moved, low, row, place, accs):
-    *sums, order = pl.pallas_call(
+def deposit(step, moved, low, row, place, rates, accs):
+    *sums, order, chem = pl.pallas_call(
         functools.partial(deposit_kernel, step),
-        out_shape=(TABLE,) * ACCS + (jax.ShapeDtypeStruct((BLK,), jnp.int32),),
-        in_specs=[VMEM, VMEM, SMEM, SMEM] + [VMEM] * ACCS,
-        out_specs=(VMEM,) * ACCS + (SMEM,),
-        input_output_aliases={4 + k: k for k in range(ACCS)},
-        scratch_shapes=[pltpu.VMEM((LANES, LANES), F32)] * 2,
+        out_shape=(TABLE,) * ACCS
+        + (jax.ShapeDtypeStruct((BLK,), jnp.int32), jax.ShapeDtypeStruct((2, S, HALF_BLK * LANES), F32)),
+        in_specs=[VMEM, VMEM, SMEM, SMEM, VMEM] + [VMEM] * ACCS,
+        out_specs=(VMEM,) * ACCS + (SMEM, VMEM),
+        input_output_aliases={5 + k: k for k in range(ACCS)},
+        scratch_shapes=[
+            pltpu.VMEM((LANES, LANES), F32),
+            pltpu.VMEM((LANES, LANES), F32),
+            pltpu.VMEM((2 * S, 4 * S), BF16),
+            pltpu.VMEM((2 * S, 2 * S), BF16),
+        ],
         compiler_params=pltpu.CompilerParams(vmem_limit_bytes=LIMIT),
         name="deposit",
-    )(moved, low, row, place, *accs)
-    return sums, order
-
-
-def split(x):
-    high = x.astype(BF16)
-    return high, (x - high.astype(F32)).astype(BF16)
-
-
-def pairs_of(rates):
-    zero = jnp.zeros((S, S), F32)
-    high, low = split(jnp.concatenate([jnp.concatenate([rates, zero], 1), jnp.concatenate([zero, rates], 1)], 0))
-    return jnp.concatenate([high, high], 1), low
+    )(moved, low, row, place, rates, *accs)
+    return sums, order, chem
 
 
 def exchange_kernel(
-    step, moved_ref, rates_hbm, mix_hbm, low_ref, row_ref, order_ref, source_ref, *rest
+    step, moved_ref, chem_ref, rates_hbm, mix_hbm, low_ref, row_ref, order_ref, source_ref, *rest
 ):
     last = step == STEPS - 1
     accs = rest[:ACCS]
@@ -267,7 +287,7 @@
         load.start()
 
     def add_up(r):
-        @pl.loop(0, QUARTER // 8)
+        @pl.loop(0, QUARTER // 8, unroll=4)
         def _(i):
             at = pl.multiple_of(i * 8, 8)
             tally = jnp.zeros((8, LANES), F32)
@@ -387,24 +407,13 @@
     add_up(1)
     for load in loads:
         load.wait()
-    high, low = pairs_of(rates_ref[...])
-    high2[...] = high
-    low1[...] = low
-    half_blk = BLK // 2
-    for b in range(BLK):
-        column = b % half_blk * LANES
-        chem[b // half_blk, :, column:column + LANES] = moved_ref[b]
+    high2[...], low1[...] = pairs_of(rates_ref[...])
+    chem[...] = chem_ref[...]
 
     def chemistry(substeps):
-        def advance(_, current):
-            state = chem[...].reshape(2 * S, half_blk * LANES)
-            high, low = split(state)
-            pushed = jnp.dot(high2[...], jnp.concatenate([high, low], 0), preferred_element_type=F32)
-            pushed = pushed + jnp.dot(low1[...], high, preferred_element_type=F32)
-            chem[...] = (state + (2.0 / SUB) * jnp.tanh(pushed)).reshape(2, S, half_blk * LANES)
-            return current
-
-        lax.fori_loop(0, substeps, advance, 0)
+        @pl.loop(0, substeps)
+        def _(_):
+            substep(chem, high2, low1)
 
     chemistry(EARLY)
 
@@ -504,38 +513,35 @@
     if not last:
         blank_strips(blanks)
     for b in range(BLK):
-        column = b % half_blk * LANES
-        reacted[b] = chem[b // half_blk, :, column:column + LANES]
-
-    @pl.when(has_up)
-    def _():
-        tally_up().wait_send()
-        for s, p in order:
-            sums_up(s, p).wait_send()
-            means_up(s, p).wait_send()
-            means_down(s, p).wait_recv()
-
-    @pl.when(has_down)
-    def _():
-        tally_down().wait_send()
-        for s, p in order:
-            sums_down(s, p).wait_send()
-            means_down(s, p).wait_send()
-            means_up(s, p).wait_recv()
-
-    tally_west().wait_send()
-    tally_east().wait_send()
-    for p in range(PIECES):
-        for copy in (sums_west(p), sums_east(p), means_west(p), means_east(p)):
-            copy.wait_send()
-
-    for r in range(3):
-        for s in range(3):
-            def unpack(i):
+        column = b % HALF_BLK * LANES
+        reacted[b] = chem[b // HALF_BLK, :, column:column + LANES]
+
+    def means_landed(sectors):
+        @pl.when(has_up)
+        def _():
+            for s, p in order:
+                if s in sectors:
+                    means_down(s, p).wait_recv()
+
+        @pl.when(has_down)
+        def _():
+            for s, p in order:
+                if s in sectors:
+                    means_up(s, p).wait_recv()
+
+    def unpack_regions(regions):
+        def unpack(i):
+            for r, s in regions:
                 found = [pltpu.roll(table[r, s, pl.ds(q * QUARTER + i, 8), :], LANES - S + 16 * q, 1) for q in range(3)]
                 table[r, s, pl.ds(PACKED + i, 8), :] = jnp.where(spot < 16, found[0], jnp.where(spot < 32, found[1], found[2]))
 
-            strips(0, QUARTER, unpack)
+        strips(0, QUARTER, unpack)
+
+    unpack_regions([(1, 0), (1, 1), (1, 2)])
+    means_landed((1,))
+    unpack_regions([(0, 1), (2, 1)])
+    means_landed((0, 2))
+    unpack_regions([(0, 0), (0, 2), (2, 0), (2, 2)])
 
     mix = jnp.broadcast_to(mix_ref[...], (LANES, S)).T
     flat = table.reshape(9 * ROWS, LANES)
@@ -556,6 +562,26 @@
         gather(second, odd)
         target[2 * i] = mixed(first, even)
         target[2 * i + 1] = mixed(second, odd)
+
+    @pl.when(has_up)
+    def _():
+        tally_up().wait_send()
+        for s, p in order:
+            sums_up(s, p).wait_send()
+            means_up(s, p).wait_send()
+
+    @pl.when(has_down)
+    def _():
+        tally_down().wait_send()
+        for s, p in order:
+            sums_down(s, p).wait_send()
+            means_down(s, p).wait_send()
+
+    tally_west().wait_send()
+    tally_east().wait_send()
+    for p in range(PIECES):
+        for copy in (sums_west(p), sums_east(p), means_west(p), means_east(p)):
+            copy.wait_send()
 
     if last:
         @pl.loop(0, BLK // 2)
@@ -591,7 +617,7 @@
             out_ref[slot] = pool[source_ref[slot]]
 
 
-def exchange(step, sums, moved, rates, mix, low, row, order, source):
+def exchange(step, sums, moved, chem, rates, mix, low, row, order, source):
     region = pltpu.VMEM((3, PACKED, LANES), F32)
     beside = pltpu.VMEM((PACKED, LANES), F32)
     tally = pltpu.VMEM((2, 24, LANES), F32)
@@ -604,7 +630,7 @@
     return pl.pallas_call(
         functools.partial(exchange_kernel, step),
         out_shape=(state,) + (TABLE,) * blanks,
-        in_specs=[VMEM, HBM, HBM, VMEM, SMEM, SMEM, SMEM] + [VMEM] * ACCS,
+        in_specs=[VMEM, VMEM, HBM, HBM, VMEM, SMEM, SMEM, SMEM] + [VMEM] * ACCS,
         out_specs=(VMEM,) * (1 + blanks),
         scratch_shapes=[
             pltpu.VMEM((3, 3, PACKED, LANES), F32),
@@ -631,7 +657,7 @@
         ],
         compiler_params=pltpu.CompilerParams(collective_id=2 + step, has_side_effects=True, vmem_limit_bytes=LIMIT),
         name="exchange",
-    )(moved, rates, mix, low, row, order, source, *sums)
+    )(moved, chem, rates, mix, low, row, order, source, *sums)
 
 
 def shards(species, reaction_rates, mix_rate, shift_list, arrival, cell_index):
@@ -639,8 +665,8 @@
     moved, row, low, place, source, *accs = migrate(*inputs)
     mix = mix_rate.reshape(1, S)
     for step in range(STEPS):
-        sums, order = deposit(step, moved, low, row, place, accs)
-        moved, *accs = exchange(step, sums, moved, reaction_rates, mix, low, row, order, source)
+        sums, order, chem = deposit(step, moved, low, row, place, reaction_rates, accs)
+        moved, *accs = exchange(step, sums, moved, chem, reaction_rates, mix, low, row, order, source)
     return moved
 
 

time: 105 us -> 99.9 us (0.951)
  Pallas kernels: 104 us -> 97.8 us
    pallas_call x2, Pallas kernels: 78.9 us -> 67.3 us  [exchange(): pl.pallas_call(functools.partial(exchange_kernel, step), out_shape=(state...]
    pallas_call x2, Pallas kernels: 12.4 us -> 18.4 us  [deposit(): pl.pallas_call(functools.partial(deposit_kernel, step), out_shape=(TABLE,...]
where the time goes in v5:
time: 99.9 us; the launch traced here: 99.5 us
  Pallas kernels  97.8 us (98%)
  local copies, waits for them, and re-layouts  1.62 us (2%)
    pallas_call x2, Pallas kernels, exchange(): pl.pallas_call(functools.partial(exchange_kernel, step), out_shape=(state...  67.3 us
    pallas_call x2, Pallas kernels, deposit(): pl.pallas_call(functools.partial(deposit_kernel, step), out_shape=(TABLE,...  18.4 us
    pallas_call x1, Pallas kernels, migrate(): pl.pallas_call(migrate_kernel, out_shape=(jax.ShapeDtypeStruct((BLK, S, L...  12.2 us

profile of v5, /device:TPU:5, one launch (start us, length us, event | category | flops | bytes accessed | tf_op | source)
XLA Modules:
  0.0 99.5 jit_solution(2931200015494583212)
XLA Ops:
  0.0 12.2 %migrate.1 = (f32[32,48,128]{2,1,0:T(8,128)S(1)}, s32[2,32,128]{2,1,0:T(8,128)S(1)}, s32[2,32,128]{2,1,0:T(8,128)S(1)}, s32[32]{0:T(128)S(1)}, s32[32]{0:T(128)S...) custom-call(s32[2,1,32]{2,1,0:T(1,128)} %shift_hbm.1, ...), custom_call_target="tpu_custom_call" | custom-call | tf_op jit(solution)/shard_map/migrate/pallas_call | solution.py:172
  12.2 0.0 copy-start
  12.2 0.7 copy-done
  13.0 0.0 copy-start.1
  13.0 9.0 %deposit.2 = (f32[4608,128]{1,0:T(8,128)S(1)}, f32[4608,128]{1,0:T(8,128)S(1)}, f32[4608,128]{1,0:T(8,128)S(1)}, f32[4608,128]{1,0:T(8,128)S(1)}, f32[4608,128]{...) custom-call(f32[32,48,128]{2,1,0:T(8,128)S(1)} %get-tuple-element.39, ...), custom_call_target="tpu_custom_call", output_to_operand_aliasing={{0}: (5, {}), {1}: (6, {}), {2}: (7, {}), {3}: (8, {}), {4}... | custom-call | tf_op jit(solution)/shard_map/deposit/pallas_call | solution.py:248
  22.0 0.0 copy-done.1
  22.0 34.7 %exchange.2 = (f32[32,48,128]{2,1,0:T(8,128)S(1)}, f32[4608,128]{1,0:T(8,128)S(1)}, f32[4608,128]{1,0:T(8,128)S(1)}, f32[4608,128]{1,0:T(8,128)S(1)}, f32[4608,1...) custom-call(f32[32,48,128]{2,1,0:T(8,128)S(1)} %get-tuple-element.39.moved_ref, ...), custom_call_target="tpu_custom_call" | custom-call | tf_op jit(solution)/shard_map/exchange/pallas_call | solution.py:630
  56.7 9.4 %deposit.3 = (f32[4608,128]{1,0:T(8,128)S(1)}, f32[4608,128]{1,0:T(8,128)S(1)}, f32[4608,128]{1,0:T(8,128)S(1)}, f32[4608,128]{1,0:T(8,128)S(1)}, f32[4608,128]{...) custom-call(f32[32,48,128]{2,1,0:T(8,128)S(1)} %get-tuple-element.58, ...), custom_call_target="tpu_custom_call", output_to_operand_aliasing={{0}: (5, {}), {1}: (6, {}), {2}: (7, {}), {3}: (8, {}), {4}... | custom-call | tf_op jit(solution)/shard_map/deposit/pallas_call | solution.py:248
  66.1 32.6 %exchange.3 = f32[32,48,128]{2,1,0:T(8,128)S(1)} custom-call(f32[32,48,128]{2,1,0:T(8,128)S(1)} %get-tuple-element.58.moved_ref, f32[2,48,2048]{2,1,0:T(8,128)S(1)} %get-tuple-element.65.chem_ref, f32[48,48]{1,0:T(8,128)S(1)} %copy-done, f32[1,48]{1,0:T(1,128)S(1)} %bitcast.2, s32[2,32,128]{2,1,0:T(8,128)S(1)} %get-tuple-element.40.low_ref, ...), custom_call_target="tpu_custom_call" | custom-call | tf_op jit(solution)/shard_map/exchange/pallas_call | solution.py:630
  98.6 0.9 copy.32
Async XLA Ops:
  12.2 0.7 copy-start
  13.0 9.0 %copy-start.1 = (f32[48]{0:T(128)S(1)}, f32[48]{0:T(128)}, u32[]{:S(2)}) copy-start(f32[48]{0:T(128)} %param.8) | copy-start | bytes 580

commit v6 on v5

--- a/solution.py
+++ b/solution.py
@@ -31,11 +31,11 @@
 BATCHES = (2, -2, 1, 1, -1, -1)
 FIRST = {2: 0, -2: 1, 1: 2, -1: 4}
 PLAN = (
-    ("a", 0), ("a", 1), 1, ("a", 2), ("a", 3), 1, ("a", 4), ("a", 5), 1,
+    ("a", 0), 1, ("a", 1), 1, ("a", 2), 1, ("a", 3), 1, ("a", 4), 1, ("a", 5), 1,
     ("o", 0), ("b", 0), ("o", 1), ("b", 1), 1, ("o", 2), ("b", 2), ("o", 3), ("b", 3), 1, ("o", 4), ("b", 4), ("o", 5), ("b", 5),
-    1, ("c", 0), 1, ("c", 1), 1, ("c", 2), 1, ("c", 3), 1, ("c", 4), 1, ("c", 5), 2,
+    3, ("c", 0), 1, ("c", 1), 1, ("c", 2), 1, ("c", 3), 1, ("c", 4), 1, ("c", 5), 4,
 )
-EARLY = 3
+EARLY = 4
 
 
 def around(axis, step):
@@ -95,13 +95,19 @@
             ref[part, :] = blank
 
 
-def migrate_kernel(shift_hbm, arrival_hbm, state_hbm, cell_hbm, moved_ref, row_ref, low_ref, place_ref, source_ref, *rest):
+def migrate_kernel(
+    shift_hbm, arrival_hbm, state_hbm, cell_hbm, rates_hbm, mix_hbm,
+    moved_ref, row_ref, low_ref, place_ref, source_ref, rates_ref, mix_ref, *rest
+):
     accs = rest[:ACCS]
     shift_ref, arrival_ref, state_ref, cell_ref, pool, pool_at, load_sem, send_sem, recv_sem = rest[ACCS:]
     loads = [
         pltpu.make_async_copy(src, dst, load_sem.at[k])
         for k, (src, dst) in enumerate(
-            ((shift_hbm, shift_ref), (arrival_hbm, arrival_ref), (state_hbm, state_ref), (cell_hbm, cell_ref))
+            (
+                (shift_hbm, shift_ref), (arrival_hbm, arrival_ref), (state_hbm, state_ref), (cell_hbm, cell_ref),
+                (rates_hbm, rates_ref), (mix_hbm, mix_ref),
+            )
         )
     ]
     for load in loads:
@@ -137,7 +143,8 @@
             batch_copy(pool, send_sem, recv_sem, k, unit).start()
 
     each_unit(polar, start)
-    loads[3].wait()
+    for load in loads[3:]:
+        load.wait()
     sectors = lax.axis_size("lon")
     cell = cell_ref[...]
     owner = cell // CELL_DEV
@@ -166,14 +173,16 @@
         moved_ref[slot] = jnp.where(at < BLK, state_ref[old], pool[at])
 
 
-def migrate(shift_list, arrival, state, cell_index):
+def migrate(shift_list, arrival, state, cell_index, rates, mix):
     whole = jax.ShapeDtypeStruct((STEPS, BLK, LANES), jnp.int32)
     slots = jax.ShapeDtypeStruct((BLK,), jnp.int32)
     return pl.pallas_call(
         migrate_kernel,
-        out_shape=(jax.ShapeDtypeStruct((BLK, S, LANES), F32), whole, whole, slots, slots) + (TABLE,) * ACCS,
-        in_specs=[HBM] * 4,
-        out_specs=(VMEM, VMEM, VMEM, SMEM, SMEM) + (VMEM,) * ACCS,
+        out_shape=(jax.ShapeDtypeStruct((BLK, S, LANES), F32), whole, whole, slots, slots)
+        + (jax.ShapeDtypeStruct((S, S), F32), jax.ShapeDtypeStruct((1, S), F32))
+        + (TABLE,) * ACCS,
+        in_specs=[HBM] * 6,
+        out_specs=(VMEM, VMEM, VMEM, SMEM, SMEM, VMEM, VMEM) + (VMEM,) * ACCS,
         scratch_shapes=[
             pltpu.SMEM((STEPS, 1, BLK), jnp.int32),
             pltpu.SMEM((STEPS, BLK), jnp.int32),
@@ -181,13 +190,13 @@
             pltpu.VMEM((STEPS, BLK, LANES), jnp.int32),
             pltpu.VMEM((2 * BLK, S, LANES), F32),
             pltpu.SMEM((BLK,), jnp.int32),
-            pltpu.SemaphoreType.DMA((4,)),
+            pltpu.SemaphoreType.DMA((6,)),
             pltpu.SemaphoreType.DMA((6,)),
             pltpu.SemaphoreType.DMA((6,)),
         ],
         compiler_params=pltpu.CompilerParams(collective_id=1, has_side_effects=True, vmem_limit_bytes=LIMIT),
         name="migrate",
-    )(shift_list, arrival, state, cell_index)
+    )(shift_list, arrival, state, cell_index, rates, mix)
 
 
 def split(x):
@@ -231,13 +240,17 @@
 
     turn(0, even)
 
-    @pl.loop(0, BLK // 2)
+    @pl.loop(0, BLK // 4)
     def _(i):
         substep(chem, high2, low1)
-        turn(2 * i + 1, odd)
-        add(2 * i, even)
-        turn(jnp.minimum(2 * i + 2, BLK - 1), even)
-        add(2 * i + 1, odd)
+        turn(4 * i + 1, odd)
+        add(4 * i, even)
+        turn(4 * i + 2, even)
+        add(4 * i + 1, odd)
+        turn(4 * i + 3, odd)
+        add(4 * i + 2, even)
+        turn(jnp.minimum(4 * i + 4, BLK - 1), even)
+        add(4 * i + 3, odd)
 
     @pl.loop(0, BLK)
     def _(slot):
@@ -265,27 +278,20 @@
 
 
 def exchange_kernel(
-    step, moved_ref, chem_ref, rates_hbm, mix_hbm, low_ref, row_ref, order_ref, source_ref, *rest
+    step, moved_ref, chem_ref, rates_ref, mix_ref, low_ref, row_ref, order_ref, source_ref, *rest
 ):
     last = step == STEPS - 1
     accs = rest[:ACCS]
     out_ref = rest[ACCS]
     blanks = () if last else rest[ACCS + 1:2 * ACCS + 1]
     (
-        sums_ref, counts, tallies, rates_ref, mix_ref, below, above, tally_below, tally_above, middle, tally_middle,
-        left, right, tally_left, tally_right, factors, table, chem, high2, low1, even, odd, reacted, pool,
-        up_sem, down_sem, west_sem, east_sem, mwest_sem, meast_sem, mup_sem, mdown_sem, tally_sem, send_sem, recv_sem, load_sem,
+        sums_ref, counts, tallies, below, above, tally_below, tally_above, middle, tally_middle,
+        left, right, tally_left, tally_right, factors, table, chem, high2, low1, even, odd, third, fourth, reacted, pool,
+        up_sem, down_sem, west_sem, east_sem, mwest_sem, meast_sem, mup_sem, mdown_sem, tally_sem, send_sem, recv_sem,
     ) = rest[ACCS + 1 + len(blanks):]
-    loads = [
-        pltpu.make_async_copy(rates_hbm, rates_ref, load_sem.at[0]),
-        pltpu.make_async_copy(mix_hbm, mix_ref, load_sem.at[1]),
-    ]
     lane = lax.broadcasted_iota(jnp.int32, (8, LANES), 1)
     spot = lane % 64
     spare = spot >= S
-    for load in loads:
-        load.start()
-
     def add_up(r):
         @pl.loop(0, QUARTER // 8, unroll=4)
         def _(i):
@@ -405,8 +411,6 @@
         table[2] = jnp.zeros_like(table[2])
 
     add_up(1)
-    for load in loads:
-        load.wait()
     high2[...], low1[...] = pairs_of(rates_ref[...])
     chem[...] = chem_ref[...]
 
@@ -584,9 +588,12 @@
             copy.wait_send()
 
     if last:
-        @pl.loop(0, BLK // 2)
+        @pl.loop(0, BLK // 4)
         def _(i):
-            pair(lambda b: b, out_ref, i)
+            for k, rows in enumerate((even, odd, third, fourth)):
+                gather(4 * i + k, rows)
+            for k, rows in enumerate((even, odd, third, fourth)):
+                out_ref[4 * i + k] = mixed(4 * i + k, rows)
     else:
         polar = is_polar()
         half_unit = jnp.where(polar, 2, 1)
@@ -630,14 +637,12 @@
     return pl.pallas_call(
         functools.partial(exchange_kernel, step),
         out_shape=(state,) + (TABLE,) * blanks,
-        in_specs=[VMEM, VMEM, HBM, HBM, VMEM, SMEM, SMEM, SMEM] + [VMEM] * ACCS,
+        in_specs=[VMEM, VMEM, VMEM, VMEM, VMEM, SMEM, SMEM, SMEM] + [VMEM] * ACCS,
         out_specs=(VMEM,) * (1 + blanks),
         scratch_shapes=[
             pltpu.VMEM((3, 3, PACKED, LANES), F32),
             square,
             pltpu.VMEM((3, 2, 64, LANES), F32),
-            pltpu.VMEM((S, S), F32),
-            pltpu.VMEM((1, S), F32),
             region, region, tally, tally, region, tally,
             beside, beside, tally_beside, tally_beside,
             square,
@@ -645,15 +650,13 @@
             pltpu.VMEM((2, S, BLK // 2 * LANES), F32),
             pltpu.VMEM((2 * S, 4 * S), BF16),
             pltpu.VMEM((2 * S, 2 * S), BF16),
-            square,
-            square,
+            square, square, square, square,
             pltpu.VMEM((BLK, S, LANES), F32),
             pltpu.VMEM((2 * BLK, S, LANES), F32),
             pair, pair, single, single, single, single, pair, pair,
             pltpu.SemaphoreType.DMA((2, 4)),
             pltpu.SemaphoreType.DMA((6,)),
             pltpu.SemaphoreType.DMA((6,)),
-            pltpu.SemaphoreType.DMA((2,)),
         ],
         compiler_params=pltpu.CompilerParams(collective_id=2 + step, has_side_effects=True, vmem_limit_bytes=LIMIT),
         name="exchange",
@@ -661,12 +664,12 @@
 
 
 def shards(species, reaction_rates, mix_rate, shift_list, arrival, cell_index):
-    inputs = (pltpu.with_memory_space_constraint(x, pltpu.HBM) for x in (shift_list, arrival, species, cell_index))
-    moved, row, low, place, source, *accs = migrate(*inputs)
-    mix = mix_rate.reshape(1, S)
+    inputs = (shift_list, arrival, species, cell_index, reaction_rates, mix_rate.reshape(1, S))
+    inputs = (pltpu.with_memory_space_constraint(x, pltpu.HBM) for x in inputs)
+    moved, row, low, place, source, rates, mix, *accs = migrate(*inputs)
     for step in range(STEPS):
-        sums, order, chem = deposit(step, moved, low, row, place, reaction_rates, accs)
-        moved, *accs = exchange(step, sums, moved, chem, reaction_rates, mix, low, row, order, source)
+        sums, order, chem = deposit(step, moved, low, row, place, rates, accs)
+        moved, *accs = exchange(step, sums, moved, chem, rates, mix, low, row, order, source)
     return moved
 
 

time: 99.9 us -> 96.5 us (0.966)
  Pallas kernels: 97.8 us -> 95.4 us
    pallas_call x2, Pallas kernels: 18.4 us -> 14.9 us  [deposit(): pl.pallas_call(functools.partial(deposit_kernel, step), out_shape=(TABLE,...]
    pallas_call x2, Pallas kernels: 67.3 us -> 68.3 us  [exchange(): pl.pallas_call(functools.partial(exchange_kernel, step), out_shape=(state...]
where the time goes in v6:
time: 96.5 us; the launch traced here: 96.4 us
  Pallas kernels  95.4 us (99%)
    pallas_call x2, Pallas kernels, exchange(): pl.pallas_call(functools.partial(exchange_kernel, step), out_shape=(state...  68.3 us
    pallas_call x2, Pallas kernels, deposit(): pl.pallas_call(functools.partial(deposit_kernel, step), out_shape=(TABLE,...  14.9 us
    pallas_call x1, Pallas kernels, migrate(): pl.pallas_call(migrate_kernel, out_shape=(jax.ShapeDtypeStruct((BLK, S, L...  12.2 us

profile of v6, /device:TPU:5, one launch (start us, length us, event | category | flops | bytes accessed | tf_op | source)
XLA Modules:
  0.0 96.4 jit_solution(13731584316202873027)
XLA Ops:
  0.0 12.2 %migrate.1 = (f32[32,48,128]{2,1,0:T(8,128)S(1)}, s32[2,32,128]{2,1,0:T(8,128)S(1)}, s32[2,32,128]{2,1,0:T(8,128)S(1)}, s32[32]{0:T(128)S(1)}, s32[32]{0:T(128)S...) custom-call(s32[2,1,32]{2,1,0:T(1,128)} %shift_hbm.1, ...), custom_call_target="tpu_custom_call" | custom-call | tf_op jit(solution)/shard_map/migrate/pallas_call | solution.py:179
  12.2 7.1 %deposit.2 = (f32[4608,128]{1,0:T(8,128)S(1)}, f32[4608,128]{1,0:T(8,128)S(1)}, f32[4608,128]{1,0:T(8,128)S(1)}, f32[4608,128]{1,0:T(8,128)S(1)}, f32[4608,128]{...) custom-call(f32[32,48,128]{2,1,0:T(8,128)S(1)} %get-tuple-element.41, ...), custom_call_target="tpu_custom_call", output_to_operand_aliasing={{0}: (5, {}), {1}: (6, {}), {2}: (7, {}), {3}: (8, {}), {4}... | custom-call | tf_op jit(solution)/shard_map/deposit/pallas_call | solution.py:261
  19.3 35.2 %exchange.2 = (f32[32,48,128]{2,1,0:T(8,128)S(1)}, f32[4608,128]{1,0:T(8,128)S(1)}, f32[4608,128]{1,0:T(8,128)S(1)}, f32[4608,128]{1,0:T(8,128)S(1)}, f32[4608,1...) custom-call(f32[32,48,128]{2,1,0:T(8,128)S(1)} %get-tuple-element.41.moved_ref, ...), custom_call_target="tpu_custom_call" | custom-call | tf_op jit(solution)/shard_map/exchange/pallas_call | solution.py:637
  54.5 7.8 %deposit.3 = (f32[4608,128]{1,0:T(8,128)S(1)}, f32[4608,128]{1,0:T(8,128)S(1)}, f32[4608,128]{1,0:T(8,128)S(1)}, f32[4608,128]{1,0:T(8,128)S(1)}, f32[4608,128]{...) custom-call(f32[32,48,128]{2,1,0:T(8,128)S(1)} %get-tuple-element.62, ...), custom_call_target="tpu_custom_call", output_to_operand_aliasing={{0}: (5, {}), {1}: (6, {}), {2}: (7, {}), {3}: (8, {}), {4}... | custom-call | tf_op jit(solution)/shard_map/deposit/pallas_call | solution.py:261
  62.3 33.1 %exchange.3 = f32[32,48,128]{2,1,0:T(8,128)S(1)} custom-call(f32[32,48,128]{2,1,0:T(8,128)S(1)} %get-tuple-element.62.moved_ref, f32[2,48,2048]{2,1,0:T(8,128)S(1)} %get-tuple-element.69.chem_ref, f32[48,48]{1,0:T(8,128)S(1)} %get-tuple-element.45.rates_ref, f32[1,48]{1,0:T(1,128)S(1)} %get-tuple-element.53.mix_ref, ...), custom_call_target="tpu_custom_call" | custom-call | tf_op jit(solution)/shard_map/exchange/pallas_call | solution.py:637
  95.5 0.9 copy.32

commit v7 on v6

--- a/solution.py
+++ b/solution.py
@@ -15,7 +15,7 @@
 ROWS = CELL_DEV // 2
 STEPS = 2
 SUB = 32
-ACCS = 6
+ACCS = 5
 QUARTER = ROWS // 4
 PACKED = 3 * QUARTER
 PIECES = 6
@@ -30,12 +30,8 @@
 LIMIT = 24 * 2**20
 BATCHES = (2, -2, 1, 1, -1, -1)
 FIRST = {2: 0, -2: 1, 1: 2, -1: 4}
-PLAN = (
-    ("a", 0), 1, ("a", 1), 1, ("a", 2), 1, ("a", 3), 1, ("a", 4), 1, ("a", 5), 1,
-    ("o", 0), ("b", 0), ("o", 1), ("b", 1), 1, ("o", 2), ("b", 2), ("o", 3), ("b", 3), 1, ("o", 4), ("b", 4), ("o", 5), ("b", 5),
-    3, ("c", 0), 1, ("c", 1), 1, ("c", 2), 1, ("c", 3), 1, ("c", 4), 1, ("c", 5), 4,
-)
-EARLY = 4
+PLAN = (('a', 0), 1, ('a', 1), 1, ('a', 2), 1, ('a', 3), 1, ('a', 4), 1, ('a', 5), 1, ('o', 0), ('b', 0), ('o', 1), ('b', 1), 1, ('o', 2), ('b', 2), ('o', 3), ('b', 3), 1, ('o', 4), ('b', 4), ('o', 5), ('b', 5), 4, ('c', 0), 1, ('c', 1), 1, ('c', 2), 1, ('c', 3), 1, ('c', 4), 1, ('c', 5), 2)
+EARLY = 5
 
 
 def around(axis, step):
@@ -129,17 +125,17 @@
     loads[1].wait()
     loads[2].wait()
 
-    @pl.loop(0, 6 * unit)
-    def _(where):
-        def seek(slot, found):
-            return jnp.where(pool_at[slot] == where + BLK, slot, found)
-
-        pool[where] = state_ref[lax.fori_loop(0, BLK, seek, jnp.int32(0), unroll=True)]
-
     pl.semaphore_wait(barrier, 4)
 
     def start(unit):
         for k in range(6):
+            @pl.loop(k * unit, k * unit + unit)
+            def _(where):
+                def seek(slot, found):
+                    return jnp.where(pool_at[slot] == where + BLK, slot, found)
+
+                pool[where] = state_ref[lax.fori_loop(0, BLK, seek, jnp.int32(0), unroll=True)]
+
             batch_copy(pool, send_sem, recv_sem, k, unit).start()
 
     each_unit(polar, start)
@@ -588,7 +584,7 @@
             copy.wait_send()
 
     if last:
-        @pl.loop(0, BLK // 4)
+        @pl.loop(0, BLK // 4, unroll=2)
         def _(i):
             for k, rows in enumerate((even, odd, third, fourth)):
                 gather(4 * i + k, rows)

time: 96.5 us -> 96.5 us (level)
  no operation moved by 1% of the time
where the time goes in v7:
time: 96.5 us; the launch traced here: 96.4 us
  Pallas kernels  95.5 us (99%)
    pallas_call x2, Pallas kernels, exchange(): pl.pallas_call(functools.partial(exchange_kernel, step), out_shape=(state...  68.3 us
    pallas_call x2, Pallas kernels, deposit(): pl.pallas_call(functools.partial(deposit_kernel, step), out_shape=(TABLE,...  15.3 us
    pallas_call x1, Pallas kernels, migrate(): pl.pallas_call(migrate_kernel, out_shape=(jax.ShapeDtypeStruct((BLK, S, L...  11.9 us

profile of v7, /device:TPU:5, one launch (start us, length us, event | category | flops | bytes accessed | tf_op | source)
XLA Modules:
  0.0 96.4 jit_solution(16144689482516628800)
XLA Ops:
  0.0 11.9 %migrate.1 = (f32[32,48,128]{2,1,0:T(8,128)S(1)}, s32[2,32,128]{2,1,0:T(8,128)S(1)}, s32[2,32,128]{2,1,0:T(8,128)S(1)}, s32[32]{0:T(128)S(1)}, s32[32]{0:T(128)S...) custom-call(s32[2,1,32]{2,1,0:T(1,128)} %shift_hbm.1, ...), custom_call_target="tpu_custom_call" | custom-call | tf_op jit(solution)/shard_map/migrate/pallas_call | solution.py:175
  11.9 7.4 %deposit.2 = (f32[4608,128]{1,0:T(8,128)S(1)}, f32[4608,128]{1,0:T(8,128)S(1)}, f32[4608,128]{1,0:T(8,128)S(1)}, f32[4608,128]{1,0:T(8,128)S(1)}, f32[4608,128]{...) custom-call(f32[32,48,128]{2,1,0:T(8,128)S(1)} %get-tuple-element.37, ...), custom_call_target="tpu_custom_call", output_to_operand_aliasing={{0}: (5, {}), {1}: (6, {}), {2}: (7, {}), {3}: (8, {}), {4}... | custom-call | tf_op jit(solution)/shard_map/deposit/pallas_call | solution.py:257
  19.3 35.8 %exchange.2 = (f32[32,48,128]{2,1,0:T(8,128)S(1)}, f32[4608,128]{1,0:T(8,128)S(1)}, f32[4608,128]{1,0:T(8,128)S(1)}, f32[4608,128]{1,0:T(8,128)S(1)}, f32[4608,128]{1,0:T(8,128)S(1)}, /*index=5*/f32[4608,128]{1,0:T(8,128)S(1)}) custom-call(f32[32,48,128]{2,1,0:T(8,128)S(1)} %get-tuple-element.37.moved_ref, f32[2,48,2048]{2,1,0:T(8,128)S(1)} %get-tuple-element.47.chem_ref, ...), custom_call_target="tpu_custom_call" | custom-call | tf_op jit(solution)/shard_map/exchange/pallas_call | solution.py:633
  55.1 7.9 %deposit.3 = (f32[4608,128]{1,0:T(8,128)S(1)}, f32[4608,128]{1,0:T(8,128)S(1)}, f32[4608,128]{1,0:T(8,128)S(1)}, f32[4608,128]{1,0:T(8,128)S(1)}, f32[4608,128]{...) custom-call(f32[32,48,128]{2,1,0:T(8,128)S(1)} %get-tuple-element.56, ...), custom_call_target="tpu_custom_call", output_to_operand_aliasing={{0}: (5, {}), {1}: (6, {}), {2}: (7, {}), {3}: (8, {}), {4}... | custom-call | tf_op jit(solution)/shard_map/deposit/pallas_call | solution.py:257
  63.1 32.4 %exchange.3 = f32[32,48,128]{2,1,0:T(8,128)S(1)} custom-call(f32[32,48,128]{2,1,0:T(8,128)S(1)} %get-tuple-element.56.moved_ref, f32[2,48,2048]{2,1,0:T(8,128)S(1)} %get-tuple-element.62.chem_ref, f32[48,48]{1,0:T(8,128)S(1)} %get-tuple-element.41.rates_ref, f32[1,48]{1,0:T(1,128)S(1)} %get-tuple-element.48.mix_ref, ...), custom_call_target="tpu_custom_call" | custom-call | tf_op jit(solution)/shard_map/exchange/pallas_call | solution.py:633
  95.5 0.9 copy.28

commit v8 on v6

--- a/solution.py
+++ b/solution.py
@@ -33,7 +33,7 @@
 PLAN = (
     ("a", 0), 1, ("a", 1), 1, ("a", 2), 1, ("a", 3), 1, ("a", 4), 1, ("a", 5), 1,
     ("o", 0), ("b", 0), ("o", 1), ("b", 1), 1, ("o", 2), ("b", 2), ("o", 3), ("b", 3), 1, ("o", 4), ("b", 4), ("o", 5), ("b", 5),
-    3, ("c", 0), 1, ("c", 1), 1, ("c", 2), 1, ("c", 3), 1, ("c", 4), 1, ("c", 5), 4,
+    ("z", 0), 3, ("c", 0), 1, ("c", 1), 1, ("c", 2), 1, ("c", 3), 1, ("c", 4), 1, ("c", 5), 4,
 )
 EARLY = 4
 
@@ -507,15 +507,13 @@
             means_down(0, p).start()
             means_down(2, p).start()
 
-    parts = {"a": sides_summed, "o": own_summed, "b": sectors_summed, "c": means_passed}
+    parts = {"z": lambda _: blank_strips(blanks) if blanks else None, "a": sides_summed, "o": own_summed, "b": sectors_summed, "c": means_passed}
     for entry in PLAN:
         if isinstance(entry, int):
             chemistry(entry)
         else:
             parts[entry[0]](entry[1])
 
-    if not last:
-        blank_strips(blanks)
     for b in range(BLK):
         column = b % HALF_BLK * LANES
         reacted[b] = chem[b // HALF_BLK, :, column:column + LANES]

time: 96.5 us -> 96.1 us (level)
  no operation moved by 1% of the time
where the time goes in v8:
time: 96.1 us; the launch traced here: 95.9 us
  Pallas kernels  95 us (99%)
    pallas_call x2, Pallas kernels, exchange(): pl.pallas_call(functools.partial(exchange_kernel, step), out_shape=(state...  67.9 us
    pallas_call x2, Pallas kernels, deposit(): pl.pallas_call(functools.partial(deposit_kernel, step), out_shape=(TABLE,...  14.9 us
    pallas_call x1, Pallas kernels, migrate(): pl.pallas_call(migrate_kernel, out_shape=(jax.ShapeDtypeStruct((BLK, S, L...  12.2 us

profile of v8, /device:TPU:5, one launch (start us, length us, event | category | flops | bytes accessed | tf_op | source)
XLA Modules:
  0.0 95.9 jit_solution(4426378564918782497)
XLA Ops:
  0.0 12.2 %migrate.1 = (f32[32,48,128]{2,1,0:T(8,128)S(1)}, s32[2,32,128]{2,1,0:T(8,128)S(1)}, s32[2,32,128]{2,1,0:T(8,128)S(1)}, s32[32]{0:T(128)S(1)}, s32[32]{0:T(128)S...) custom-call(s32[2,1,32]{2,1,0:T(1,128)} %shift_hbm.1, ...), custom_call_target="tpu_custom_call" | custom-call | tf_op jit(solution)/shard_map/migrate/pallas_call | solution.py:179
  12.2 7.1 %deposit.2 = (f32[4608,128]{1,0:T(8,128)S(1)}, f32[4608,128]{1,0:T(8,128)S(1)}, f32[4608,128]{1,0:T(8,128)S(1)}, f32[4608,128]{1,0:T(8,128)S(1)}, f32[4608,128]{...) custom-call(f32[32,48,128]{2,1,0:T(8,128)S(1)} %get-tuple-element.41, ...), custom_call_target="tpu_custom_call", output_to_operand_aliasing={{0}: (5, {}), {1}: (6, {}), {2}: (7, {}), {3}: (8, {}), {4}... | custom-call | tf_op jit(solution)/shard_map/deposit/pallas_call | solution.py:261
  19.3 36.3 %exchange.2 = (f32[32,48,128]{2,1,0:T(8,128)S(1)}, f32[4608,128]{1,0:T(8,128)S(1)}, f32[4608,128]{1,0:T(8,128)S(1)}, f32[4608,128]{1,0:T(8,128)S(1)}, f32[4608,1...) custom-call(f32[32,48,128]{2,1,0:T(8,128)S(1)} %get-tuple-element.41.moved_ref, ...), custom_call_target="tpu_custom_call" | custom-call | tf_op jit(solution)/shard_map/exchange/pallas_call | solution.py:635
  55.6 7.8 %deposit.3 = (f32[4608,128]{1,0:T(8,128)S(1)}, f32[4608,128]{1,0:T(8,128)S(1)}, f32[4608,128]{1,0:T(8,128)S(1)}, f32[4608,128]{1,0:T(8,128)S(1)}, f32[4608,128]{...) custom-call(f32[32,48,128]{2,1,0:T(8,128)S(1)} %get-tuple-element.62, ...), custom_call_target="tpu_custom_call", output_to_operand_aliasing={{0}: (5, {}), {1}: (6, {}), {2}: (7, {}), {3}: (8, {}), {4}... | custom-call | tf_op jit(solution)/shard_map/deposit/pallas_call | solution.py:261
  63.5 31.6 %exchange.3 = f32[32,48,128]{2,1,0:T(8,128)S(1)} custom-call(f32[32,48,128]{2,1,0:T(8,128)S(1)} %get-tuple-element.62.moved_ref, f32[2,48,2048]{2,1,0:T(8,128)S(1)} %get-tuple-element.69.chem_ref, f32[48,48]{1,0:T(8,128)S(1)} %get-tuple-element.45.rates_ref, f32[1,48]{1,0:T(1,128)S(1)} %get-tuple-element.53.mix_ref, ...), custom_call_target="tpu_custom_call" | custom-call | tf_op jit(solution)/shard_map/exchange/pallas_call | solution.py:635
  95.1 0.9 copy.32
